TPU v7x, 128 devices: a whole 4x4x4 slice. The times are simulated.
128 devices in a mesh: lat: 32 (over z, y_hi, x), lon: 4 (over y_lo, core).
Axes of the slice: x: 4, y: 4 (y_hi: 2, y_lo: 2; y = y_hi * 2 + y_lo), z: 4, core: 2. Of those that a mesh axis runs over, the one named last changes fastest.
Arguments:
- features: bfloat16 [192, 256, 768], P('lat', 'lon'), may hold values from -6 to 6
- upstream: bfloat16 [192, 256, 768], P('lat', 'lon'), may hold values from -6 to 6
- weights: bfloat16 [3072, 768], replicated, may hold values from -0.109375 to 0.109375
- filter_basis: bfloat16 [4, 192, 7, 7], replicated, may hold values from -0.875 to 0.875
- lat_width: int32 [192], replicated, may hold values from 1 to 7
- lat_offset: int32 [192], replicated, may hold values from 0 to 6, as said below
- lon_reach: int32 [192], replicated, may hold values from 0 to 3
Outputs:
- convolved: bfloat16 [192, 256, 768], P('lat', 'lon')
- state_grad: bfloat16 [192, 256, 768], P('lat', 'lon')
- weight_grad: float32 [3072, 768], P(('lat', 'lon'))
Inputs may be any that keep to these rules, and one draw needn't show every extreme that they name: lat_offset + lat_width <= 7 at every latitude.
All inputs are finite; a program needn't handle non-finite values.
Results may differ from a plain program's by a relative error of at most 0.0055.
Values may be sent and summed in bfloat16 or wider, within the bound.
No kernel may reach another device: no remote copies, remote signals or barrier semaphores. Data moves between devices by JAX's collectives and lax.ppermute only.
A program may use at most 128 MiB of HBM per device.

v0:
```python
import jax
import jax.numpy as jnp
from jax import lax
from jax.sharding import PartitionSpec as P

CHANNELS = 768
NBASIS = 4
HALO = 3
TAPS = 7
LAT_DEV = 6
LON_DEV = 64


def with_halo(cells, sides, width):
    for axis, dim in sides:
        count = lax.axis_size(axis)
        head = lax.slice_in_dim(cells, 0, width, axis=dim)
        tail = lax.slice_in_dim(cells, cells.shape[dim] - width, cells.shape[dim], axis=dim)
        cells = jnp.concatenate(
            [
                lax.ppermute(tail, axis, [(i, (i + 1) % count) for i in range(count)]),
                cells,
                lax.ppermute(head, axis, [((i + 1) % count, i) for i in range(count)]),
            ],
            axis=dim,
        )
    return cells


def from_behind(block, axis, distance):
    devices = range(lax.axis_size(axis))
    route = [((i - distance) % len(devices), i) for i in devices]
    return lax.ppermute(block, axis, route)


def support_filter(filter_rows, widths, offsets, reaches):
    tap_ids = jnp.arange(TAPS, dtype=jnp.int32)
    lat_keep = (tap_ids[None, :] >= offsets[:, None]) & (
        tap_ids[None, :] < offsets[:, None] + widths[:, None]
    )
    lon_keep = jnp.abs(tap_ids - HALO)[None, :] <= reaches[:, None]
    kept_taps = lat_keep[None, :, :, None] & lon_keep[None, :, None, :]
    return jnp.where(kept_taps, filter_rows, jnp.zeros_like(filter_rows))


def on_device(features, upstream, weights, filter_basis, lat_width, lat_offset, lon_reach):
    lat_index = lax.axis_index("lat")
    lat_count = lax.axis_size("lat")
    half_turn = lax.axis_size("lon") // 2
    row_start = lat_index * LAT_DEV
    filters = support_filter(
        lax.dynamic_slice_in_dim(filter_basis, row_start, LAT_DEV, 1),
        lax.dynamic_slice_in_dim(lat_width, row_start, LAT_DEV, 0),
        lax.dynamic_slice_in_dim(lat_offset, row_start, LAT_DEV, 0),
        lax.dynamic_slice_in_dim(lon_reach, row_start, LAT_DEV, 0),
    )
    is_first = lat_index == 0
    is_last = lat_index == lat_count - 1
    col_span = LON_DEV + 2 * HALO
    padded = with_halo(features, (("lat", 0), ("lon", 1)), HALO)
    polar_rows = jnp.concatenate(
        [padded[HALO : 2 * HALO][::-1], padded[LAT_DEV : LAT_DEV + HALO][::-1]], 0
    )
    mirrored = from_behind(polar_rows, "lon", half_turn)
    upper_rows = jnp.where(is_first, mirrored[:HALO], padded[:HALO])
    lower_rows = jnp.where(is_last, mirrored[HALO:], padded[LAT_DEV + HALO :])
    extended = jnp.concatenate([upper_rows, padded[HALO : LAT_DEV + HALO], lower_rows], 0)
    windows = jnp.stack([extended[shift_row : shift_row + LAT_DEV] for shift_row in range(TAPS)], 1)
    basis_acc = jnp.zeros((LAT_DEV, NBASIS, LON_DEV, CHANNELS), jnp.float32)
    for shift_col in range(TAPS):
        basis_acc = basis_acc + jnp.einsum(
            "kia,iajc->ikjc",
            filters[:, :, :, shift_col],
            windows[:, :, shift_col : shift_col + LON_DEV],
            preferred_element_type=jnp.float32,
        )
    basis_rows = basis_acc.astype(jnp.bfloat16)
    mixing = weights.reshape(NBASIS, CHANNELS, CHANNELS)
    convolved = jnp.einsum(
        "ikjc,kcd->ijd", basis_rows, mixing, preferred_element_type=jnp.float32
    ).astype(jnp.bfloat16)
    grad_full = jnp.einsum(
        "ikjc,ijd->kcd", basis_rows, upstream, preferred_element_type=jnp.float32
    ).reshape(NBASIS * CHANNELS, CHANNELS)
    weight_grad = lax.psum_scatter(grad_full, ("lat", "lon"), scatter_dimension=0, tiled=True)
    basis_grad = jnp.einsum(
        "ijd,kcd->ijkc", upstream, mixing, preferred_element_type=jnp.float32
    ).astype(jnp.bfloat16)
    accumulated = jnp.zeros((LAT_DEV, TAPS, col_span, CHANNELS), jnp.float32)
    for shift_col in range(TAPS):
        accumulated = accumulated.at[:, :, shift_col : shift_col + LON_DEV].add(
            jnp.einsum(
                "kia,ijkc->iajc",
                filters[:, :, :, shift_col],
                basis_grad,
                preferred_element_type=jnp.float32,
            )
        )
    row_map = (
        jnp.arange(LAT_DEV + 2 * HALO)[:, None, None]
        == jnp.arange(LAT_DEV)[None, :, None] + jnp.arange(TAPS)[None, None, :]
    ).astype(jnp.float32)
    spread = jnp.einsum("ria,iamc->rmc", row_map, accumulated, precision=lax.Precision.HIGHEST)
    pole_rows = jnp.concatenate([spread[:HALO][::-1], spread[LAT_DEV + HALO :][::-1]], 0)
    returned = from_behind(pole_rows.astype(jnp.bfloat16), "lon", half_turn).astype(pole_rows.dtype)
    zero_rim = jnp.zeros((HALO, col_span, CHANNELS), jnp.float32)
    middle = spread[HALO : LAT_DEV + HALO]
    middle = middle.at[:HALO].add(jnp.where(is_first, returned[:HALO], zero_rim))
    middle = middle.at[LAT_DEV - HALO :].add(jnp.where(is_last, returned[HALO:], zero_rim))
    cleared = jnp.concatenate(
        [
            jnp.where(is_first, zero_rim, spread[:HALO]),
            middle,
            jnp.where(is_last, zero_rim, spread[LAT_DEV + HALO :]),
        ],
        0,
    )
    gathered = with_halo(cleared, (("lat", 0), ("lon", 1)), HALO)
    by_rows = gathered[2 * HALO : LAT_DEV + 2 * HALO]
    by_rows = by_rows.at[:HALO].add(gathered[:HALO])
    by_rows = by_rows.at[LAT_DEV - HALO :].add(gathered[LAT_DEV + 3 * HALO :])
    by_cols = by_rows[:, 2 * HALO : LON_DEV + 2 * HALO]
    by_cols = by_cols.at[:, :HALO].add(by_rows[:, :HALO])
    by_cols = by_cols.at[:, LON_DEV - HALO :].add(by_rows[:, LON_DEV + 3 * HALO :])
    state_grad = by_cols.astype(jnp.bfloat16)
    return (convolved, state_grad, weight_grad)


def solution(mesh):
    return jax.shard_map(
        on_device,
        mesh=mesh,
        in_specs=(P("lat", "lon", None), P("lat", "lon", None), P(), P(), P(), P(), P()),
        out_specs=(P("lat", "lon", None), P("lat", "lon", None), P(("lat", "lon"), None)),
        check_vma=False,
    )
```

profile of v0, /device:TPU:0, one launch (start us, length us, event | category | flops | bytes accessed | tf_op | source)
XLA Modules:
  0.0 805.9 jit_solution(2953748738754744649)
XLA Ops:
  7.2 1.5 copy.185
  9.0 9.0 %collective-permute-start.1 = (bf16[3,64,768]{2,0,1:T(4,128)(2,1)S(1)}, bf16[3,64,768]{2,0,1:T(4,128)(2,1)S(1)}, u32[]{:S(2)}, u32[]{:S(2)}) collective-permute-start(bf16[3,64,768]{2,0,1:T(4,128)(2,1)S(1)} %get-tuple-element.192), channel_id=1, source_target_pairs={{4,0},{8,4},{12,8},{16,12},{20,16},{24,20},{28,24},{32,28},{36,32}... | collective-permute-start | bytes 884744 | tf_op jit(solution)/shard_map/ppermute | solution.py:23
  19.7 6.7 collective-permute-done.1
  26.4 7.9 collective-permute-done
  35.1 0.9 copy.247
  36.0 0.9 collective-permute-done.3
  37.6 0.8 collective-permute-done.2
  38.4 2.0 pad_maximum_fusion.1
  40.4 1.2 fusion.61
  41.6 3.2 rev.13
  44.8 2.4 rev.12
  47.3 1.4 pad_maximum_fusion.4
  48.8 1.6 collective-permute-start.4
  50.8 2.1 copy.201
  52.9 13.2 %collective-permute-done.4 = bf16[6,70,768]{2,1,0:T(8,128)(2,1)S(1)} collective-permute-done((bf16[6,70,768]{2,1,0:T(8,128)(2,1)S(1)}, bf16[6,70,768]{2,1,0:T(8,128)(2,1)S(1)}, u32[]{:S(2)}, u32[]{:S(2)}) %collective-permute-start.4) | collective-permute-done | bytes 645152 | tf_op jit(solution)/shard_map/ppermute | solution.py:33
  66.7 2.2 fusion.41
  68.9 1.0 copy.198
  69.9 2.1 copy.199
  72.0 2.1 copy.200
  74.0 2.2 copy.202
  76.2 2.1 copy.203
  78.3 2.1 copy.204
  80.3 26.8 %stack.31 = bf16[6,7,70,768]{3,1,2,0:T(8,128)(2,1)} concatenate(bf16[6,1,70,768]{3,1,2,0:T(2,128)(2,1)S(1)} %copy.198, bf16[6,1,70,768]{3,1,2,0:T(2,128)(2,1)} %copy.199, bf16[6,1,70,768]{3,1,2,0:T(2,128)(2,1)} %copy.200, bf16[6,1,70,768]{3,1,2,0:T(2,128)(2,1)S(1)} %copy-done.7, bf16[6,1,70,768]{3,1,2,0:T(2,128)(2,1)} %copy.202, bf16[6,1,70,768]{3,1,2,0:T(2,128)(2,1)} %copy.203, ...), dimensions={1} | concatenate | bytes 9031680 | tf_op jit(solution)/shard_map/stack | solution.py:68
  107.1 3.9 fusion.5
  111.0 3.5 fusion.7
  114.5 3.5 fusion.9
  118.0 3.6 fusion.11
  121.6 3.5 fusion.13
  125.1 3.5 fusion.15
  128.7 11.2 %add_convert_fusion = bf16[6,4,64,768]{3,1,2,0:T(4,128)(2,1)} fusion(f32[6,4,64,768]{3,1,2,0:T(4,128)S(1)} %fusion.5, f32[6,4,64,768]{3,1,2,0:T(4,128)} %fusion.7, f32[6,4,64,768]{3,1,2,0:T(4,128)} %fusion.9, f32[6,4,64,768]{3,1,2,0:T(4,128)} %fusion.11, f32[6,4,64,768]{3,1,2,0:T(4,128)} %fusion.13, f32[6,4,64,768]{3,1,2,0:T(4,128)} %fusion.15, ...), kind=kOutput, calls=%fused_computation.26 | convolution fusion | flops 24772608 | bytes 35395584 | tf_op jit(solution)/shard_map/kia,iajc->ikjc/dot_general | solution.py:71
  139.8 8.0 fusion.19
  147.8 4.4 convolution_convert_fusion
  152.2 4.7 fusion.50
  156.9 4.6 scatter-add.44
  161.5 4.6 add_dynamic-update-slice_fusion
  166.1 4.6 fusion.4
  170.8 4.8 fusion.3
  175.6 4.6 fusion.2
  180.2 4.6 fusion.1
  184.8 5.0 fusion
  189.8 5.9 convolution_bitcast_fusion
  195.7 1.8 copy-done.3
  197.9 1.0 rev.15
  198.9 1.0 rev.14
  200.5 1.9 collective-permute-start.6
  202.3 16.4 %collective-permute-done.6 = bf16[6,70,768]{2,1,0:T(8,128)(2,1)S(1)} collective-permute-done((bf16[6,70,768]{2,1,0:T(8,128)(2,1)S(1)}, bf16[6,70,768]{2,1,0:T(8,128)(2,1)S(1)}, u32[]{:S(2)}, u32[]{:S(2)}) %collective-permute-start.6) | collective-permute-done | bytes 645152 | tf_op jit(solution)/shard_map/ppermute | solution.py:33
  218.9 4.8 fusion.40
  223.7 1.1 copy.214
  224.9 1.0 copy.217
  225.9 7.7 collective-permute-start.7
  233.9 13.1 %scatter-add.55 = f32[6,70,768]{2,0,1:T(8,128)S(1)} dynamic-update-slice(f32[6,70,768]{2,0,1:T(8,128)S(1)} %slice.588, f32[3,70,768]{2,0,1:T(4,128)} %get-tuple-element.169, s32[]{:T(128)} %constant.346.clone.1, s32[]{:T(128)} %constant.346.clone.1, s32[]{:T(128)} %constant.346.clone.1) | dynamic-update-slice | bytes 1290244 | tf_op jit(solution)/shard_map/scatter-add | solution.py:108
  247.0 2.8 fusion.39
  249.8 13.1 %scatter-add.56 = f32[6,70,768]{2,0,1:T(8,128)S(1)} dynamic-update-slice(f32[6,70,768]{2,0,1:T(8,128)S(1)} %scatter-add.55, f32[3,70,768]{2,0,1:T(4,128)} %fusion.39, s32[]{:T(128)} %constant.354.clone.1, s32[]{:T(128)} %constant.346.clone.1, s32[]{:T(128)} %constant.346.clone.1) | dynamic-update-slice | bytes 1290244 | tf_op jit(solution)/shard_map/scatter-add | solution.py:109
  262.9 2.3 copy.218
  265.3 2.4 copy.219
  267.6 42.9 %concatenate.62 = f32[18,70,768]{2,0,1:T(8,128)} concatenate(f32[3,70,768]{2,0,1:T(4,128)} %copy.218, f32[3,70,768]{2,0,1:T(4,128)} %copy-done.5, f32[6,70,768]{2,0,1:T(8,128)S(1)} %scatter-add.56, f32[3,70,768]{2,0,1:T(4,128)S(1)} %get-tuple-element.170, f32[3,70,768]{2,0,1:T(4,128)} %copy.219), dimensions={0} | concatenate | bytes 7741440 | tf_op jit(solution)/shard_map/concatenate | solution.py:19
  310.5 1.1 fusion.59
  312.2 6.0 fusion.28
  318.3 2.0 collective-permute-done.8
  321.2 9.2 %scatter-add.59 = f32[6,76,768]{2,0,1:T(8,128)S(1)} dynamic-update-slice(f32[6,76,768]{2,0,1:T(8,128)S(1)} %slice.595, f32[3,76,768]{2,0,1:T(4,128)S(1)} %maximum_add_fusion.1, s32[]{:T(128)} %constant.346.clone.1, s32[]{:T(128)} %constant.346.clone.1, s32[]{:T(128)} %constant.346.clone.1) | dynamic-update-slice | bytes 1400836 | tf_op jit(solution)/shard_map/scatter-add | solution.py:120
  330.4 2.4 maximum_add_fusion
  332.8 9.2 %scatter-add.60 = f32[6,76,768]{2,0,1:T(8,128)S(1)} dynamic-update-slice(f32[6,76,768]{2,0,1:T(8,128)S(1)} %scatter-add.59, f32[3,76,768]{2,0,1:T(4,128)S(1)} %maximum_add_fusion, s32[]{:T(128)} %constant.354.clone.1, s32[]{:T(128)} %constant.346.clone.1, s32[]{:T(128)} %constant.346.clone.1) | dynamic-update-slice | bytes 1400836 | tf_op jit(solution)/shard_map/scatter-add | solution.py:121
  342.3 0.9 copy.221
  343.2 455.6 %reduce-scatter.2.cloned.1.call-done = f32[24,768]{1,0:T(8,128)} async-done(((f32[3072,768]{1,0:T(8,128)}), f32[24,768]{1,0:T(8,128)}) %reduce-scatter.2.cloned.1.call-update) | async-done | bytes 73744 | tf_op jit(solution)/shard_map/reduce_scatter | solution.py:85
  (66 shorter events, 7.8 us)
Async XLA Ops:
  7.2 132.7 %copy-start = (bf16[6,64,768]{2,1,0:T(8,128)(2,1)S(1)}, bf16[6,64,768]{2,1,0:T(8,128)(2,1)}, u32[]{:S(2)}) copy-start(bf16[6,64,768]{2,1,0:T(8,128)(2,1)} %param.34) | copy-start | bytes 1769476
  7.2 27.8 %copy-start.11 = (bf16[4,192,7,7]{1,0,3,2:T(4,128)(2,1)S(1)}, bf16[4,192,7,7]{1,0,3,2:T(4,128)(2,1)}, u32[]{:S(2)}) copy-start(bf16[4,192,7,7]{1,0,3,2:T(4,128)(2,1)} %param.36) | copy-start | bytes 225796
  7.2 791.6 %reduce-scatter.2.cloned.1.call-start = ((), (), s32[]{:S(2)}) async-start(), calls=%async_computation.1 | async-start | bytes 9510912 | tf_op jit(solution)/shard_map/reduce_scatter | solution.py:85
  9.0 17.4 %collective-permute-start.1 = (bf16[3,64,768]{2,0,1:T(4,128)(2,1)S(1)}, bf16[3,64,768]{2,0,1:T(4,128)(2,1)S(1)}, u32[]{:S(2)}, u32[]{:S(2)}) collective-permute-start(bf16[3,64,768]{2,0,1:T(4,128)(2,1)S(1)} %get-tuple-element.192), channel_id=1, source_target_pairs={{4,0},{8,4},{12,8},{16,12},{20,16},{24,20},{28,24},{32,28},{36,32}... | collective-permute-start | bytes 884744 | tf_op jit(solution)/shard_map/ppermute | solution.py:23
  18.0 16.3 %collective-permute-start = (bf16[3,64,768]{2,0,1:T(4,128)(2,1)S(1)}, bf16[3,64,768]{2,0,1:T(4,128)(2,1)S(1)}, u32[]{:S(2)}, u32[]{:S(2)}) collective-permute-start(bf16[3,64,768]{2,0,1:T(4,128)(2,1)S(1)} %get-tuple-element.191), channel_id=1, source_target_pairs={{0,4},{4,8},{8,12},{12,16},{16,20},{20,24},{24,28},{28,32},{32,36}... | collective-permute-start | bytes 884744 | tf_op jit(solution)/shard_map/ppermute | solution.py:21
  34.3 2.6 copy-start.8
  34.4 2.6 collective-permute-start.3
  34.5 4.0 collective-permute-start.2
  36.9 0.6 copy-start.10
  40.4 10.1 %copy-start.9 = (bf16[4,6,7,7]{2,0,1,3:T(4,128)(2,1)S(1)}, bf16[4,6,7,7]{2,0,1,3:T(4,128)(2,1)}, u32[]{:S(2)}) copy-start(bf16[4,6,7,7]{2,0,1,3:T(4,128)(2,1)} %copy.247) | copy-start | bytes 7060
  48.8 17.2 %collective-permute-start.4 = (bf16[6,70,768]{2,1,0:T(8,128)(2,1)S(1)}, bf16[6,70,768]{2,1,0:T(8,128)(2,1)S(1)}, u32[]{:S(2)}, u32[]{:S(2)}) collective-permute-start(bf16[6,70,768]{2,1,0:T(8,128)(2,1)S(1)} %copy.188), channel_id=1, source_target_pairs={{2,0},{3,1},{0,2},{1,3},{6,4},{7,5},{4,6},{5,7},{10,8},{11,9},{8,1... | collective-permute-start | bytes 1935368 | tf_op jit(solution)/shard_map/ppermute | solution.py:33
  74.0 6.3 copy-start.7
  107.1 3.9 copy-start.2
  195.7 1.8 copy-start.3
  200.5 18.3 %collective-permute-start.6 = (bf16[6,70,768]{2,1,0:T(8,128)(2,1)S(1)}, bf16[6,70,768]{2,1,0:T(8,128)(2,1)S(1)}, u32[]{:S(2)}, u32[]{:S(2)}) collective-permute-start(bf16[6,70,768]{2,1,0:T(8,128)(2,1)S(1)} %copy.215), channel_id=1, source_target_pairs={{2,0},{3,1},{0,2},{1,3},{6,4},{7,5},{4,6},{5,7},{10,8},{11,9},{8,1... | collective-permute-start | bytes 1935368 | tf_op jit(solution)/shard_map/ppermute | solution.py:33
  218.9 5.9 copy-start.6
  218.9 14.7 %copy-start.4 = (f32[12,70,768]{2,0,1:T(8,128)S(1)}, f32[12,70,768]{2,0,1:T(8,128)}, u32[]{:S(2)}) copy-start(f32[12,70,768]{2,0,1:T(8,128)} %copy-done.3) | copy-start | bytes 7741444
  223.7 10.2 %copy-start.5 = (f32[3,70,768]{2,0,1:T(4,128)}, f32[3,70,768]{2,0,1:T(4,128)S(1)}, u32[]{:S(2)}) copy-start(f32[3,70,768]{2,0,1:T(4,128)S(1)} %get-tuple-element.171) | copy-start | bytes 1935364
  224.8 38.2 %collective-permute-start.5 = (f32[3,70,768]{2,1,0:T(8,128)}, f32[3,70,768]{2,1,0:T(8,128)}, u32[]{:S(2)}, u32[]{:S(2)}) collective-permute-start(f32[3,70,768]{2,1,0:T(8,128)} %copy.214), channel_id=1, source_target_pairs={{0,4},{4,8},{8,12},{12,16},{16,20},{20,24},{24,28},{28,32},{32,36}... | collective-permute-start | bytes 1935368 | tf_op jit(solution)/shard_map/ppermute | solution.py:21
  225.9 39.4 %collective-permute-start.7 = (f32[3,70,768]{2,1,0:T(8,128)}, f32[3,70,768]{2,1,0:T(8,128)}, u32[]{:S(2)}, u32[]{:S(2)}) collective-permute-start(f32[3,70,768]{2,1,0:T(8,128)} %copy.217), channel_id=1, source_target_pairs={{4,0},{8,4},{12,8},{16,12},{20,16},{24,20},{28,24},{32,28},{36,32}... | collective-permute-start | bytes 1935368 | tf_op jit(solution)/shard_map/ppermute | solution.py:23
  311.6 6.7 collective-permute-start.9
  312.2 8.1 %slice-start = ((s8[5160960]{0:T(1024)(128)(4,1)}), s8[4194304]{0:T(1024)(128)(4,1)S(1)}, s32[]{:S(2)}) async-start(s8[5160960]{0:T(1024)(128)(4,1)} %bitcast.81), calls=%async_computation.2 | async-start | bytes 8388608
  312.2 8.1 %slice-start.1 = ((s8[5160960]{0:T(1024)(128)(4,1)}), s8[966656]{0:T(1024)(128)(4,1)S(1)}, s32[]{:S(2)}) async-start(s8[5160960]{0:T(1024)(128)(4,1)} %bitcast.81), calls=%async_computation.3 | async-start | bytes 1933312
  312.2 8.1 %collective-permute-start.8 = (f32[18,3,768]{2,0,1:T(8,128)S(1)}, f32[18,3,768]{2,0,1:T(8,128)S(1)}, u32[]{:S(2)}, u32[]{:S(2)}) collective-permute-start(f32[18,3,768]{2,0,1:T(8,128)S(1)} %get-tuple-element.167), channel_id=1, source_target_pairs={{0,1},{1,2},{2,3},{3,0},{4,5},{5,6},{6,7},{7,4},{8,9},{9,10},{10,1... | collective-permute-start | bytes 497672 | tf_op jit(solution)/shard_map/ppermute | solution.py:21
  332.8 466.0 %copy-start.1 = (bf16[6,64,768]{2,1,0:T(8,128)(2,1)S(1)}, bf16[6,64,768]{2,1,0:T(8,128)(2,1)}, u32[]{:S(2)}) copy-start(bf16[6,64,768]{2,1,0:T(8,128)(2,1)} %param.34) | copy-start | bytes 1769476
Sparse Core Ops, SparseCore 0:
  148.0 650.8 reduce-scatter.1
where the time goes:
time: 820 us; the launch traced here: 806 us
  waiting for transfers between devices  504 us (61%)
  local copies, waits for them, and re-layouts  157 us (19%)
  matrix products  89.9 us (11%)
  starting transfers between devices  21.6 us (3%)
  other arithmetic  18.7 us (2%)
  between operations  14.7 us (2%)
    reduce_scatter x1, waiting for transfers between devices, on_device(): lax.psum_scatter(grad_full, ('lat', 'lon'), scatter_dimension=0, tiled=True)  456 us
    concatenate x1, local copies, waits for them, and re-layouts, with_halo(): jnp.concatenate([lax.ppermute(tail, axis, [(i, (i + 1) % count) for i in...  42.9 us
    another operation x9, local copies, waits for them, and re-layouts, on_device(): jnp.stack([extended[shift_row:shift_row + LAT_DEV] for shift_row in range...  40.5 us
    dot_general x7, matrix products, on_device(): jnp.einsum('kia,ijkc->iajc', filters[:, :, :, shift_col], basis_grad, pre...  33 us
    dot_general x7, matrix products, on_device(): jnp.einsum('kia,iajc->ikjc', filters[:, :, :, shift_col], windows[:, :, s...  32.7 us
    ppermute x2, waiting for transfers between devices, from_behind(): return lax.ppermute(block, axis, route)  29.6 us
    ppermute x4, starting transfers between devices, with_halo(): lax.ppermute(head, axis, [((i + 1) % count, i) for i in range(count)])  17.5 us
  transfers between devices with their start and end apart: 11, of which 8 were waited for; matrix products, arithmetic and copies ran while one was open for 21% of the time, Pallas kernels for 0%

commit v1 on v0

v1 whole, which is shorter than its diff:
```python
import jax
import jax.numpy as jnp
from jax import lax
from jax.experimental import pallas as pl
from jax.experimental.pallas import tpu as pltpu
from jax.sharding import PartitionSpec as P

CHANNELS = 768
NBASIS = 4
HALO = 3
TAPS = 7
LAT = 32
LON = 4
ROWS = 6
COLS = 64
EDGE = 16
WIN = COLS + 2 * EDGE
EXT = ROWS + 2 * HALO
HALF = CHANNELS // 2
CELLS = ROWS * COLS
BAND = (TAPS + 1) * WIN
SPAN = NBASIS * WIN
BF = jnp.bfloat16
F32 = jnp.float32
BOTH = ("lat", "lon")

VMEM = pl.BlockSpec(memory_space=pltpu.VMEM)
SMEM = pl.BlockSpec(memory_space=pltpu.SMEM)
PARAMS = pltpu.CompilerParams(vmem_limit_bytes=56 * 1024 * 1024)


def route(move):
    pairs = []
    for lat in range(LAT):
        for lon in range(LON):
            to = move(lat, lon)
            if to is not None:
                pairs.append((lat * LON + lon, to[0] * LON + to[1]))
    return pairs


def send(block, move):
    return lax.ppermute(block, BOTH, route(move))


def to_partner(lat, lon):
    return lat, lon ^ 1


def to_chip(lat, lon):
    return lat, lon ^ 2


def down(lat, lon):
    return (lat + 1, lon) if lat + 1 < LAT else None


def up(lat, lon):
    return (lat - 1, lon) if lat > 0 else None


def down_chip(lat, lon):
    return (lat + 1, lon ^ 2) if lat + 1 < LAT else None


def up_chip(lat, lon):
    return (lat - 1, lon ^ 2) if lat > 0 else None


def mirror(lat, lon):
    return (lat, lon ^ 2) if lat in (0, LAT - 1) else None


def bands_kernel(vec_ref, band_ref):
    for i in range(ROWS):
        for k in range(NBASIS):
            row = jnp.broadcast_to(vec_ref[i, k : k + 1, :], (COLS, BAND))
            block = pltpu.roll(row, 0, 1, stride=1, stride_axis=0)
            band_ref[i, k * COLS : (k + 1) * COLS, :] = block.astype(BF)


def pack_kernel(flag, up_ref, down_ref, mirror_ref, edge_ref, up_edge_ref, down_edge_ref, own_edge_ref, out_ref):
    out_ref[:, COLS + EDGE :, :] = edge_ref[...]
    first = flag[1] == 1
    last = flag[2] == 1

    @pl.when(first)
    def _():
        for m in range(HALO):
            out_ref[m, :COLS, :] = mirror_ref[HALO - 1 - m]
            out_ref[m, COLS : COLS + EDGE, :] = own_edge_ref[HALO - 1 - m]

    @pl.when(jnp.logical_not(first))
    def _():
        for m in range(HALO):
            out_ref[m, :COLS, :] = up_ref[m]
            out_ref[m, COLS : COLS + EDGE, :] = up_edge_ref[m]

    @pl.when(last)
    def _():
        for m in range(HALO):
            out_ref[HALO + m, :COLS, :] = mirror_ref[HALO - 1 - m]
            out_ref[HALO + m, COLS : COLS + EDGE, :] = own_edge_ref[ROWS - 1 - m]

    @pl.when(jnp.logical_not(last))
    def _():
        for m in range(HALO):
            out_ref[HALO + m, :COLS, :] = down_ref[m]
            out_ref[HALO + m, COLS : COLS + EDGE, :] = down_edge_ref[m]


def fill_left(x, f0, h0, f1, h1):
    mid = slice(HALO, HALO + ROWS)
    x[mid, :EDGE, :] = h1[:, COLS + EDGE :, :]
    x[mid, EDGE : EDGE + COLS, :] = f0[...]
    x[mid, EDGE + COLS :, :] = f1[:, :EDGE, :]
    for at, src in ((slice(0, HALO), slice(0, HALO)), (slice(HALO + ROWS, EXT), slice(HALO, 2 * HALO))):
        x[at, :EDGE, :] = h1[src, COLS : COLS + EDGE, :]
        x[at, EDGE : EDGE + COLS, :] = h0[src, :COLS, :]
        x[at, EDGE + COLS :, :] = h1[src, :EDGE, :]


def fill_right(x, f0, h0, f1, h1):
    mid = slice(HALO, HALO + ROWS)
    x[mid, :EDGE, :] = f0[:, COLS - EDGE :, :]
    x[mid, EDGE : EDGE + COLS, :] = f1[...]
    x[mid, EDGE + COLS :, :] = h0[:, COLS + EDGE :, :]
    for at, src in ((slice(0, HALO), slice(0, HALO)), (slice(HALO + ROWS, EXT), slice(HALO, 2 * HALO))):
        x[at, :EDGE, :] = h0[src, COLS - EDGE : COLS, :]
        x[at, EDGE : EDGE + COLS, :] = h1[src, :COLS, :]
        x[at, EDGE + COLS :, :] = h0[src, COLS : COLS + EDGE, :]


def grad_kernel(flag, f_own, f_part, h_own, h_part, u_own, u_part, band_ref, g_ref, own_ref, x0, x1, basis, ud):
    core = flag[0]
    for x in (x0, x1):
        x[EXT : EXT + 1, :, :] = jnp.zeros((1, WIN, CHANNELS), BF)

    @pl.when(core == 0)
    def _():
        fill_left(x0, f_own, h_own, f_part, h_part)
        fill_right(x1, f_own, h_own, f_part, h_part)
        ud[:CELLS, :] = u_own[:, :, :HALF].reshape(CELLS, HALF)
        ud[CELLS:, :] = u_part[:, :, :HALF].reshape(CELLS, HALF)

    @pl.when(core == 1)
    def _():
        fill_left(x0, f_part, h_part, f_own, h_own)
        fill_right(x1, f_part, h_part, f_own, h_own)
        ud[:CELLS, :] = u_part[:, :, HALF:].reshape(CELLS, HALF)
        ud[CELLS:, :] = u_own[:, :, HALF:].reshape(CELLS, HALF)

    for i in range(ROWS):
        for w, x in enumerate((x0, x1)):
            cells = x[i : i + TAPS + 1].reshape(BAND, CHANNELS)
            rows = jnp.dot(band_ref[i], cells, preferred_element_type=F32).astype(BF)
            for k in range(NBASIS):
                basis[k, w * CELLS + i * COLS : w * CELLS + (i + 1) * COLS, :] = rows[k * COLS : (k + 1) * COLS]
    for k in range(NBASIS):
        g = lax.dot_general(basis[k], ud[...], (((0,), (0,)), ((), ())), preferred_element_type=F32)
        g_ref[k * CHANNELS : (k + 1) * CHANNELS, :] = g.astype(BF)

    @pl.when(core == 0)
    def _():
        own_ref[...] = basis[:, :CELLS, :]

    @pl.when(core == 1)
    def _():
        own_ref[...] = basis[:, CELLS:, :]


def local_kernel(flag, own_ref, w_ref, vec_ref, u_own, u_part, h_own, h_part, conv_ref, state_ref, x, bg, acc):
    core = flag[0]

    @pl.when(core == 0)
    def _():
        fill_left(x, u_own, h_own, u_part, h_part)

    @pl.when(core == 1)
    def _():
        fill_right(x, u_part, h_part, u_own, h_own)

    total = jnp.zeros((CELLS, CHANNELS), F32)
    for k in range(NBASIS):
        total = total + jnp.dot(own_ref[k], w_ref[k * CHANNELS : (k + 1) * CHANNELS, :], preferred_element_type=F32)
    conv_ref[...] = total.astype(BF).reshape(ROWS, COLS, CHANNELS)
    for k in range(NBASIS):
        wk = w_ref[k * CHANNELS : (k + 1) * CHANNELS, :]
        for part in range(3):
            cells = x[part * 4 : (part + 1) * 4].reshape(4 * WIN, CHANNELS)
            got = lax.dot_general(cells, wk, (((1,), (1,)), ((), ())), preferred_element_type=F32)
            bg[part * 4 : (part + 1) * 4, k * WIN : (k + 1) * WIN, :] = got.astype(BF).reshape(4, WIN, CHANNELS)
    acc[...] = jnp.zeros((ROWS, COLS, CHANNELS), F32)
    for e in range(EXT):
        rows = [r for r in range(ROWS) if 0 <= r + TAPS - 1 - e < TAPS]
        blocks = []
        for r in rows:
            a = r + TAPS - 1 - e
            row = jnp.broadcast_to(vec_ref[e, a : a + 1, :], (COLS, SPAN))
            blocks.append(pltpu.roll(row, 0, 1, stride=1, stride_axis=0).astype(BF))
        got = jnp.dot(jnp.concatenate(blocks, 0), bg[e], preferred_element_type=F32)
        for n, r in enumerate(rows):
            acc[r] += got[n * COLS : (n + 1) * COLS]
    state_ref[...] = acc[...].astype(BF)


def support_filter(filter_rows, widths, offsets, reaches):
    tap_ids = jnp.arange(TAPS, dtype=jnp.int32)
    lat_keep = (tap_ids[None, :] >= offsets[:, None]) & (
        tap_ids[None, :] < offsets[:, None] + widths[:, None]
    )
    lon_keep = jnp.abs(tap_ids - HALO)[None, :] <= reaches[:, None]
    kept_taps = lat_keep[None, :, :, None] & lon_keep[None, :, None, :]
    return jnp.where(kept_taps, filter_rows, jnp.zeros_like(filter_rows))


def extended_filters(filter_basis, lat_width, lat_offset, lon_reach, lat):
    start = lat * ROWS

    def rows(at, size):
        return support_filter(
            lax.dynamic_slice_in_dim(filter_basis, at, size, 1),
            lax.dynamic_slice_in_dim(lat_width, at, size, 0),
            lax.dynamic_slice_in_dim(lat_offset, at, size, 0),
            lax.dynamic_slice_in_dim(lon_reach, at, size, 0),
        )

    above = rows(jnp.maximum(start - HALO, 0), HALO)
    below = rows(jnp.minimum(start + ROWS, LAT * ROWS - HALO), HALO)
    above = jnp.where(lat == 0, above[:, ::-1, ::-1], above)
    below = jnp.where(lat == LAT - 1, below[:, ::-1, ::-1], below)
    return jnp.concatenate([above, rows(start, ROWS), below], 1)


def halo(field, core, lat, flag):
    edge = jnp.where(core == 0, field[:, :EDGE], field[:, COLS - EDGE :])
    head, tail = field[:HALO], field[ROWS - HALO :]
    from_up = send(tail, down)
    from_down = send(head, up)
    mirrored = send(jnp.where(lat == 0, head, tail), mirror)
    from_chip = send(edge, to_chip)
    up_edge = send(edge[ROWS - HALO :], down_chip)
    down_edge = send(edge[:HALO], up_chip)
    return pl.pallas_call(
        pack_kernel,
        out_shape=jax.ShapeDtypeStruct((ROWS, WIN, CHANNELS), BF),
        in_specs=[SMEM] + [VMEM] * 7,
        out_specs=VMEM,
        compiler_params=PARAMS,
        name="pack",
    )(flag, from_up, from_down, mirrored, from_chip, up_edge, down_edge, edge)


def on_device(features, upstream, weights, filter_basis, lat_width, lat_offset, lon_reach):
    lat = lax.axis_index("lat")
    core = lax.axis_index("lon") % 2
    flag = jnp.stack([core, lat == 0, lat == LAT - 1]).astype(jnp.int32)

    f_part = send(features, to_partner)
    u_part = send(upstream, to_partner)
    h_own = halo(features, core, lat, flag)
    h_part = send(h_own, to_partner)

    filters = extended_filters(filter_basis, lat_width, lat_offset, lon_reach, lat).astype(F32)
    own_rows = jnp.transpose(filters[:, HALO : HALO + ROWS], (1, 0, 2, 3))
    at = EDGE - HALO
    band_vec = jnp.pad(own_rows, ((0, 0), (0, 0), (0, 1), (at, WIN - at - TAPS))).reshape(ROWS, NBASIS, BAND)
    spread_rows = jnp.transpose(filters[:, :, :, ::-1], (1, 2, 0, 3))
    spread_vec = jnp.pad(spread_rows, ((0, 0), (0, 0), (0, 0), (at, WIN - at - TAPS))).reshape(EXT, TAPS, SPAN)
    bands = pl.pallas_call(
        bands_kernel,
        out_shape=jax.ShapeDtypeStruct((ROWS, NBASIS * COLS, BAND), BF),
        in_specs=[VMEM],
        out_specs=VMEM,
        compiler_params=PARAMS,
        name="bands",
    )(band_vec)

    partial, basis_own = pl.pallas_call(
        grad_kernel,
        out_shape=(
            jax.ShapeDtypeStruct((NBASIS * CHANNELS, HALF), BF),
            jax.ShapeDtypeStruct((NBASIS, CELLS, CHANNELS), BF),
        ),
        in_specs=[SMEM] + [VMEM] * 7,
        out_specs=(VMEM, VMEM),
        scratch_shapes=[
            pltpu.VMEM((EXT + 1, WIN, CHANNELS), BF),
            pltpu.VMEM((EXT + 1, WIN, CHANNELS), BF),
            pltpu.VMEM((NBASIS, 2 * CELLS, CHANNELS), BF),
            pltpu.VMEM((2 * CELLS, HALF), BF),
        ],
        compiler_params=PARAMS,
        cost_estimate=pl.CostEstimate(flops=5_400_000_000, bytes_accessed=12_000_000, transcendentals=0),
        name="grad",
    )(flag, features, f_part, h_own, h_part, upstream, u_part, bands)

    pieces = lax.all_to_all(partial.reshape(LAT * LON, 24, HALF), BOTH, 0, 0, tiled=True)

    hu_own = halo(upstream, core, lat, flag)
    hu_part = send(hu_own, to_partner)
    convolved, state_grad = pl.pallas_call(
        local_kernel,
        out_shape=(
            jax.ShapeDtypeStruct((ROWS, COLS, CHANNELS), BF),
            jax.ShapeDtypeStruct((ROWS, COLS, CHANNELS), BF),
        ),
        in_specs=[SMEM] + [VMEM] * 7,
        out_specs=(VMEM, VMEM),
        scratch_shapes=[
            pltpu.VMEM((EXT, WIN, CHANNELS), BF),
            pltpu.VMEM((EXT, SPAN, CHANNELS), BF),
            pltpu.VMEM((ROWS, COLS, CHANNELS), F32),
        ],
        compiler_params=PARAMS,
        cost_estimate=pl.CostEstimate(flops=9_000_000_000, bytes_accessed=12_000_000, transcendentals=0),
        name="local",
    )(flag, basis_own, weights, spread_vec, upstream, u_part, hu_own, hu_part)

    summed = pieces.astype(F32).reshape(LAT * LON // 2, 2, 24, HALF).sum(0)
    weight_grad = jnp.concatenate([summed[0], summed[1]], 1)
    return convolved, state_grad, weight_grad


def solution(mesh):
    return jax.shard_map(
        on_device,
        mesh=mesh,
        in_specs=(P("lat", "lon", None), P("lat", "lon", None), P(), P(), P(), P(), P()),
        out_specs=(P("lat", "lon", None), P("lat", "lon", None), P(("lat", "lon"), None)),
        check_vma=False,
    )
```

time: 820 us -> 129 us (0.16); the launches traced: 806 us -> 128 us
  waiting for transfers between devices: 504 us -> 41.3 us
  local copies, waits for them, and re-layouts: 157 us -> 6.96 us
  matrix products: 89.9 us -> 0 us
  Pallas kernels: 0 us -> 34.4 us
  starting transfers between devices: 21.6 us -> 37.5 us
  between operations: 14.7 us -> 1.07 us
  other arithmetic: 18.7 us -> 6.2 us
    reduce_scatter x1 -> x0, waiting for transfers between devices: 456 us -> none  [on_device(): lax.psum_scatter(grad_full, ('lat', 'lon'), scatter_dimension=0, tiled=True)]
    dot_general x18 -> x0, matrix products: 89.9 us -> none  [the longest x7 33 us: on_device(): jnp.einsum('kia,ijkc->iajc', filters[:, :, :, shift_col], basis_grad, pre...]
    scatter-add x5 -> x0, local copies, waits for them, and re-layouts: 49.2 us -> none  [the longest x1 13.1 us: on_device(): middle.at[:HALO].add(jnp.where(is_first, returned[:HALO], zero_rim))]
    concatenate x3 -> x0, local copies, waits for them, and re-layouts: 43.1 us -> none  [the longest x1 42.9 us: with_halo(): jnp.concatenate([lax.ppermute(tail, axis, [(i, (i + 1) % count) for i in...]
    another operation x9 -> x0, local copies, waits for them, and re-layouts: 40.5 us -> none  [on_device(): jnp.stack([extended[shift_row:shift_row + LAT_DEV] for shift_row in range...]
    pallas_call x0 -> x5, Pallas kernels: none -> 34.4 us  [the longest x1 14.9 us: on_device(): pl.pallas_call(local_kernel, out_shape=(jax.ShapeDtypeStruct((ROWS, COLS,...]
    all_to_all x0 -> x1, starting transfers between devices: none -> 10.3 us  [on_device(): lax.all_to_all(partial.reshape(LAT * LON, 24, HALF), BOTH, 0, 0, tiled=True)]
    add x5 -> x0, other arithmetic: 10.3 us -> none  [the longest x1 4.76 us: on_device(): middle.at[:HALO].add(jnp.where(is_first, returned[:HALO], zero_rim))]
  transfers between devices with their start and end apart: 11 -> 17, of which waited for: 8 -> 6; matrix products, arithmetic and copies ran while one was open for 21% -> 7% of each run, Pallas kernels for 0% -> 18%
where the time goes in v1:
time: 129 us; the launch traced here: 128 us
  waiting for transfers between devices  41.3 us (32%)
  starting transfers between devices  37.5 us (29%)
  Pallas kernels  34.4 us (27%)
  local copies, waits for them, and re-layouts  6.96 us (5%)
  other arithmetic  6.2 us (5%)
    ppermute x16, waiting for transfers between devices, send(): return lax.ppermute(block, BOTH, route(move))  41.3 us
    ppermute x16, starting transfers between devices, send(): return lax.ppermute(block, BOTH, route(move))  27.2 us
    pallas_call x1, Pallas kernels, on_device(): pl.pallas_call(local_kernel, out_shape=(jax.ShapeDtypeStruct((ROWS, COLS,...  14.9 us
    pallas_call x1, Pallas kernels, on_device(): pl.pallas_call(grad_kernel, out_shape=(jax.ShapeDtypeStruct((NBASIS * CHA...  11.8 us
    all_to_all x1, starting transfers between devices, on_device(): lax.all_to_all(partial.reshape(LAT * LON, 24, HALF), BOTH, 0, 0, tiled=True)  10.3 us
    pallas_call x2, Pallas kernels, halo(): pl.pallas_call(pack_kernel, out_shape=jax.ShapeDtypeStruct((ROWS, WIN, CH...  4.7 us
    pallas_call x1, Pallas kernels, on_device(): pl.pallas_call(bands_kernel, out_shape=jax.ShapeDtypeStruct((ROWS, NBASIS...  2.99 us
  transfers between devices with their start and end apart: 17, of which 6 were waited for; matrix products, arithmetic and copies ran while one was open for 7% of the time, Pallas kernels for 18%

profile of v1, /device:TPU:0, one launch (start us, length us, event | category | flops | bytes accessed | tf_op | source)
XLA Modules:
  0.0 127.5 jit_solution(12450688702995787146)
XLA Ops:
  0.6 0.0 copy-start.2
  0.7 0.0 copy-start.3
  0.7 1.1 slice_select_fusion.1.own_edge_ref
  1.8 1.7 %collective-permute-start.4 = (bf16[6,16,768]{2,1,0:T(8,128)(2,1)S(1)}, bf16[6,16,768]{2,1,0:T(8,128)(2,1)}, u32[]{:S(2)}, u32[]{:S(2)}) collective-permute-start(bf16[6,16,768]{2,1,0:T(8,128)(2,1)S(1)} %slice_select_fusion.1.own_edge_ref), channel_id=1, source_target_pairs={{0,2},{1,3},{2,0},{3,1},{4,6},{5,7},{6,4},{7,5},{8,10},{9,11},{10,... | collective-permute-start | bytes 442376 | tf_op jit(solution)/shard_map/ppermute | solution.py:43
  3.5 0.7 fusion.4
  4.2 3.3 %collective-permute-start.5 = (bf16[3,16,768]{2,1,0:T(8,128)(2,1)}, bf16[3,16,768]{2,1,0:T(8,128)(2,1)S(1)}, u32[]{:S(2)}, u32[]{:S(2)}) collective-permute-start(bf16[3,16,768]{2,1,0:T(8,128)(2,1)} %get-tuple-element.26), channel_id=1, source_target_pairs={{0,6},{1,7},{2,4},{3,5},{4,10},{5,11},{6,8},{7,9},{8,14},{9,15},{1... | collective-permute-start | bytes 221192 | tf_op jit(solution)/shard_map/ppermute | solution.py:43
  7.5 1.1 broadcast_select_fusion.1
  8.6 3.4 %collective-permute-start.1 = (bf16[3,64,768]{2,1,0:T(8,128)(2,1)S(1)}, bf16[3,64,768]{2,1,0:T(8,128)(2,1)S(1)}, u32[]{:S(2)}, u32[]{:S(2)}) collective-permute-start(bf16[3,64,768]{2,1,0:T(8,128)(2,1)S(1)} %get-tuple-element.22), channel_id=1, source_target_pairs={{0,4},{1,5},{2,6},{3,7},{4,8},{5,9},{6,10},{7,11},{8,12},{9,13},{1... | collective-permute-start | bytes 884744 | tf_op jit(solution)/shard_map/ppermute | solution.py:43
  12.0 1.3 %collective-permute-start.2 = (bf16[3,64,768]{2,1,0:T(8,128)(2,1)S(1)}, bf16[3,64,768]{2,1,0:T(8,128)(2,1)S(1)}, u32[]{:S(2)}, u32[]{:S(2)}) collective-permute-start(bf16[3,64,768]{2,1,0:T(8,128)(2,1)S(1)} %get-tuple-element.21), channel_id=1, source_target_pairs={{4,0},{5,1},{6,2},{7,3},{8,4},{9,5},{10,6},{11,7},{12,8},{13,9},{1... | collective-permute-start | bytes 884744 | tf_op jit(solution)/shard_map/ppermute | solution.py:43
  13.3 3.5 %collective-permute-start.3 = (bf16[3,64,768]{2,1,0:T(8,128)(2,1)S(1)}, bf16[3,64,768]{2,1,0:T(8,128)(2,1)S(1)}, u32[]{:S(2)}, u32[]{:S(2)}) collective-permute-start(bf16[3,64,768]{2,1,0:T(8,128)(2,1)S(1)} %get-tuple-element.20), channel_id=1, source_target_pairs={{0,2},{1,3},{2,0},{3,1},{124,126},{125,127},{126,124},{127,125}} | collective-permute-start | bytes 884744 | tf_op jit(solution)/shard_map/ppermute | solution.py:43
  16.8 0.8 dynamic_slice.42
  17.6 0.8 dynamic-slice_add_fusion.1
  18.4 0.8 dynamic-slice_add_fusion.2
  19.2 0.1 broadcast_compare_fusion.2
  19.3 0.2 dynamic-slice_select_fusion.2
  19.5 0.2 rev.10
  19.7 0.1 fusion.1
  19.8 1.3 %collective-permute-start.6 = (bf16[3,16,768]{2,1,0:T(8,128)(2,1)}, bf16[3,16,768]{2,1,0:T(8,128)(2,1)S(1)}, u32[]{:S(2)}, u32[]{:S(2)}) collective-permute-start(bf16[3,16,768]{2,1,0:T(8,128)(2,1)} %get-tuple-element.25), channel_id=1, source_target_pairs={{4,2},{5,3},{6,0},{7,1},{8,6},{9,7},{10,4},{11,5},{12,10},{13,11},... | collective-permute-start | bytes 221192 | tf_op jit(solution)/shard_map/ppermute | solution.py:43
  21.1 0.7 pad_add_fusion.flag
  21.7 5.5 %collective-permute-done.6.down_edge_ref = bf16[3,16,768]{2,1,0:T(8,128)(2,1)S(1)} collective-permute-done((bf16[3,16,768]{2,1,0:T(8,128)(2,1)}, bf16[3,16,768]{2,1,0:T(8,128)(2,1)S(1)}, u32[]{:S(2)}, u32[]{:S(2)}) %collective-permute-start.6) | collective-permute-done | bytes 73760 | tf_op jit(solution)/shard_map/ppermute | solution.py:43
  27.3 0.0 collective-permute-done.4.edge_ref
  27.3 0.5 collective-permute-start.8
  27.8 0.0 collective-permute-done.2.down_ref
  27.8 0.0 copy-start.6
  27.8 2.8 %collective-permute-done.3.mirror_ref = bf16[3,64,768]{2,1,0:T(8,128)(2,1)S(1)} collective-permute-done((bf16[3,64,768]{2,1,0:T(8,128)(2,1)S(1)}, bf16[3,64,768]{2,1,0:T(8,128)(2,1)S(1)}, u32[]{:S(2)}, u32[]{:S(2)}) %collective-permute-start.3) | collective-permute-done | bytes 294944 | tf_op jit(solution)/shard_map/ppermute | solution.py:43
  30.6 0.7 copy-done.7
  31.3 2.4 %pack.2.h_own = bf16[6,96,768]{2,1,0:T(8,128)(2,1)} custom-call(s32[3]{0:T(128)} %pad_add_fusion.flag, bf16[3,64,768]{2,1,0:T(8,128)(2,1)} %copy-done.5, bf16[3,64,768]{2,1,0:T(8,128)(2,1)} %copy-done.6, bf16[3,64,768]{2,1,0:T(8,128)(2,1)} %copy-done.7, bf16[6,16,768]{2,1,0:T(8,128)(2,1)} %collective-permute-done.4.edge_ref, bf16[3,16,768]{2,1,0:T(8,128)(2,1)} %copy-done.13, ...), custom_call_target="tpu_custom_call" | custom-call | tf_op jit(solution)/shard_map/pack/pallas_call | solution.py:244
  33.7 0.0 collective-permute-start.7
  33.7 0.1 dynamic-slice_select_fusion.1
  33.8 0.2 rev.9
  34.0 0.1 maximum_convert_fusion
  34.2 0.1 slice_bitcast_fusion
  34.3 0.2 pad.8
  34.5 1.3 copy.12.vec_ref
  35.8 3.0 %bands.1.band_ref = bf16[6,256,768]{2,1,0:T(8,128)(2,1)} custom-call(f32[6,4,768]{2,1,0:T(4,128)} %copy.12.vec_ref), custom_call_target="tpu_custom_call" | custom-call | tf_op jit(solution)/shard_map/bands/pallas_call | solution.py:270
  38.8 0.0 collective-permute-done.8.u_part
  38.8 0.0 collective-permute-done.f_part
  38.8 0.0 collective-permute-done.7.h_part
  38.8 11.8 %grad.1 = (bf16[3072,384]{1,0:T(8,128)(2,1)}, bf16[4,384,768]{2,1,0:T(8,128)(2,1)}) custom-call(s32[3]{0:T(128)} %pad_add_fusion.flag, bf16[6,64,768]{2,1,0:T(8,128)(2,1)} %f_own.1, bf16[6,64,768]{2,1,0:T(8,128)(2,1)} %collective-permute-done.f_part, bf16[6,96,768]{2,1,0:T(8,128)(2,1)} %pack.2.h_own, bf16[6,96,768]{2,1,0:T(8,128)(2,1)} %collective-permute-done.7.h_part, ...), custom_call_target="tpu_custom_call" | custom-call | flops 5400000000 | bytes 12000000 | tf_op jit(solution)/shard_map/grad/pallas_call | solution.py:279
  50.6 10.3 %all-to-all-start = ((bf16[128,24,384]{2,1,0:T(8,128)(2,1)}), bf16[128,24,384]{2,1,0:T(8,128)(2,1)S(1)}, u32[]{:S(2)}, u32[]{:S(2)}) async-start(bf16[128,24,384]{2,1,0:T(8,128)(2,1)} %bitcast.17), calls=%async_computation | async-start | bytes 4718592 | tf_op jit(solution)/shard_map/all_to_all | solution.py:298
  61.0 0.1 broadcast_select_fusion
  61.0 1.3 %collective-permute-start.10 = (bf16[3,64,768]{2,1,0:T(8,128)(2,1)S(1)}, bf16[3,64,768]{2,1,0:T(8,128)(2,1)S(1)}, u32[]{:S(2)}, u32[]{:S(2)}) collective-permute-start(bf16[3,64,768]{2,1,0:T(8,128)(2,1)S(1)} %get-tuple-element.18), channel_id=1, source_target_pairs={{4,0},{5,1},{6,2},{7,3},{8,4},{9,5},{10,6},{11,7},{12,8},{13,9},{1... | collective-permute-start | bytes 884744 | tf_op jit(solution)/shard_map/ppermute | solution.py:43
  62.3 2.9 %collective-permute-start.11 = (bf16[3,64,768]{2,1,0:T(8,128)(2,1)S(1)}, bf16[3,64,768]{2,1,0:T(8,128)(2,1)S(1)}, u32[]{:S(2)}, u32[]{:S(2)}) collective-permute-start(bf16[3,64,768]{2,1,0:T(8,128)(2,1)S(1)} %get-tuple-element.17), channel_id=1, source_target_pairs={{0,2},{1,3},{2,0},{3,1},{124,126},{125,127},{126,124},{127,125}} | collective-permute-start | bytes 884744 | tf_op jit(solution)/shard_map/ppermute | solution.py:43
  65.2 2.4 %collective-permute-start.9 = (bf16[3,64,768]{2,1,0:T(8,128)(2,1)S(1)}, bf16[3,64,768]{2,1,0:T(8,128)(2,1)S(1)}, u32[]{:S(2)}, u32[]{:S(2)}) collective-permute-start(bf16[3,64,768]{2,1,0:T(8,128)(2,1)S(1)} %get-tuple-element.19), channel_id=1, source_target_pairs={{0,4},{1,5},{2,6},{3,7},{4,8},{5,9},{6,10},{7,11},{8,12},{9,13},{1... | collective-permute-start | bytes 884744 | tf_op jit(solution)/shard_map/ppermute | solution.py:43
  67.6 3.8 %collective-permute-start.13 = (bf16[3,16,768]{2,1,0:T(8,128)(2,1)S(1)}, bf16[3,16,768]{2,1,0:T(8,128)(2,1)S(1)}, u32[]{:S(2)}, u32[]{:S(2)}) collective-permute-start(bf16[3,16,768]{2,1,0:T(8,128)(2,1)S(1)} %get-tuple-element.24), channel_id=1, source_target_pairs={{0,6},{1,7},{2,4},{3,5},{4,10},{5,11},{6,8},{7,9},{8,14},{9,15},{1... | collective-permute-start | bytes 221192 | tf_op jit(solution)/shard_map/ppermute | solution.py:43
  71.4 0.6 collective-permute-start.12
  72.0 21.3 %collective-permute-done.13.up_edge_ref = bf16[3,16,768]{2,1,0:T(8,128)(2,1)S(1)} collective-permute-done((bf16[3,16,768]{2,1,0:T(8,128)(2,1)S(1)}, bf16[3,16,768]{2,1,0:T(8,128)(2,1)S(1)}, u32[]{:S(2)}, u32[]{:S(2)}) %collective-permute-start.13) | collective-permute-done | bytes 73760 | tf_op jit(solution)/shard_map/ppermute | solution.py:43
  93.3 1.3 %collective-permute-start.14 = (bf16[3,16,768]{2,1,0:T(8,128)(2,1)S(1)}, bf16[3,16,768]{2,1,0:T(8,128)(2,1)S(1)}, u32[]{:S(2)}, u32[]{:S(2)}) collective-permute-start(bf16[3,16,768]{2,1,0:T(8,128)(2,1)S(1)} %get-tuple-element.23), channel_id=1, source_target_pairs={{4,2},{5,3},{6,0},{7,1},{8,6},{9,7},{10,4},{11,5},{12,10},{13,11},... | collective-permute-start | bytes 221192 | tf_op jit(solution)/shard_map/ppermute | solution.py:43
  94.6 6.4 %collective-permute-done.14.down_edge_ref = bf16[3,16,768]{2,1,0:T(8,128)(2,1)S(1)} collective-permute-done((bf16[3,16,768]{2,1,0:T(8,128)(2,1)S(1)}, bf16[3,16,768]{2,1,0:T(8,128)(2,1)S(1)}, u32[]{:S(2)}, u32[]{:S(2)}) %collective-permute-start.14) | collective-permute-done | bytes 73760 | tf_op jit(solution)/shard_map/ppermute | solution.py:43
  101.0 3.9 %collective-permute-done.12.edge_ref = bf16[6,16,768]{2,1,0:T(8,128)(2,1)S(1)} collective-permute-done((bf16[6,16,768]{2,1,0:T(8,128)(2,1)S(1)}, bf16[6,16,768]{2,1,0:T(8,128)(2,1)S(1)}, u32[]{:S(2)}, u32[]{:S(2)}) %collective-permute-start.12) | collective-permute-done | bytes 147488 | tf_op jit(solution)/shard_map/ppermute | solution.py:43
  104.9 0.0 collective-permute-done.10.down_ref
  105.0 0.6 copy-done.12
  105.6 0.1 copy-done.8
  105.7 0.1 copy-done.9
  105.8 0.7 copy-done.10
  106.5 2.3 %pack.3.h_own = bf16[6,96,768]{2,1,0:T(8,128)(2,1)} custom-call(s32[3]{0:T(128)} %pad_add_fusion.flag, bf16[3,64,768]{2,1,0:T(8,128)(2,1)} %copy-done.10, bf16[3,64,768]{2,1,0:T(8,128)(2,1)} %copy-done.8, bf16[3,64,768]{2,1,0:T(8,128)(2,1)} %copy-done.9, bf16[6,16,768]{2,1,0:T(8,128)(2,1)} %copy-done.12, bf16[3,16,768]{2,1,0:T(8,128)(2,1)} %copy-done.15, ...), custom_call_target="tpu_custom_call" | custom-call | tf_op jit(solution)/shard_map/pack/pallas_call | solution.py:244
  108.8 0.0 collective-permute-start.15
  108.8 0.3 copy.13
  109.1 0.2 pad.9.clone
  109.3 0.8 reshape.255.vec_ref
  110.1 1.5 %collective-permute-done.15.h_part = bf16[6,96,768]{2,1,0:T(8,128)(2,1)} collective-permute-done((bf16[6,96,768]{2,1,0:T(8,128)(2,1)}, bf16[6,96,768]{2,1,0:T(8,128)(2,1)}, u32[]{:S(2)}, u32[]{:S(2)}) %collective-permute-start.15) | collective-permute-done | bytes 884768 | tf_op jit(solution)/shard_map/ppermute | solution.py:43
  111.6 14.9 %local.1 = (bf16[6,64,768]{2,1,0:T(8,128)(2,1)}, bf16[6,64,768]{2,1,0:T(8,128)(2,1)}) custom-call(s32[3]{0:T(128)} %pad_add_fusion.flag, bf16[4,384,768]{2,1,0:T(8,128)(2,1)} %get-tuple-element.7.own_ref, bf16[3072,768]{1,0:T(8,128)(2,1)} %w_ref.1, f32[12,7,384]{2,1,0:T(8,128)} %reshape.255.vec_ref, bf16[6,64,768]{2,1,0:T(8,128)(2,1)} %u_own.3, ...), custom_call_target="tpu_custom_call" | custom-call | flops 8999999488 | bytes 12000000 | tf_op jit(solution)/shard_map/local/pallas_call | solution.py:302
  126.5 0.3 convert_reduce_fusion
  126.9 0.6 pad_maximum_fusion
  (44 shorter events, 0.2 us)
Async XLA Ops:
  0.6 26.6 %copy-start.2 = (bf16[6,64,768]{2,1,0:T(8,128)(2,1)S(1)}, bf16[6,64,768]{2,1,0:T(8,128)(2,1)}, u32[]{:S(2)}) copy-start(bf16[6,64,768]{2,1,0:T(8,128)(2,1)} %f_own.1) | copy-start | bytes 1769476
  0.6 18.7 %copy-start.11 = (bf16[4,192,7,7]{1,0,3,2:T(4,128)(2,1)S(1)}, bf16[4,192,7,7]{1,0,3,2:T(4,128)(2,1)}, u32[]{:S(2)}) copy-start(bf16[4,192,7,7]{1,0,3,2:T(4,128)(2,1)} %param.10) | copy-start | bytes 225796
  0.7 26.6 %copy-start.3 = (bf16[6,64,768]{2,1,0:T(8,128)(2,1)S(1)}, bf16[6,64,768]{2,1,0:T(8,128)(2,1)}, u32[]{:S(2)}) copy-start(bf16[6,64,768]{2,1,0:T(8,128)(2,1)} %u_own.3) | copy-start | bytes 1769476
  1.8 28.8 %copy-start = (bf16[6,16,768]{2,1,0:T(8,128)(2,1)}, bf16[6,16,768]{2,1,0:T(8,128)(2,1)S(1)}, u32[]{:S(2)}) copy-start(bf16[6,16,768]{2,1,0:T(8,128)(2,1)S(1)} %slice_select_fusion.1.own_edge_ref) | copy-start | bytes 442372
  1.8 25.5 %collective-permute-start.4 = (bf16[6,16,768]{2,1,0:T(8,128)(2,1)S(1)}, bf16[6,16,768]{2,1,0:T(8,128)(2,1)}, u32[]{:S(2)}, u32[]{:S(2)}) collective-permute-start(bf16[6,16,768]{2,1,0:T(8,128)(2,1)S(1)} %slice_select_fusion.1.own_edge_ref), channel_id=1, source_target_pairs={{0,2},{1,3},{2,0},{3,1},{4,6},{5,7},{6,4},{7,5},{8,10},{9,11},{10,... | collective-permute-start | bytes 442376 | tf_op jit(solution)/shard_map/ppermute | solution.py:43
  4.2 15.6 %collective-permute-start.5 = (bf16[3,16,768]{2,1,0:T(8,128)(2,1)}, bf16[3,16,768]{2,1,0:T(8,128)(2,1)S(1)}, u32[]{:S(2)}, u32[]{:S(2)}) collective-permute-start(bf16[3,16,768]{2,1,0:T(8,128)(2,1)} %get-tuple-element.26), channel_id=1, source_target_pairs={{0,6},{1,7},{2,4},{3,5},{4,10},{5,11},{6,8},{7,9},{8,14},{9,15},{1... | collective-permute-start | bytes 221192 | tf_op jit(solution)/shard_map/ppermute | solution.py:43
  8.6 19.2 %collective-permute-start.1 = (bf16[3,64,768]{2,1,0:T(8,128)(2,1)S(1)}, bf16[3,64,768]{2,1,0:T(8,128)(2,1)S(1)}, u32[]{:S(2)}, u32[]{:S(2)}) collective-permute-start(bf16[3,64,768]{2,1,0:T(8,128)(2,1)S(1)} %get-tuple-element.22), channel_id=1, source_target_pairs={{0,4},{1,5},{2,6},{3,7},{4,8},{5,9},{6,10},{7,11},{8,12},{9,13},{1... | collective-permute-start | bytes 884744 | tf_op jit(solution)/shard_map/ppermute | solution.py:43
  12.0 15.7 %collective-permute-start.2 = (bf16[3,64,768]{2,1,0:T(8,128)(2,1)S(1)}, bf16[3,64,768]{2,1,0:T(8,128)(2,1)S(1)}, u32[]{:S(2)}, u32[]{:S(2)}) collective-permute-start(bf16[3,64,768]{2,1,0:T(8,128)(2,1)S(1)} %get-tuple-element.21), channel_id=1, source_target_pairs={{4,0},{5,1},{6,2},{7,3},{8,4},{9,5},{10,6},{11,7},{12,8},{13,9},{1... | collective-permute-start | bytes 884744 | tf_op jit(solution)/shard_map/ppermute | solution.py:43
  13.3 17.2 %collective-permute-start.3 = (bf16[3,64,768]{2,1,0:T(8,128)(2,1)S(1)}, bf16[3,64,768]{2,1,0:T(8,128)(2,1)S(1)}, u32[]{:S(2)}, u32[]{:S(2)}) collective-permute-start(bf16[3,64,768]{2,1,0:T(8,128)(2,1)S(1)} %get-tuple-element.20), channel_id=1, source_target_pairs={{0,2},{1,3},{2,0},{3,1},{124,126},{125,127},{126,124},{127,125}} | collective-permute-start | bytes 884744 | tf_op jit(solution)/shard_map/ppermute | solution.py:43
  19.8 10.8 %copy-start.13 = (bf16[3,16,768]{2,1,0:T(8,128)(2,1)}, bf16[3,16,768]{2,1,0:T(8,128)(2,1)S(1)}, u32[]{:S(2)}) copy-start(bf16[3,16,768]{2,1,0:T(8,128)(2,1)S(1)} %collective-permute-done.5.up_edge_ref) | copy-start | bytes 221188
  19.8 7.5 %collective-permute-start.6 = (bf16[3,16,768]{2,1,0:T(8,128)(2,1)}, bf16[3,16,768]{2,1,0:T(8,128)(2,1)S(1)}, u32[]{:S(2)}, u32[]{:S(2)}) collective-permute-start(bf16[3,16,768]{2,1,0:T(8,128)(2,1)} %get-tuple-element.25), channel_id=1, source_target_pairs={{4,2},{5,3},{6,0},{7,1},{8,6},{9,7},{10,4},{11,5},{12,10},{13,11},... | collective-permute-start | bytes 221192 | tf_op jit(solution)/shard_map/ppermute | solution.py:43
  27.2 3.3 %copy-start.14 = (bf16[3,16,768]{2,1,0:T(8,128)(2,1)}, bf16[3,16,768]{2,1,0:T(8,128)(2,1)S(1)}, u32[]{:S(2)}) copy-start(bf16[3,16,768]{2,1,0:T(8,128)(2,1)S(1)} %collective-permute-done.6.down_edge_ref) | copy-start | bytes 221188
  27.2 11.6 %collective-permute-start = (bf16[6,64,768]{2,1,0:T(8,128)(2,1)S(1)}, bf16[6,64,768]{2,1,0:T(8,128)(2,1)}, u32[]{:S(2)}, u32[]{:S(2)}) collective-permute-start(bf16[6,64,768]{2,1,0:T(8,128)(2,1)S(1)} %copy-done.2), channel_id=1, source_target_pairs={{0,1},{1,0},{2,3},{3,2},{4,5},{5,4},{6,7},{7,6},{8,9},{9,8},{10,11... | collective-permute-start | bytes 1769480 | tf_op jit(solution)/shard_map/ppermute | solution.py:43
  27.3 11.5 %collective-permute-start.8 = (bf16[6,64,768]{2,1,0:T(8,128)(2,1)S(1)}, bf16[6,64,768]{2,1,0:T(8,128)(2,1)}, u32[]{:S(2)}, u32[]{:S(2)}) collective-permute-start(bf16[6,64,768]{2,1,0:T(8,128)(2,1)S(1)} %copy-done.3), channel_id=1, source_target_pairs={{0,1},{1,0},{2,3},{3,2},{4,5},{5,4},{6,7},{7,6},{8,9},{9,8},{10,11... | collective-permute-start | bytes 1769480 | tf_op jit(solution)/shard_map/ppermute | solution.py:43
  27.8 2.8 %copy-start.5 = (bf16[3,64,768]{2,1,0:T(8,128)(2,1)}, bf16[3,64,768]{2,1,0:T(8,128)(2,1)S(1)}, u32[]{:S(2)}) copy-start(bf16[3,64,768]{2,1,0:T(8,128)(2,1)S(1)} %collective-permute-done.1.up_ref) | copy-start | bytes 884740
  27.8 2.8 %copy-start.6 = (bf16[3,64,768]{2,1,0:T(8,128)(2,1)}, bf16[3,64,768]{2,1,0:T(8,128)(2,1)S(1)}, u32[]{:S(2)}) copy-start(bf16[3,64,768]{2,1,0:T(8,128)(2,1)S(1)} %collective-permute-done.2.down_ref) | copy-start | bytes 884740
  30.6 0.7 copy-start.7
  33.7 5.1 %collective-permute-start.7 = (bf16[6,96,768]{2,1,0:T(8,128)(2,1)}, bf16[6,96,768]{2,1,0:T(8,128)(2,1)}, u32[]{:S(2)}, u32[]{:S(2)}) collective-permute-start(bf16[6,96,768]{2,1,0:T(8,128)(2,1)} %pack.2.h_own), channel_id=1, source_target_pairs={{0,1},{1,0},{2,3},{3,2},{4,5},{5,4},{6,7},{7,6},{8,9},{9,8},{10,11... | collective-permute-start | bytes 2654216 | tf_op jit(solution)/shard_map/ppermute | solution.py:43
  50.6 10.3 %copy-start.4 = (bf16[6,64,768]{2,1,0:T(8,128)(2,1)S(1)}, bf16[6,64,768]{2,1,0:T(8,128)(2,1)}, u32[]{:S(2)}) copy-start(bf16[6,64,768]{2,1,0:T(8,128)(2,1)} %u_own.3) | copy-start | bytes 1769476
  50.6 75.9 %all-to-all-start = ((bf16[128,24,384]{2,1,0:T(8,128)(2,1)}), bf16[128,24,384]{2,1,0:T(8,128)(2,1)S(1)}, u32[]{:S(2)}, u32[]{:S(2)}) async-start(bf16[128,24,384]{2,1,0:T(8,128)(2,1)} %bitcast.17), calls=%async_computation | async-start | bytes 4718592 | tf_op jit(solution)/shard_map/all_to_all | solution.py:298
  61.0 43.9 %collective-permute-start.10 = (bf16[3,64,768]{2,1,0:T(8,128)(2,1)S(1)}, bf16[3,64,768]{2,1,0:T(8,128)(2,1)S(1)}, u32[]{:S(2)}, u32[]{:S(2)}) collective-permute-start(bf16[3,64,768]{2,1,0:T(8,128)(2,1)S(1)} %get-tuple-element.18), channel_id=1, source_target_pairs={{4,0},{5,1},{6,2},{7,3},{8,4},{9,5},{10,6},{11,7},{12,8},{13,9},{1... | collective-permute-start | bytes 884744 | tf_op jit(solution)/shard_map/ppermute | solution.py:43
  62.3 42.6 %collective-permute-start.11 = (bf16[3,64,768]{2,1,0:T(8,128)(2,1)S(1)}, bf16[3,64,768]{2,1,0:T(8,128)(2,1)S(1)}, u32[]{:S(2)}, u32[]{:S(2)}) collective-permute-start(bf16[3,64,768]{2,1,0:T(8,128)(2,1)S(1)} %get-tuple-element.17), channel_id=1, source_target_pairs={{0,2},{1,3},{2,0},{3,1},{124,126},{125,127},{126,124},{127,125}} | collective-permute-start | bytes 884744 | tf_op jit(solution)/shard_map/ppermute | solution.py:43
  65.2 39.7 %collective-permute-start.9 = (bf16[3,64,768]{2,1,0:T(8,128)(2,1)S(1)}, bf16[3,64,768]{2,1,0:T(8,128)(2,1)S(1)}, u32[]{:S(2)}, u32[]{:S(2)}) collective-permute-start(bf16[3,64,768]{2,1,0:T(8,128)(2,1)S(1)} %get-tuple-element.19), channel_id=1, source_target_pairs={{0,4},{1,5},{2,6},{3,7},{4,8},{5,9},{6,10},{7,11},{8,12},{9,13},{1... | collective-permute-start | bytes 884744 | tf_op jit(solution)/shard_map/ppermute | solution.py:43
  67.6 37.3 %copy-start.1 = (bf16[6,16,768]{2,1,0:T(8,128)(2,1)}, bf16[6,16,768]{2,1,0:T(8,128)(2,1)S(1)}, u32[]{:S(2)}) copy-start(bf16[6,16,768]{2,1,0:T(8,128)(2,1)S(1)} %slice_select_fusion.own_edge_ref) | copy-start | bytes 442372
  67.6 25.7 %collective-permute-start.13 = (bf16[3,16,768]{2,1,0:T(8,128)(2,1)S(1)}, bf16[3,16,768]{2,1,0:T(8,128)(2,1)S(1)}, u32[]{:S(2)}, u32[]{:S(2)}) collective-permute-start(bf16[3,16,768]{2,1,0:T(8,128)(2,1)S(1)} %get-tuple-element.24), channel_id=1, source_target_pairs={{0,6},{1,7},{2,4},{3,5},{4,10},{5,11},{6,8},{7,9},{8,14},{9,15},{1... | collective-permute-start | bytes 221192 | tf_op jit(solution)/shard_map/ppermute | solution.py:43
  71.4 33.5 %collective-permute-start.12 = (bf16[6,16,768]{2,1,0:T(8,128)(2,1)S(1)}, bf16[6,16,768]{2,1,0:T(8,128)(2,1)S(1)}, u32[]{:S(2)}, u32[]{:S(2)}) collective-permute-start(bf16[6,16,768]{2,1,0:T(8,128)(2,1)S(1)} %slice_select_fusion.own_edge_ref), channel_id=1, source_target_pairs={{0,2},{1,3},{2,0},{3,1},{4,6},{5,7},{6,4},{7,5},{8,10},{9,11},{10,... | collective-permute-start | bytes 442376 | tf_op jit(solution)/shard_map/ppermute | solution.py:43
  93.3 11.6 %copy-start.15 = (bf16[3,16,768]{2,1,0:T(8,128)(2,1)}, bf16[3,16,768]{2,1,0:T(8,128)(2,1)S(1)}, u32[]{:S(2)}) copy-start(bf16[3,16,768]{2,1,0:T(8,128)(2,1)S(1)} %collective-permute-done.13.up_edge_ref) | copy-start | bytes 221188
  93.3 7.7 %collective-permute-start.14 = (bf16[3,16,768]{2,1,0:T(8,128)(2,1)S(1)}, bf16[3,16,768]{2,1,0:T(8,128)(2,1)S(1)}, u32[]{:S(2)}, u32[]{:S(2)}) collective-permute-start(bf16[3,16,768]{2,1,0:T(8,128)(2,1)S(1)} %get-tuple-element.23), channel_id=1, source_target_pairs={{4,2},{5,3},{6,0},{7,1},{8,6},{9,7},{10,4},{11,5},{12,10},{13,11},... | collective-permute-start | bytes 221192 | tf_op jit(solution)/shard_map/ppermute | solution.py:43
  101.0 3.9 %copy-start.16 = (bf16[3,16,768]{2,1,0:T(8,128)(2,1)}, bf16[3,16,768]{2,1,0:T(8,128)(2,1)S(1)}, u32[]{:S(2)}) copy-start(bf16[3,16,768]{2,1,0:T(8,128)(2,1)S(1)} %collective-permute-done.14.down_edge_ref) | copy-start | bytes 221188
  104.9 0.7 copy-start.12
  104.9 0.8 copy-start.8
  104.9 0.8 copy-start.9
  105.8 0.7 copy-start.10
  108.8 2.8 %collective-permute-start.15 = (bf16[6,96,768]{2,1,0:T(8,128)(2,1)}, bf16[6,96,768]{2,1,0:T(8,128)(2,1)}, u32[]{:S(2)}, u32[]{:S(2)}) collective-permute-start(bf16[6,96,768]{2,1,0:T(8,128)(2,1)} %pack.3.h_own), channel_id=1, source_target_pairs={{0,1},{1,0},{2,3},{3,2},{4,5},{5,4},{6,7},{7,6},{8,9},{9,8},{10,11... | collective-permute-start | bytes 2654216 | tf_op jit(solution)/shard_map/ppermute | solution.py:43

commit v2 on v1

v2 whole, which is shorter than its diff:
```python
import jax
import jax.numpy as jnp
from jax import lax
from jax.experimental import pallas as pl
from jax.experimental.pallas import tpu as pltpu
from jax.sharding import PartitionSpec as P

CHANNELS = 768
NBASIS = 4
HALO = 3
TAPS = 7
LAT = 32
LON = 4
NLAT = 192
ROWS = 6
COLS = 64
EDGE = 16
WIN = COLS + 2 * EDGE
CHIP = 2 * COLS
WIDE = CHIP + 2 * EDGE
EXT = ROWS + 2 * HALO
HALF = CHANNELS // 2
CELLS = ROWS * COLS
BAND = (TAPS + 1) * WIN
SPAN = NBASIS * WIN
PLACES = TAPS * TAPS * NBASIS
OWNED = NBASIS * CHANNELS // (LAT * LON)
BF = jnp.bfloat16
F32 = jnp.float32
BOTH = ("lat", "lon")
DEVICES = [(lat, lon) for lat in range(LAT) for lon in range(LON)]

VMEM = pl.BlockSpec(memory_space=pltpu.VMEM)
SMEM = pl.BlockSpec(memory_space=pltpu.SMEM)
ANY = pl.BlockSpec(memory_space=pl.ANY)
HBM = pl.BlockSpec(memory_space=pltpu.HBM)
MIB = 1024 * 1024


def params(mib):
    return pltpu.CompilerParams(vmem_limit_bytes=mib * MIB)


def cost(flops, size):
    return pl.CostEstimate(flops=flops, bytes_accessed=size, transcendentals=0)


def send(block, move):
    pairs = []
    for lat, lon in DEVICES:
        to = move(lat, lon)
        if to is not None:
            pairs.append((lat * LON + lon, to[0] * LON + to[1]))
    return lax.ppermute(block, BOTH, pairs)


def to_partner(lat, lon):
    return lat, lon ^ 1


def to_chip(lat, lon):
    return lat, lon ^ 2


def along_meridian(lat, lon):
    if lon % 2 == 0:
        return (lat + 1, lon) if lat + 1 < LAT else (lat, lon ^ 3)
    return (lat - 1, lon) if lat > 0 else (lat, lon ^ 3)


def across(lat, lon):
    to_lat = lat + 1 if lon % 2 == 0 else lat - 1
    return (to_lat, lon ^ 2) if 0 <= to_lat < LAT else None


def split(values, size):
    high = jnp.floor((values.astype(F32) + 0.5) * (1.0 / size)).astype(jnp.int32)
    return high, values - high * size


def bands_kernel(info, filt, band_ref, vec_ref):
    lat = info[1]
    lane = lax.broadcasted_iota(jnp.int32, (1, 128), 1)
    row_of = lat * ROWS + lane - HALO
    row_of = jnp.where(row_of < 0, -1 - row_of, row_of)
    row_of = jnp.where(row_of >= NLAT, 2 * NLAT - 1 - row_of, row_of)
    pick = lax.broadcasted_iota(jnp.int32, (NLAT, 128), 0) == row_of
    rows = jnp.dot(filt[...], pick.astype(F32).astype(BF), preferred_element_type=F32)
    low = jnp.zeros((1, 128), jnp.int32)
    high = jnp.zeros((1, 128), jnp.int32)
    far = jnp.zeros((1, 128), jnp.int32)
    for e in range(EXT):
        row = lat * ROWS + e - HALO
        row = jnp.where(row < 0, -1 - row, row)
        row = jnp.where(row >= NLAT, 2 * NLAT - 1 - row, row)
        width, offset, reach = info[2 + row], info[2 + NLAT + row], info[2 + 2 * NLAT + row]
        low = jnp.where(lane == e, offset, low)
        high = jnp.where(lane == e, offset + width, high)
        far = jnp.where(lane == e, reach, far)
    a, rest = split(lax.broadcasted_iota(jnp.int32, (PLACES, 128), 0), TAPS * NBASIS)
    b, _ = split(rest, NBASIS)
    keep = (a >= low) & (a < high) & (jnp.abs(b - HALO) <= far)
    rows = jnp.where(keep, rows, 0.0).astype(BF)
    over = (((0,), (0,)), ((), ()))
    a, b = split(lax.broadcasted_iota(jnp.int32, (1, BAND), 1), WIN)
    b = b - (EDGE - HALO)
    band_at = jnp.where((a < TAPS) & (b >= 0) & (b < TAPS), (a * TAPS + b) * NBASIS, -PLACES)
    place = lax.broadcasted_iota(jnp.int32, (PLACES, BAND), 0)
    for k in range(NBASIS):
        put = (place == band_at + k).astype(F32).astype(BF)
        vec = lax.dot_general(rows, put, over, preferred_element_type=F32)
        for i in range(ROWS):
            row = jnp.broadcast_to(vec[HALO + i : HALO + i + 1, :], (COLS, BAND))
            block = pltpu.roll(row, 0, 1, stride=1, stride_axis=0)
            band_ref[i, k * COLS : (k + 1) * COLS, :] = block.astype(BF)
    k, b = split(lax.broadcasted_iota(jnp.int32, (1, SPAN), 1), WIN)
    b = EDGE + HALO - b
    spread_at = jnp.where((b >= 0) & (b < TAPS), b * NBASIS + k, -PLACES)
    place = lax.broadcasted_iota(jnp.int32, (PLACES, SPAN), 0)
    vecs = []
    for a in range(TAPS):
        put = (place == spread_at + a * TAPS * NBASIS).astype(F32).astype(BF)
        vecs.append(lax.dot_general(rows, put, over, preferred_element_type=F32)[:16])
    e = lax.broadcasted_iota(jnp.int32, (16, SPAN), 0)
    beyond = ((lat == 0) & (e < HALO)) | ((lat == LAT - 1) & (e >= HALO + ROWS))
    for a in range(TAPS):
        vec_ref[a] = jnp.where(beyond, vecs[TAPS - 1 - a], vecs[a])


def each(todo, act):
    for c in todo:
        act(c)


def start_copy(c):
    c.start()


def wait_copy(c):
    c.wait()


def run(todo):
    each(todo, start_copy)
    each(todo, wait_copy)


def rows_kernel(info, own, part, out, sems):
    for core_is, row in enumerate((ROWS - HALO, 0)):
        low, high = slice(0, COLS), slice(COLS, CHIP)
        mine, other = (low, high) if core_is == 0 else (high, low)

        @pl.when(info[0] == core_is)
        def _():
            run(
                [
                    pltpu.make_async_copy(own, out.at[:, mine], sems.at[0]),
                    pltpu.make_async_copy(part.at[row : row + HALO], out.at[:, other], sems.at[1]),
                ]
            )


def relay_kernel(info, a_own, e_own, c_own, u_own, u_part, out, u_rows, sems):
    todo = [
        pltpu.make_async_copy(a_own, out.at[0:HALO], sems.at[0]),
        pltpu.make_async_copy(e_own, out.at[HALO, 0:COLS], sems.at[1]),
        pltpu.make_async_copy(c_own, out.at[HALO, COLS:CHIP], sems.at[2]),
    ]
    each(todo, start_copy)
    for core_is, row in enumerate((ROWS - HALO, 0)):
        half0, half1 = (u_own, u_part) if core_is == 0 else (u_part, u_own)
        at = slice(row, row + HALO)

        @pl.when(info[0] == core_is)
        def _():
            run(
                [
                    pltpu.make_async_copy(half0.at[at], u_rows.at[:, 0:COLS], sems.at[3]),
                    pltpu.make_async_copy(half1.at[at], u_rows.at[:, COLS:CHIP], sems.at[4]),
                ]
            )

    each(todo, wait_copy)


def slots(which, group):
    at = (2 * which + group) * EDGE
    return slice(at, at + EDGE)


def gather_columns(rows, first):
    slot = lax.broadcasted_iota(jnp.int32, (EDGE, CHANNELS), 0)
    out = jnp.zeros((EDGE, CHANNELS), F32)
    for m, row in enumerate(rows):
        shift = (4 * m - (0 if first else EDGE - HALO)) % EDGE
        moved = pltpu.roll(row.astype(F32), shift, 0)
        out = jnp.where((slot >= 4 * m) & (slot < 4 * m + HALO), moved, out)
    return out.astype(BF)


def spread_columns(block, m, first):
    slot = lax.broadcasted_iota(jnp.int32, (EDGE, CHANNELS), 0)
    moved = pltpu.roll(block.astype(F32), ((0 if first else EDGE - HALO) - 4 * m) % EDGE, 0)
    keep = slot < HALO if first else slot >= EDGE - HALO
    return jnp.where(keep, moved, 0.0).astype(BF)


def edges_kernel(info, f_own, f_part, u_own, u_part, after, edge, corner, outer, sides, sems):
    first, last = slice(0, EDGE), slice(COLS - EDGE, COLS)

    def copies(columns, row, halves):
        todo = []
        for n, (own, half0, half1) in enumerate(halves):
            at = pl.ds(row, HALO)
            todo.append(pltpu.make_async_copy(own.at[:, columns], outer.at[n], sems.at[3 * n]))
            todo.append(pltpu.make_async_copy(half0.at[at, first], sides.at[n, 0], sems.at[3 * n + 1]))
            todo.append(pltpu.make_async_copy(half1.at[at, last], sides.at[n, 1], sems.at[3 * n + 2]))
        return todo

    @pl.when(info[0] == 0)
    def _():
        run(copies(first, ROWS - HALO, ((f_own, f_own, f_part), (u_own, u_own, u_part))))
        for n in range(2):
            for g in range(2):
                edge[slots(n, g)] = gather_columns([outer[n, 3 * g + m] for m in range(HALO)], True)

    @pl.when(info[0] == 1)
    def _():
        run(copies(last, 0, ((f_own, f_part, f_own), (u_own, u_part, u_own))))
        for n in range(2):
            for g in range(2):
                edge[slots(n, g)] = gather_columns([outer[n, 3 * g + m] for m in range(HALO)], False)

    for n in range(2):
        for side in range(2):
            corner[slots(n, side)] = gather_columns([sides[n, side, m] for m in range(HALO)], side == 0)


def fill_copies(x, rim, sems, which, lat_is, half0, half1, passed0, passed1, rows0, rows1, start, stop):
    todo = []

    def put(ref, columns, at, rows, n):
        low, high = max(at, start), min(at + columns.stop - columns.start, stop)
        if low < high:
            src = ref.at[:, columns.start + low - at : columns.start + high - at]
            todo.append(pltpu.make_async_copy(src, x.at[rows, low - start : high - start], sems.at[n]))

    def put_row(ref, row, columns, at, to, n):
        low, high = max(at, start), min(at + columns.stop - columns.start, stop)
        if low < high:
            src = ref.at[row, columns.start + low - at : columns.start + high - at]
            todo.append(pltpu.make_async_copy(src, x.at[to, low - start : high - start], sems.at[n]))

    whole, first, last = slice(0, COLS), slice(0, EDGE), slice(COLS - EDGE, COLS)
    left, right = 0, EDGE + CHIP
    mid = slice(HALO, HALO + ROWS)
    for n, (ref, at) in enumerate(((passed1, 0), (passed0, 0), (passed0, COLS), (passed1, COLS))):
        at += 2 * EDGE * which
        todo.append(pltpu.make_async_copy(ref.at[HALO, at : at + 2 * EDGE], rim.at[n], sems.at[n]))
    put(half0, whole, EDGE, mid, 4)
    put(half1, whole, EDGE + COLS, mid, 5)
    n = 6
    for side, rows in enumerate((rows0, rows1)):
        to = side * (HALO + ROWS)
        if lat_is == side:
            for m in range(HALO):
                own = HALO - 1 - m + side * (ROWS - HALO)
                put_row(rows, HALO - 1 - m, slice(0, CHIP), EDGE, to + m, n + 3 * m)
                put_row(half1, own, last, left, to + m, n + 3 * m + 1)
                put_row(half0, own, first, right, to + m, n + 3 * m + 2)
        else:
            put(rows.at[0:HALO], slice(0, CHIP), EDGE, slice(to, to + HALO), n)
        n += 9
    return todo


FILL_SEMS = 24


def fill(act, info, x, rim, sems, which, half, passed, rows, window):
    core, lat = info[0], info[1]
    for core_is in range(2):
        refs = [pair[core_is ^ c] for pair in (half, passed, rows) for c in range(2)]
        start, stop = (core_is * COLS, core_is * COLS + WIN) if window else (0, WIDE)
        for lat_is, here in ((0, lat == 0), (1, lat == LAT - 1), (None, (lat > 0) & (lat < LAT - 1))):

            @pl.when((core == core_is) & here)
            def _():
                each(fill_copies(x, rim, sems, which, lat_is, *refs, start, stop), act)


def fill_rim(info, x, rim, left, right):
    lat = info[1]
    for at, first in ((left, False), (right, True)):
        if at is None:
            continue
        to = slice(at, at + EDGE)
        for r in range(ROWS):
            x[HALO + r, to, :] = spread_columns(rim[int(first), slots(0, r // HALO)], r % HALO, first)
        for side, pole in ((0, 0), (1, LAT - 1)):

            @pl.when(lat != pole)
            def _():
                for m in range(HALO):
                    x[side * (HALO + ROWS) + m, to, :] = spread_columns(rim[2 + side, slots(0, 1 - int(first))], m, first)


def grad_kernel(info, f_own, f_part, p_own, p_part, u_own, u_part, bands, g_ref, own_ref, x, rim, band, basis, ud, g, sems):
    core = info[0]
    band_copy = pltpu.make_async_copy(bands, band, sems.at[FILL_SEMS])

    def inputs(act):
        fill(act, info, x, rim, sems, 0, (f_own, f_part), (p_own, p_part), (p_own, p_part), False)
        for core_is, (u0, u1) in enumerate(((u_own, u_part), (u_part, u_own))):
            cols = slice(core_is * HALF, (core_is + 1) * HALF)

            @pl.when(core == core_is)
            def _():
                act(pltpu.make_async_copy(u0.at[:, :, cols], ud.at[0:ROWS], sems.at[FILL_SEMS + 1]))
                act(pltpu.make_async_copy(u1.at[:, :, cols], ud.at[ROWS : 2 * ROWS], sems.at[FILL_SEMS + 2]))

    inputs(start_copy)
    band_copy.start()
    x[EXT : EXT + 1, :, :] = jnp.zeros((1, WIDE, CHANNELS), BF)
    band_copy.wait()
    inputs(wait_copy)
    fill_rim(info, x, rim, 0, EDGE + CHIP)
    for i in range(ROWS):
        for w in range(2):
            cells = x[i : i + TAPS + 1, w * COLS : w * COLS + WIN].reshape(BAND, CHANNELS)
            rows = jnp.dot(band[i], cells, preferred_element_type=F32).astype(BF)
            for k in range(NBASIS):
                basis[k, w * CELLS + i * COLS : w * CELLS + (i + 1) * COLS, :] = rows[k * COLS : (k + 1) * COLS]
    at = pl.multiple_of(core * CELLS, CELLS)
    own_copy = pltpu.make_async_copy(basis.at[:, pl.ds(at, CELLS)], own_ref, sems.at[FILL_SEMS])
    own_copy.start()
    up = ud[...].reshape(2 * CELLS, HALF)
    outs = []
    for k in range(NBASIS):
        to = slice(k * CHANNELS, (k + 1) * CHANNELS)
        g[to, :] = lax.dot_general(basis[k], up, (((0,), (0,)), ((), ())), preferred_element_type=F32).astype(BF)
        outs.append(pltpu.make_async_copy(g.at[to], g_ref.at[to], sems.at[k]))
        outs[-1].start()
    own_copy.wait()
    each(outs, wait_copy)


def tie_kernel(partial, after, out):
    del partial, after, out


def local_kernel(info, own_ref, w_ref, vec_ref, u_own, u_part, p_own, p_part, a_own, a_part, conv_ref, state_ref, x, rim, bg, acc, sems):
    def inputs(act):
        fill(act, info, x, rim, sems, 1, (u_own, u_part), (p_own, p_part), (a_own, a_part), True)

    inputs(start_copy)
    total = jnp.zeros((CELLS, CHANNELS), F32)
    for k in range(NBASIS):
        total = total + jnp.dot(own_ref[k], w_ref[k * CHANNELS : (k + 1) * CHANNELS, :], preferred_element_type=F32)
    conv_ref[...] = total.astype(BF).reshape(ROWS, COLS, CHANNELS)
    inputs(wait_copy)

    @pl.when(info[0] == 0)
    def _():
        fill_rim(info, x, rim, 0, None)

    @pl.when(info[0] == 1)
    def _():
        fill_rim(info, x, rim, None, WIN - EDGE)

    for k in range(NBASIS):
        wk = w_ref[k * CHANNELS : (k + 1) * CHANNELS, :]
        for part in range(3):
            cells = x[part * 4 : (part + 1) * 4].reshape(4 * WIN, CHANNELS)
            got = lax.dot_general(cells, wk, (((1,), (1,)), ((), ())), preferred_element_type=F32)
            bg[part * 4 : (part + 1) * 4, k * WIN : (k + 1) * WIN, :] = got.astype(BF).reshape(4, WIN, CHANNELS)
    acc[...] = jnp.zeros((ROWS, COLS, CHANNELS), F32)
    for e in range(EXT):
        rows = [r for r in range(ROWS) if 0 <= r + TAPS - 1 - e < TAPS]
        blocks = []
        for r in rows:
            a = r + TAPS - 1 - e
            row = jnp.broadcast_to(vec_ref[a, e : e + 1, :], (COLS, SPAN))
            blocks.append(pltpu.roll(row, 0, 1, stride=1, stride_axis=0).astype(BF))
        got = jnp.dot(jnp.concatenate(blocks, 0), bg[e], preferred_element_type=F32)
        for n, r in enumerate(rows):
            acc[r] += got[n * COLS : (n + 1) * COLS]
    state_ref[...] = acc[...].astype(BF)


def on_device(features, upstream, weights, filter_basis, lat_width, lat_offset, lon_reach):
    lat = lax.axis_index("lat")
    core = lax.axis_index("lon") % 2
    info = jnp.concatenate([jnp.stack([core, lat]).astype(jnp.int32), lat_width, lat_offset, lon_reach])

    f_part = send(features, to_partner)
    u_part = send(upstream, to_partner)
    own_rows = jnp.where(core == 0, features[ROWS - HALO :], features[:HALO])
    rows = pl.pallas_call(
        rows_kernel,
        out_shape=jax.ShapeDtypeStruct((HALO, CHIP, CHANNELS), BF),
        in_specs=[SMEM, ANY, ANY],
        out_specs=ANY,
        scratch_shapes=[pltpu.SemaphoreType.DMA((2,))],
        compiler_params=params(4),
        cost_estimate=cost(1000, 2_000_000),
        name="rows",
    )(info, own_rows, f_part)
    af_own = send(rows, along_meridian)
    filt = jnp.transpose(filter_basis, (2, 3, 0, 1)).reshape(PLACES, NLAT)
    bands, vecs = pl.pallas_call(
        bands_kernel,
        out_shape=(
            jax.ShapeDtypeStruct((ROWS, NBASIS * COLS, BAND), BF),
            jax.ShapeDtypeStruct((TAPS, 16, SPAN), F32),
        ),
        in_specs=[SMEM, VMEM],
        out_specs=(VMEM, VMEM),
        compiler_params=params(16),
        cost_estimate=cost(2_000_000_000, 5_000_000),
        name="bands",
    )(info, filt)

    edges, corners = pl.pallas_call(
        edges_kernel,
        out_shape=(
            jax.ShapeDtypeStruct((COLS, CHANNELS), BF),
            jax.ShapeDtypeStruct((COLS, CHANNELS), BF),
        ),
        in_specs=[SMEM] + [ANY] * 5,
        out_specs=(VMEM, VMEM),
        scratch_shapes=[
            pltpu.VMEM((2, ROWS, EDGE, CHANNELS), BF),
            pltpu.VMEM((2, 2, HALO, EDGE, CHANNELS), BF),
            pltpu.SemaphoreType.DMA((6,)),
        ],
        compiler_params=params(4),
        cost_estimate=cost(1000, 1_000_000),
        name="edges",
    )(info, features, f_part, upstream, u_part, vecs)
    e_own = send(edges, to_chip)
    c_own = send(corners, across)
    passed, u_rows = pl.pallas_call(
        relay_kernel,
        out_shape=(
            jax.ShapeDtypeStruct((HALO + 1, CHIP, CHANNELS), BF),
            jax.ShapeDtypeStruct((HALO, CHIP, CHANNELS), BF),
        ),
        in_specs=[SMEM] + [ANY] * 5,
        out_specs=(ANY, ANY),
        scratch_shapes=[pltpu.SemaphoreType.DMA((5,))],
        compiler_params=params(4),
        cost_estimate=cost(1000, 4_000_000),
        name="relay",
    )(info, af_own, e_own, c_own, upstream, u_part)
    p_part = send(passed, to_partner)
    au_own = send(u_rows, along_meridian)
    au_part = send(au_own, to_partner)

    partial, basis_own = pl.pallas_call(
        grad_kernel,
        out_shape=(
            jax.ShapeDtypeStruct((NBASIS * CHANNELS, HALF), BF),
            pltpu.HBM((NBASIS, CELLS, CHANNELS), BF),
        ),
        in_specs=[SMEM] + [ANY] * 7,
        out_specs=(HBM, HBM),
        scratch_shapes=[
            pltpu.VMEM((EXT + 1, WIDE, CHANNELS), BF),
            pltpu.VMEM((4, 2 * EDGE, CHANNELS), BF),
            pltpu.VMEM((ROWS, NBASIS * COLS, BAND), BF),
            pltpu.VMEM((NBASIS, 2 * CELLS, CHANNELS), BF),
            pltpu.VMEM((2 * ROWS, COLS, HALF), BF),
            pltpu.VMEM((NBASIS * CHANNELS, HALF), BF),
            pltpu.SemaphoreType.DMA((FILL_SEMS + 3,)),
        ],
        compiler_params=params(32),
        cost_estimate=cost(8_000_000_000, 12_000_000),
        name="grad",
    )(info, features, f_part, passed, p_part, upstream, u_part, bands)

    partial = pl.pallas_call(
        tie_kernel,
        out_shape=jax.ShapeDtypeStruct(partial.shape, BF),
        in_specs=[ANY, ANY],
        out_specs=ANY,
        input_output_aliases={0: 0},
        compiler_params=params(1),
        name="tie",
    )(partial, au_own)
    pieces = lax.all_to_all(partial.reshape(LAT * LON, OWNED, HALF), BOTH, 0, 0, tiled=True)

    convolved, state_grad = pl.pallas_call(
        local_kernel,
        out_shape=(
            jax.ShapeDtypeStruct((ROWS, COLS, CHANNELS), BF),
            jax.ShapeDtypeStruct((ROWS, COLS, CHANNELS), BF),
        ),
        in_specs=[SMEM] + [VMEM] * 3 + [ANY] * 6,
        out_specs=(VMEM, VMEM),
        scratch_shapes=[
            pltpu.VMEM((EXT, WIN, CHANNELS), BF),
            pltpu.VMEM((4, 2 * EDGE, CHANNELS), BF),
            pltpu.VMEM((EXT, SPAN, CHANNELS), BF),
            pltpu.VMEM((ROWS, COLS, CHANNELS), F32),
            pltpu.SemaphoreType.DMA((FILL_SEMS,)),
        ],
        compiler_params=params(32),
        cost_estimate=cost(10_000_000_000, 12_000_000),
        name="local",
    )(info, basis_own, weights, vecs, upstream, u_part, passed, p_part, au_own, au_part)

    summed = pieces.astype(F32).reshape(LAT * LON // 2, 2, OWNED, HALF).sum(0)
    weight_grad = jnp.concatenate([summed[0], summed[1]], 1)
    return convolved, state_grad, weight_grad


def solution(mesh):
    return jax.shard_map(
        on_device,
        mesh=mesh,
        in_specs=(P("lat", "lon", None), P("lat", "lon", None), P(), P(), P(), P(), P()),
        out_specs=(P("lat", "lon", None), P("lat", "lon", None), P(("lat", "lon"), None)),
        check_vma=False,
    )
```

time: 129 us -> 85.6 us (0.66)
  starting transfers between devices: 37.5 us -> 18.8 us
  waiting for transfers between devices: 41.3 us -> 27.1 us
  Pallas kernels: 34.4 us -> 27.5 us
  other arithmetic: 6.2 us -> 3.74 us
    ppermute x16 -> x8, waiting for transfers between devices: 41.3 us -> 16.1 us  [send(): return lax.ppermute(block, BOTH, pairs)]
    ppermute x16 -> x8, starting transfers between devices: 27.2 us -> 8.21 us  [send(): return lax.ppermute(block, BOTH, pairs)]
    all_to_all x1, waiting for transfers between devices: 0.01 us -> 11 us  [on_device(): lax.all_to_all(partial.reshape(LAT * LON, OWNED, HALF), BOTH, 0, 0, tiled...]
    unnamed x35 -> x18, local copies, waits for them, and re-layouts: 2.57 us -> 6.29 us
    pallas_call x3 -> x5, Pallas kernels: 7.69 us -> 4.62 us  [the longest x1 1.99 us: on_device(): pl.pallas_call(bands_kernel, out_shape=(jax.ShapeDtypeStruct((ROWS, NBASI...]
    pallas_call x1, Pallas kernels: 11.8 us -> 9.68 us  [on_device(): pl.pallas_call(grad_kernel, out_shape=(jax.ShapeDtypeStruct((NBASIS * CHA...]
    reshape x2 -> x1, local copies, waits for them, and re-layouts: 2.09 us -> 0.06 us  [on_device(): filt = jnp.transpose(filter_basis, (2, 3, 0, 1)).reshape(PLACES, NLAT)]
    pallas_call x1, Pallas kernels: 14.9 us -> 13.2 us  [on_device(): pl.pallas_call(local_kernel, out_shape=(jax.ShapeDtypeStruct((ROWS, COLS,...]
  transfers between devices with their start and end apart: 17 -> 9, of which waited for: 6 -> 6; matrix products, arithmetic and copies ran while one was open for 7% -> 2% of each run, Pallas kernels for 18% -> 31%
where the time goes in v2:
time: 85.6 us; the launch traced here: 85.1 us
  Pallas kernels  27.5 us (32%)
  waiting for transfers between devices  27.1 us (32%)
  starting transfers between devices  18.8 us (22%)
  local copies, waits for them, and re-layouts  7.15 us (8%)
  other arithmetic  3.74 us (4%)
    ppermute x8, waiting for transfers between devices, send(): return lax.ppermute(block, BOTH, pairs)  16.1 us
    pallas_call x1, Pallas kernels, on_device(): pl.pallas_call(local_kernel, out_shape=(jax.ShapeDtypeStruct((ROWS, COLS,...  13.2 us
    all_to_all x1, waiting for transfers between devices, on_device(): lax.all_to_all(partial.reshape(LAT * LON, OWNED, HALF), BOTH, 0, 0, tiled...  11 us
    all_to_all x1, starting transfers between devices, on_device(): lax.all_to_all(partial.reshape(LAT * LON, OWNED, HALF), BOTH, 0, 0, tiled...  10.6 us
    pallas_call x1, Pallas kernels, on_device(): pl.pallas_call(grad_kernel, out_shape=(jax.ShapeDtypeStruct((NBASIS * CHA...  9.68 us
    ppermute x8, starting transfers between devices, send(): return lax.ppermute(block, BOTH, pairs)  8.21 us
    unnamed x18, local copies, waits for them, and re-layouts  6.29 us
    reduce_sum x1, other arithmetic, on_device(): summed = pieces.astype(F32).reshape(LAT * LON // 2, 2, OWNED, HALF).sum(0)  2.02 us
  transfers between devices with their start and end apart: 9, of which 6 were waited for; matrix products, arithmetic and copies ran while one was open for 2% of the time, Pallas kernels for 31%

profile of v2, /device:TPU:0, one launch (start us, length us, event | category | flops | bytes accessed | tf_op | source)
XLA Modules:
  0.0 85.1 jit_solution(2980762882482379492)
XLA Ops:
  0.6 0.0 copy-start.8
  0.6 0.1 collective-permute-start
  0.7 0.5 collective-permute-start.2
  1.2 1.1 %slice_select_fusion.own = bf16[3,64,768]{2,1,0:T(8,128)(2,1)S(1)} fusion(bf16[6,64,768]{2,1,0:T(8,128)(2,1)} %f_own.3, pred[]{:T(512)S(6)} %eq.5), kind=kLoop, calls=%fused_computation.1 | loop fusion | flops 147456 | bytes 884737 | tf_op jit(solution)/shard_map/jit(_where)/select_n | solution.py:398
  2.3 0.8 concatenate.6.info
  3.1 0.0 collective-permute-done.part.f_part
  3.1 0.7 rows.1
  3.8 1.6 %collective-permute-start.1 = (bf16[3,128,768]{2,1,0:T(8,128)(2,1)S(1)}, bf16[3,128,768]{2,1,0:T(8,128)(2,1)S(1)}, u32[]{:S(2)}, u32[]{:S(2)}) collective-permute-start(bf16[3,128,768]{2,1,0:T(8,128)(2,1)S(1)} %rows.1), channel_id=1, source_target_pairs={{0,4},{1,2},{2,6},{3,0},{4,8},{5,1},{6,10},{7,3},{8,12},{9,5},{10,... | collective-permute-start | bytes 1769480 | tf_op jit(solution)/shard_map/ppermute | solution.py:54
  5.4 0.0 copy-done.8
  5.4 0.1 reshape.18.filt
  5.5 0.0 copy-start
  5.5 0.0 copy-start.1
  5.5 2.0 %bands.1 = (bf16[6,256,768]{2,1,0:T(8,128)(2,1)S(1)}, f32[7,16,384]{2,1,0:T(8,128)S(1)}) custom-call(s32[578]{0:T(1024)S(1)} %concatenate.6.info, bf16[196,192]{1,0:T(8,128)(2,1)S(1)} %reshape.18.filt), custom_call_target="tpu_custom_call" | custom-call | flops 2000000000 | bytes 5000000 | tf_op jit(solution)/shard_map/bands/pallas_call | solution.py:411
  7.5 0.0 collective-permute-done.2.u_part
  7.5 0.0 copy-done
  7.5 0.0 copy-done.1
  7.5 0.9 %edges.1 = (bf16[64,768]{1,0:T(8,128)(2,1)S(1)}, bf16[64,768]{1,0:T(8,128)(2,1)S(1)}) custom-call(s32[578]{0:T(1024)S(1)} %concatenate.6.info, bf16[6,64,768]{2,1,0:T(8,128)(2,1)S(1)} %copy-done, bf16[6,64,768]{2,1,0:T(8,128)(2,1)S(1)} %collective-permute-done.part.f_part, bf16[6,64,768]{2,1,0:T(8,128)(2,1)S(1)} %copy-done.1, ...), custom_call_target="tpu_custom_call" | custom-call | flops 1000 | bytes 1000000 | tf_op jit(solution)/shard_map/edges/pallas_call | solution.py:424
  8.5 1.6 %collective-permute-start.3 = (bf16[64,768]{1,0:T(8,128)(2,1)S(1)}, bf16[64,768]{1,0:T(8,128)(2,1)S(1)}, u32[]{:S(2)}, u32[]{:S(2)}) collective-permute-start(bf16[64,768]{1,0:T(8,128)(2,1)S(1)} %get-tuple-element.14), channel_id=1, source_target_pairs={{0,2},{1,3},{2,0},{3,1},{4,6},{5,7},{6,4},{7,5},{8,10},{9,11},{10,... | collective-permute-start | bytes 294920 | tf_op jit(solution)/shard_map/ppermute | solution.py:54
  10.1 3.3 %collective-permute-start.4 = (bf16[64,768]{1,0:T(8,128)(2,1)S(1)}, bf16[64,768]{1,0:T(8,128)(2,1)S(1)}, u32[]{:S(2)}, u32[]{:S(2)}) collective-permute-start(bf16[64,768]{1,0:T(8,128)(2,1)S(1)} %get-tuple-element.15), channel_id=1, source_target_pairs={{0,6},{2,4},{4,10},{5,3},{6,8},{7,1},{8,14},{9,7},{10,12},{11,5},{... | collective-permute-start | bytes 294920 | tf_op jit(solution)/shard_map/ppermute | solution.py:54
  13.4 7.7 %collective-permute-done.3.e_own = bf16[64,768]{1,0:T(8,128)(2,1)S(1)} collective-permute-done((bf16[64,768]{1,0:T(8,128)(2,1)S(1)}, bf16[64,768]{1,0:T(8,128)(2,1)S(1)}, u32[]{:S(2)}, u32[]{:S(2)}) %collective-permute-start.3) | collective-permute-done | bytes 98336 | tf_op jit(solution)/shard_map/ppermute | solution.py:54
  21.1 0.0 collective-permute-done.4.c_own
  21.1 0.5 collective-permute-done.1.a_own
  21.6 1.1 %relay.1 = (bf16[4,128,768]{2,1,0:T(8,128)(2,1)S(1)}, bf16[3,128,768]{2,1,0:T(8,128)(2,1)S(1)}) custom-call(s32[578]{0:T(1024)S(1)} %concatenate.6.info, bf16[3,128,768]{2,1,0:T(8,128)(2,1)S(1)} %collective-permute-done.1.a_own, bf16[64,768]{1,0:T(8,128)(2,1)S(1)} %collective-permute-done.3.e_own, bf16[64,768]{1,0:T(8,128)(2,1)S(1)} %collective-permute-done.4.c_own, ...), custom_call_target="tpu_custom_call" | custom-call | flops 1000 | bytes 4000000 | tf_op jit(solution)/shard_map/relay/pallas_call | solution.py:443
  22.6 0.0 copy-start.3
  22.7 1.0 %collective-permute-start.5 = (bf16[4,128,768]{2,1,0:T(8,128)(2,1)S(1)}, bf16[4,128,768]{2,1,0:T(8,128)(2,1)S(1)}, u32[]{:S(2)}, u32[]{:S(2)}) collective-permute-start(bf16[4,128,768]{2,1,0:T(8,128)(2,1)S(1)} %get-tuple-element.16.p_own), channel_id=1, source_target_pairs={{0,1},{1,0},{2,3},{3,2},{4,5},{5,4},{6,7},{7,6},{8,9},{9,8},{10,11... | collective-permute-start | bytes 2359304 | tf_op jit(solution)/shard_map/ppermute | solution.py:54
  23.6 0.0 collective-permute-start.6
  23.6 1.9 %collective-permute-done.5.p_part = bf16[4,128,768]{2,1,0:T(8,128)(2,1)S(1)} collective-permute-done((bf16[4,128,768]{2,1,0:T(8,128)(2,1)S(1)}, bf16[4,128,768]{2,1,0:T(8,128)(2,1)S(1)}, u32[]{:S(2)}, u32[]{:S(2)}) %collective-permute-start.5) | collective-permute-done | bytes 786464 | tf_op jit(solution)/shard_map/ppermute | solution.py:54
  25.5 0.0 copy-start.5
  25.5 9.7 %grad.1 = (bf16[3072,384]{1,0:T(8,128)(2,1)}, bf16[4,384,768]{2,1,0:T(8,128)(2,1)}) custom-call(s32[578]{0:T(1024)S(1)} %concatenate.6.info, bf16[6,64,768]{2,1,0:T(8,128)(2,1)S(1)} %copy-done, bf16[6,64,768]{2,1,0:T(8,128)(2,1)S(1)} %collective-permute-done.part.f_part, bf16[4,128,768]{2,1,0:T(8,128)(2,1)S(1)} %get-tuple-element.16.p_own, ...), custom_call_target="tpu_custom_call" | custom-call | flops 8000000000 | bytes 12000000 | tf_op jit(solution)/shard_map/grad/pallas_call | solution.py:460
  35.2 0.0 copy-done.3
  35.2 0.0 copy-done.5
  35.2 4.0 %collective-permute-done.6.a_own.after = bf16[3,128,768]{2,1,0:T(8,128)(2,1)S(1)} collective-permute-done((bf16[3,128,768]{2,1,0:T(8,128)(2,1)S(1)}, bf16[3,128,768]{2,1,0:T(8,128)(2,1)S(1)}, u32[]{:S(2)}, u32[]{:S(2)}) %collective-permute-start.6) | collective-permute-done | bytes 589856 | tf_op jit(solution)/shard_map/ppermute | solution.py:54
  39.3 10.6 %all-to-all-start = ((bf16[128,24,384]{2,1,0:T(8,128)(2,1)}), bf16[128,24,384]{2,1,0:T(8,128)(2,1)}, u32[]{:S(2)}, u32[]{:S(2)}) async-start(bf16[128,24,384]{2,1,0:T(8,128)(2,1)} %bitcast.3), calls=%async_computation | async-start | bytes 4718592 | tf_op jit(solution)/shard_map/all_to_all | solution.py:491
  49.9 0.1 collective-permute-start.7
  50.0 2.0 %collective-permute-done.7.a_part = bf16[3,128,768]{2,1,0:T(8,128)(2,1)S(1)} collective-permute-done((bf16[3,128,768]{2,1,0:T(8,128)(2,1)S(1)}, bf16[3,128,768]{2,1,0:T(8,128)(2,1)S(1)}, u32[]{:S(2)}, u32[]{:S(2)}) %collective-permute-start.7) | collective-permute-done | bytes 589856 | tf_op jit(solution)/shard_map/ppermute | solution.py:54
  51.9 0.0 copy-start.2
  52.0 2.3 %copy-done.2 = bf16[3072,768]{1,0:T(8,128)(2,1)S(1)} copy-done((bf16[3072,768]{1,0:T(8,128)(2,1)S(1)}, bf16[3072,768]{1,0:T(8,128)(2,1)}, u32[]{:S(2)}) %copy-start.2) | copy-done | bytes 4718616
  54.3 0.0 copy-start.4
  54.3 1.1 %copy-done.4 = bf16[4,128,768]{2,1,0:T(8,128)(2,1)S(1)} copy-done((bf16[4,128,768]{2,1,0:T(8,128)(2,1)S(1)}, bf16[4,128,768]{2,1,0:T(8,128)(2,1)}, u32[]{:S(2)}) %copy-start.4) | copy-done | bytes 786456
  55.4 0.0 copy-start.6
  55.4 1.1 %copy-done.6 = bf16[4,128,768]{2,1,0:T(8,128)(2,1)S(1)} copy-done((bf16[4,128,768]{2,1,0:T(8,128)(2,1)S(1)}, bf16[4,128,768]{2,1,0:T(8,128)(2,1)}, u32[]{:S(2)}) %copy-start.6) | copy-done | bytes 786456
  56.6 0.0 copy-start.7
  56.6 1.7 %copy-done.7 = bf16[4,384,768]{2,1,0:T(8,128)(2,1)S(1)} copy-done((bf16[4,384,768]{2,1,0:T(8,128)(2,1)S(1)}, bf16[4,384,768]{2,1,0:T(8,128)(2,1)}, u32[]{:S(2)}) %copy-start.7) | copy-done | bytes 2359320
  58.2 13.2 %local.1 = (bf16[6,64,768]{2,1,0:T(8,128)(2,1)}, bf16[6,64,768]{2,1,0:T(8,128)(2,1)}) custom-call(s32[578]{0:T(1024)S(1)} %concatenate.6.info, bf16[4,384,768]{2,1,0:T(8,128)(2,1)S(1)} %copy-done.7, bf16[3072,768]{1,0:T(8,128)(2,1)S(1)} %copy-done.2, f32[7,16,384]{2,1,0:T(8,128)S(1)} %get-tuple-element.13.after.vec_ref, bf16[6,64,768]{2,1,0:T(8,128)(2,1)S(1)} %copy-done.1, ...), custom_call_target="tpu_custom_call" | custom-call | flops 10000000000 | bytes 12000000 | tf_op jit(solution)/shard_map/local/pallas_call | solution.py:493
  71.4 11.0 %all-to-all-done = bf16[128,24,384]{2,1,0:T(8,128)(2,1)} async-done(((bf16[128,24,384]{2,1,0:T(8,128)(2,1)}), bf16[128,24,384]{2,1,0:T(8,128)(2,1)}, u32[]{:S(2)}, u32[]{:S(2)}) %all-to-all-start) | async-done | bytes 2359328 | tf_op jit(solution)/shard_map/all_to_all | solution.py:491
  82.5 2.0 %convert_reduce_fusion = f32[2,24,384]{2,1,0:T(8,128)S(1)} fusion(bf16[64,2,24,384]{3,2,1,0:T(8,128)(2,1)} %bitcast.7), kind=kLoop, calls=%fused_computation | loop fusion | flops 2340864 | bytes 2433024 | tf_op jit(solution)/shard_map/reduce_sum | solution.py:513
  84.5 0.6 pad_maximum_fusion
  (2 shorter events, 0.0 us)
Async XLA Ops:
  0.6 4.8 %copy-start.8 = (bf16[4,192,7,7]{1,0,3,2:T(4,128)(2,1)S(1)}, bf16[4,192,7,7]{1,0,3,2:T(4,128)(2,1)}, u32[]{:S(2)}) copy-start(bf16[4,192,7,7]{1,0,3,2:T(4,128)(2,1)} %param.10) | copy-start | bytes 225796
  0.6 2.5 %collective-permute-start = (bf16[6,64,768]{2,1,0:T(8,128)(2,1)}, bf16[6,64,768]{2,1,0:T(8,128)(2,1)S(1)}, u32[]{:S(2)}, u32[]{:S(2)}) collective-permute-start(bf16[6,64,768]{2,1,0:T(8,128)(2,1)} %f_own.3), channel_id=1, source_target_pairs={{0,1},{1,0},{2,3},{3,2},{4,5},{5,4},{6,7},{7,6},{8,9},{9,8},{10,11... | collective-permute-start | bytes 1769480 | tf_op jit(solution)/shard_map/ppermute | solution.py:54
  0.7 6.8 %collective-permute-start.2 = (bf16[6,64,768]{2,1,0:T(8,128)(2,1)}, bf16[6,64,768]{2,1,0:T(8,128)(2,1)S(1)}, u32[]{:S(2)}, u32[]{:S(2)}) collective-permute-start(bf16[6,64,768]{2,1,0:T(8,128)(2,1)} %u_own.7), channel_id=1, source_target_pairs={{0,1},{1,0},{2,3},{3,2},{4,5},{5,4},{6,7},{7,6},{8,9},{9,8},{10,11... | collective-permute-start | bytes 1769480 | tf_op jit(solution)/shard_map/ppermute | solution.py:54
  3.8 17.8 %collective-permute-start.1 = (bf16[3,128,768]{2,1,0:T(8,128)(2,1)S(1)}, bf16[3,128,768]{2,1,0:T(8,128)(2,1)S(1)}, u32[]{:S(2)}, u32[]{:S(2)}) collective-permute-start(bf16[3,128,768]{2,1,0:T(8,128)(2,1)S(1)} %rows.1), channel_id=1, source_target_pairs={{0,4},{1,2},{2,6},{3,0},{4,8},{5,1},{6,10},{7,3},{8,12},{9,5},{10,... | collective-permute-start | bytes 1769480 | tf_op jit(solution)/shard_map/ppermute | solution.py:54
  5.5 2.0 %copy-start = (bf16[6,64,768]{2,1,0:T(8,128)(2,1)S(1)}, bf16[6,64,768]{2,1,0:T(8,128)(2,1)}, u32[]{:S(2)}) copy-start(bf16[6,64,768]{2,1,0:T(8,128)(2,1)} %f_own.3) | copy-start | bytes 1769476
  5.5 2.0 %copy-start.1 = (bf16[6,64,768]{2,1,0:T(8,128)(2,1)S(1)}, bf16[6,64,768]{2,1,0:T(8,128)(2,1)}, u32[]{:S(2)}) copy-start(bf16[6,64,768]{2,1,0:T(8,128)(2,1)} %u_own.7) | copy-start | bytes 1769476
  8.5 12.6 %collective-permute-start.3 = (bf16[64,768]{1,0:T(8,128)(2,1)S(1)}, bf16[64,768]{1,0:T(8,128)(2,1)S(1)}, u32[]{:S(2)}, u32[]{:S(2)}) collective-permute-start(bf16[64,768]{1,0:T(8,128)(2,1)S(1)} %get-tuple-element.14), channel_id=1, source_target_pairs={{0,2},{1,3},{2,0},{3,1},{4,6},{5,7},{6,4},{7,5},{8,10},{9,11},{10,... | collective-permute-start | bytes 294920 | tf_op jit(solution)/shard_map/ppermute | solution.py:54
  10.1 11.0 %collective-permute-start.4 = (bf16[64,768]{1,0:T(8,128)(2,1)S(1)}, bf16[64,768]{1,0:T(8,128)(2,1)S(1)}, u32[]{:S(2)}, u32[]{:S(2)}) collective-permute-start(bf16[64,768]{1,0:T(8,128)(2,1)S(1)} %get-tuple-element.15), channel_id=1, source_target_pairs={{0,6},{2,4},{4,10},{5,3},{6,8},{7,1},{8,14},{9,7},{10,12},{11,5},{... | collective-permute-start | bytes 294920 | tf_op jit(solution)/shard_map/ppermute | solution.py:54
  22.6 12.6 %copy-start.3 = (bf16[4,128,768]{2,1,0:T(8,128)(2,1)}, bf16[4,128,768]{2,1,0:T(8,128)(2,1)S(1)}, u32[]{:S(2)}) copy-start(bf16[4,128,768]{2,1,0:T(8,128)(2,1)S(1)} %get-tuple-element.16.p_own) | copy-start | bytes 2359300
  22.7 2.9 %collective-permute-start.5 = (bf16[4,128,768]{2,1,0:T(8,128)(2,1)S(1)}, bf16[4,128,768]{2,1,0:T(8,128)(2,1)S(1)}, u32[]{:S(2)}, u32[]{:S(2)}) collective-permute-start(bf16[4,128,768]{2,1,0:T(8,128)(2,1)S(1)} %get-tuple-element.16.p_own), channel_id=1, source_target_pairs={{0,1},{1,0},{2,3},{3,2},{4,5},{5,4},{6,7},{7,6},{8,9},{9,8},{10,11... | collective-permute-start | bytes 2359304 | tf_op jit(solution)/shard_map/ppermute | solution.py:54
  23.6 15.6 %collective-permute-start.6 = (bf16[3,128,768]{2,1,0:T(8,128)(2,1)S(1)}, bf16[3,128,768]{2,1,0:T(8,128)(2,1)S(1)}, u32[]{:S(2)}, u32[]{:S(2)}) collective-permute-start(bf16[3,128,768]{2,1,0:T(8,128)(2,1)S(1)} %get-tuple-element.19), channel_id=1, source_target_pairs={{0,4},{1,2},{2,6},{3,0},{4,8},{5,1},{6,10},{7,3},{8,12},{9,5},{10,... | collective-permute-start | bytes 1769480 | tf_op jit(solution)/shard_map/ppermute | solution.py:54
  25.5 9.7 %copy-start.5 = (bf16[4,128,768]{2,1,0:T(8,128)(2,1)}, bf16[4,128,768]{2,1,0:T(8,128)(2,1)S(1)}, u32[]{:S(2)}) copy-start(bf16[4,128,768]{2,1,0:T(8,128)(2,1)S(1)} %collective-permute-done.5.p_part) | copy-start | bytes 2359300
  39.3 43.2 %all-to-all-start = ((bf16[128,24,384]{2,1,0:T(8,128)(2,1)}), bf16[128,24,384]{2,1,0:T(8,128)(2,1)}, u32[]{:S(2)}, u32[]{:S(2)}) async-start(bf16[128,24,384]{2,1,0:T(8,128)(2,1)} %bitcast.3), calls=%async_computation | async-start | bytes 4718592 | tf_op jit(solution)/shard_map/all_to_all | solution.py:491
  49.9 2.1 %collective-permute-start.7 = (bf16[3,128,768]{2,1,0:T(8,128)(2,1)S(1)}, bf16[3,128,768]{2,1,0:T(8,128)(2,1)S(1)}, u32[]{:S(2)}, u32[]{:S(2)}) collective-permute-start(bf16[3,128,768]{2,1,0:T(8,128)(2,1)S(1)} %collective-permute-done.6.a_own.after), channel_id=1, source_target_pairs={{0,1},{1,0},{2,3},{3,2},{4,5},{5,4},{6,7},{7,6},{8,9},{9,8},{10,11... | collective-permute-start | bytes 1769480 | tf_op jit(solution)/shard_map/ppermute | solution.py:54
  51.9 2.3 %copy-start.2 = (bf16[3072,768]{1,0:T(8,128)(2,1)S(1)}, bf16[3072,768]{1,0:T(8,128)(2,1)}, u32[]{:S(2)}) copy-start(bf16[3072,768]{1,0:T(8,128)(2,1)} %w_ref.1) | copy-start | bytes 14155780
  54.3 1.1 %copy-start.4 = (bf16[4,128,768]{2,1,0:T(8,128)(2,1)S(1)}, bf16[4,128,768]{2,1,0:T(8,128)(2,1)}, u32[]{:S(2)}) copy-start(bf16[4,128,768]{2,1,0:T(8,128)(2,1)} %copy-done.3) | copy-start | bytes 2359300
  55.4 1.1 %copy-start.6 = (bf16[4,128,768]{2,1,0:T(8,128)(2,1)S(1)}, bf16[4,128,768]{2,1,0:T(8,128)(2,1)}, u32[]{:S(2)}) copy-start(bf16[4,128,768]{2,1,0:T(8,128)(2,1)} %copy-done.5) | copy-start | bytes 2359300
  56.6 1.7 %copy-start.7 = (bf16[4,384,768]{2,1,0:T(8,128)(2,1)S(1)}, bf16[4,384,768]{2,1,0:T(8,128)(2,1)}, u32[]{:S(2)}) copy-start(bf16[4,384,768]{2,1,0:T(8,128)(2,1)} %get-tuple-element.18.own_ref) | copy-start | bytes 7077892

commit v3 on v2

--- a/solution.py
+++ b/solution.py
@@ -41,6 +41,10 @@
     return pltpu.CompilerParams(vmem_limit_bytes=mib * MIB)
 
 
+def in_hbm(block):
+    return pltpu.with_memory_space_constraint(block, pltpu.HBM)
+
+
 def cost(flops, size):
     return pl.CostEstimate(flops=flops, bytes_accessed=size, transcendentals=0)
 
@@ -79,7 +83,7 @@
 
 
 def bands_kernel(info, filt, band_ref, vec_ref):
-    lat = info[1]
+    lat = my_lat()
     lane = lax.broadcasted_iota(jnp.int32, (1, 128), 1)
     row_of = lat * ROWS + lane - HALO
     row_of = jnp.where(row_of < 0, -1 - row_of, row_of)
@@ -93,7 +97,7 @@
         row = lat * ROWS + e - HALO
         row = jnp.where(row < 0, -1 - row, row)
         row = jnp.where(row >= NLAT, 2 * NLAT - 1 - row, row)
-        width, offset, reach = info[2 + row], info[2 + NLAT + row], info[2 + 2 * NLAT + row]
+        width, offset, reach = info[row], info[NLAT + row], info[2 * NLAT + row]
         low = jnp.where(lane == e, offset, low)
         high = jnp.where(lane == e, offset + width, high)
         far = jnp.where(lane == e, reach, far)
@@ -140,17 +144,25 @@
     c.wait()
 
 
+def my_core():
+    return lax.rem(lax.axis_index("lon"), 2)
+
+
+def my_lat():
+    return lax.axis_index("lat")
+
+
 def run(todo):
     each(todo, start_copy)
     each(todo, wait_copy)
 
 
-def rows_kernel(info, own, part, out, sems):
+def rows_kernel(own, part, out, sems):
     for core_is, row in enumerate((ROWS - HALO, 0)):
         low, high = slice(0, COLS), slice(COLS, CHIP)
         mine, other = (low, high) if core_is == 0 else (high, low)
 
-        @pl.when(info[0] == core_is)
+        @pl.when(my_core() == core_is)
         def _():
             run(
                 [
@@ -160,18 +172,18 @@
             )
 
 
-def relay_kernel(info, a_own, e_own, c_own, u_own, u_part, out, u_rows, sems):
+def relay_kernel(a_own, e_own, c_own, u_own, u_part, out, u_rows, sems):
     todo = [
         pltpu.make_async_copy(a_own, out.at[0:HALO], sems.at[0]),
-        pltpu.make_async_copy(e_own, out.at[HALO, 0:COLS], sems.at[1]),
-        pltpu.make_async_copy(c_own, out.at[HALO, COLS:CHIP], sems.at[2]),
+        pltpu.make_async_copy(e_own, out.at[HALO, 0:PACKED], sems.at[1]),
+        pltpu.make_async_copy(c_own, out.at[HALO, COLS : COLS + PACKED], sems.at[2]),
     ]
     each(todo, start_copy)
     for core_is, row in enumerate((ROWS - HALO, 0)):
         half0, half1 = (u_own, u_part) if core_is == 0 else (u_part, u_own)
         at = slice(row, row + HALO)
 
-        @pl.when(info[0] == core_is)
+        @pl.when(my_core() == core_is)
         def _():
             run(
                 [
@@ -183,29 +195,36 @@
     each(todo, wait_copy)
 
 
-def slots(which, group):
-    at = (2 * which + group) * EDGE
-    return slice(at, at + EDGE)
-
-
-def gather_columns(rows, first):
+PACKED = 3 * EDGE
+
+
+def gather_columns(rows, firsts):
     slot = lax.broadcasted_iota(jnp.int32, (EDGE, CHANNELS), 0)
     out = jnp.zeros((EDGE, CHANNELS), F32)
-    for m, row in enumerate(rows):
+    for m, (row, first) in enumerate(zip(rows, firsts)):
         shift = (4 * m - (0 if first else EDGE - HALO)) % EDGE
         moved = pltpu.roll(row.astype(F32), shift, 0)
         out = jnp.where((slot >= 4 * m) & (slot < 4 * m + HALO), moved, out)
     return out.astype(BF)
 
 
-def spread_columns(block, m, first):
+def pack_columns(out, rows, firsts):
+    for g in range(3):
+        four = slice(4 * g, 4 * g + 4)
+        out[g * EDGE : (g + 1) * EDGE] = gather_columns(rows[four], firsts[four])
+
+
+def spread_columns(rim, which, row, first):
+    at = 2 * HALO * which + row
+    block, m = at // 4 - which, at % 4
     slot = lax.broadcasted_iota(jnp.int32, (EDGE, CHANNELS), 0)
-    moved = pltpu.roll(block.astype(F32), ((0 if first else EDGE - HALO) - 4 * m) % EDGE, 0)
+    shift = ((0 if first else EDGE - HALO) - 4 * m) % EDGE
+    moved = pltpu.roll(rim[block * EDGE : (block + 1) * EDGE].astype(F32), shift, 0)
     keep = slot < HALO if first else slot >= EDGE - HALO
     return jnp.where(keep, moved, 0.0).astype(BF)
 
 
-def edges_kernel(info, f_own, f_part, u_own, u_part, after, edge, corner, outer, sides, sems):
+def edges_kernel(f_own, f_part, u_own, u_part, after, edge, corner, outer, sides, sems):
     first, last = slice(0, EDGE), slice(COLS - EDGE, COLS)
 
     def copies(columns, row, halves):
@@ -217,23 +236,18 @@
             todo.append(pltpu.make_async_copy(half1.at[at, last], sides.at[n, 1], sems.at[3 * n + 2]))
         return todo
 
-    @pl.when(info[0] == 0)
+    @pl.when(my_core() == 0)
     def _():
         run(copies(first, ROWS - HALO, ((f_own, f_own, f_part), (u_own, u_own, u_part))))
-        for n in range(2):
-            for g in range(2):
-                edge[slots(n, g)] = gather_columns([outer[n, 3 * g + m] for m in range(HALO)], True)
-
-    @pl.when(info[0] == 1)
+        pack_columns(edge, [outer[n, r] for n in range(2) for r in range(ROWS)], [True] * (2 * ROWS))
+
+    @pl.when(my_core() == 1)
     def _():
         run(copies(last, 0, ((f_own, f_part, f_own), (u_own, u_part, u_own))))
-        for n in range(2):
-            for g in range(2):
-                edge[slots(n, g)] = gather_columns([outer[n, 3 * g + m] for m in range(HALO)], False)
-
-    for n in range(2):
-        for side in range(2):
-            corner[slots(n, side)] = gather_columns([sides[n, side, m] for m in range(HALO)], side == 0)
+        pack_columns(edge, [outer[n, r] for n in range(2) for r in range(ROWS)], [False] * (2 * ROWS))
+
+    places = [(n, side, m) for n in range(2) for side in range(2) for m in range(HALO)]
+    pack_columns(corner, [sides[at] for at in places], [side == 0 for _, side, _ in places])
 
 
 def fill_copies(x, rim, sems, which, lat_is, half0, half1, passed0, passed1, rows0, rows1, start, stop):
@@ -255,7 +269,7 @@
     left, right = 0, EDGE + CHIP
     mid = slice(HALO, HALO + ROWS)
     for n, (ref, at) in enumerate(((passed1, 0), (passed0, 0), (passed0, COLS), (passed1, COLS))):
-        at += 2 * EDGE * which
+        at += EDGE * which
         todo.append(pltpu.make_async_copy(ref.at[HALO, at : at + 2 * EDGE], rim.at[n], sems.at[n]))
     put(half0, whole, EDGE, mid, 4)
     put(half1, whole, EDGE + COLS, mid, 5)
@@ -277,8 +291,8 @@
 FILL_SEMS = 24
 
 
-def fill(act, info, x, rim, sems, which, half, passed, rows, window):
-    core, lat = info[0], info[1]
+def fill(act, x, rim, sems, which, half, passed, rows, window):
+    core, lat = my_core(), my_lat()
     for core_is in range(2):
         refs = [pair[core_is ^ c] for pair in (half, passed, rows) for c in range(2)]
         start, stop = (core_is * COLS, core_is * COLS + WIN) if window else (0, WIDE)
@@ -289,28 +303,27 @@
                 each(fill_copies(x, rim, sems, which, lat_is, *refs, start, stop), act)
 
 
-def fill_rim(info, x, rim, left, right):
-    lat = info[1]
+def fill_rim(x, rim, which, left, right):
+    lat = my_lat()
     for at, first in ((left, False), (right, True)):
         if at is None:
             continue
         to = slice(at, at + EDGE)
         for r in range(ROWS):
-            x[HALO + r, to, :] = spread_columns(rim[int(first), slots(0, r // HALO)], r % HALO, first)
+            x[HALO + r, to, :] = spread_columns(rim[int(first)], which, r, first)
         for side, pole in ((0, 0), (1, LAT - 1)):
 
             @pl.when(lat != pole)
             def _():
                 for m in range(HALO):
-                    x[side * (HALO + ROWS) + m, to, :] = spread_columns(rim[2 + side, slots(0, 1 - int(first))], m, first)
-
-
-def grad_kernel(info, f_own, f_part, p_own, p_part, u_own, u_part, bands, g_ref, own_ref, x, rim, band, basis, ud, g, sems):
-    core = info[0]
-    band_copy = pltpu.make_async_copy(bands, band, sems.at[FILL_SEMS])
+                    x[side * (HALO + ROWS) + m, to, :] = spread_columns(rim[2 + side], which, m + (0 if first else HALO), first)
+
+
+def grad_kernel(f_own, f_part, p_own, p_part, u_own, u_part, band, g_ref, own_ref, x, rim, basis, ud, g, sems):
+    core = my_core()
 
     def inputs(act):
-        fill(act, info, x, rim, sems, 0, (f_own, f_part), (p_own, p_part), (p_own, p_part), False)
+        fill(act, x, rim, sems, 0, (f_own, f_part), (p_own, p_part), (p_own, p_part), False)
         for core_is, (u0, u1) in enumerate(((u_own, u_part), (u_part, u_own))):
             cols = slice(core_is * HALF, (core_is + 1) * HALF)
 
@@ -320,11 +333,9 @@
                 act(pltpu.make_async_copy(u1.at[:, :, cols], ud.at[ROWS : 2 * ROWS], sems.at[FILL_SEMS + 2]))
 
     inputs(start_copy)
-    band_copy.start()
     x[EXT : EXT + 1, :, :] = jnp.zeros((1, WIDE, CHANNELS), BF)
-    band_copy.wait()
     inputs(wait_copy)
-    fill_rim(info, x, rim, 0, EDGE + CHIP)
+    fill_rim(x, rim, 0, 0, EDGE + CHIP)
     for i in range(ROWS):
         for w in range(2):
             cells = x[i : i + TAPS + 1, w * COLS : w * COLS + WIN].reshape(BAND, CHANNELS)
@@ -334,11 +345,11 @@
     at = pl.multiple_of(core * CELLS, CELLS)
     own_copy = pltpu.make_async_copy(basis.at[:, pl.ds(at, CELLS)], own_ref, sems.at[FILL_SEMS])
     own_copy.start()
-    up = ud[...].reshape(2 * CELLS, HALF)
+    up = ud[...].reshape(2 * CELLS, HALF).T
     outs = []
     for k in range(NBASIS):
         to = slice(k * CHANNELS, (k + 1) * CHANNELS)
-        g[to, :] = lax.dot_general(basis[k], up, (((0,), (0,)), ((), ())), preferred_element_type=F32).astype(BF)
+        g[to, :] = jnp.dot(up, basis[k], preferred_element_type=F32).astype(BF).T
         outs.append(pltpu.make_async_copy(g.at[to], g_ref.at[to], sems.at[k]))
         outs[-1].start()
     own_copy.wait()
@@ -349,9 +360,9 @@
     del partial, after, out
 
 
-def local_kernel(info, own_ref, w_ref, vec_ref, u_own, u_part, p_own, p_part, a_own, a_part, conv_ref, state_ref, x, rim, bg, acc, sems):
+def local_kernel(own_ref, w_ref, vec_ref, u_own, u_part, p_own, p_part, a_own, a_part, conv_ref, state_ref, x, rim, bg, acc, sems):
     def inputs(act):
-        fill(act, info, x, rim, sems, 1, (u_own, u_part), (p_own, p_part), (a_own, a_part), True)
+        fill(act, x, rim, sems, 1, (u_own, u_part), (p_own, p_part), (a_own, a_part), True)
 
     inputs(start_copy)
     total = jnp.zeros((CELLS, CHANNELS), F32)
@@ -360,13 +371,13 @@
     conv_ref[...] = total.astype(BF).reshape(ROWS, COLS, CHANNELS)
     inputs(wait_copy)
 
-    @pl.when(info[0] == 0)
+    @pl.when(my_core() == 0)
     def _():
-        fill_rim(info, x, rim, 0, None)
-
-    @pl.when(info[0] == 1)
+        fill_rim(x, rim, 1, 0, None)
+
+    @pl.when(my_core() == 1)
     def _():
-        fill_rim(info, x, rim, None, WIN - EDGE)
+        fill_rim(x, rim, 1, None, WIN - EDGE)
 
     for k in range(NBASIS):
         wk = w_ref[k * CHANNELS : (k + 1) * CHANNELS, :]
@@ -388,10 +399,14 @@
     state_ref[...] = acc[...].astype(BF)
 
 
+def total_kernel(pieces, out):
+    for t in range(2):
+        out[:, t * HALF : (t + 1) * HALF] = jnp.sum(pieces[:, t].astype(F32), 0)
+
+
 def on_device(features, upstream, weights, filter_basis, lat_width, lat_offset, lon_reach):
-    lat = lax.axis_index("lat")
-    core = lax.axis_index("lon") % 2
-    info = jnp.concatenate([jnp.stack([core, lat]).astype(jnp.int32), lat_width, lat_offset, lon_reach])
+    core = my_core()
+    info = jnp.concatenate([lat_width, lat_offset, lon_reach])
 
     f_part = send(features, to_partner)
     u_part = send(upstream, to_partner)
@@ -399,13 +414,13 @@
     rows = pl.pallas_call(
         rows_kernel,
         out_shape=jax.ShapeDtypeStruct((HALO, CHIP, CHANNELS), BF),
-        in_specs=[SMEM, ANY, ANY],
+        in_specs=[ANY, ANY],
         out_specs=ANY,
         scratch_shapes=[pltpu.SemaphoreType.DMA((2,))],
         compiler_params=params(4),
         cost_estimate=cost(1000, 2_000_000),
         name="rows",
-    )(info, own_rows, f_part)
+    )(own_rows, f_part)
     af_own = send(rows, along_meridian)
     filt = jnp.transpose(filter_basis, (2, 3, 0, 1)).reshape(PLACES, NLAT)
     bands, vecs = pl.pallas_call(
@@ -424,10 +439,10 @@
     edges, corners = pl.pallas_call(
         edges_kernel,
         out_shape=(
-            jax.ShapeDtypeStruct((COLS, CHANNELS), BF),
-            jax.ShapeDtypeStruct((COLS, CHANNELS), BF),
+            jax.ShapeDtypeStruct((PACKED, CHANNELS), BF),
+            jax.ShapeDtypeStruct((PACKED, CHANNELS), BF),
         ),
-        in_specs=[SMEM] + [ANY] * 5,
+        in_specs=[ANY] * 5,
         out_specs=(VMEM, VMEM),
         scratch_shapes=[
             pltpu.VMEM((2, ROWS, EDGE, CHANNELS), BF),
@@ -437,7 +452,7 @@
         compiler_params=params(4),
         cost_estimate=cost(1000, 1_000_000),
         name="edges",
-    )(info, features, f_part, upstream, u_part, vecs)
+    )(features, f_part, upstream, u_part, vecs)
     e_own = send(edges, to_chip)
     c_own = send(corners, across)
     passed, u_rows = pl.pallas_call(
@@ -446,13 +461,13 @@
             jax.ShapeDtypeStruct((HALO + 1, CHIP, CHANNELS), BF),
             jax.ShapeDtypeStruct((HALO, CHIP, CHANNELS), BF),
         ),
-        in_specs=[SMEM] + [ANY] * 5,
+        in_specs=[ANY] * 5,
         out_specs=(ANY, ANY),
         scratch_shapes=[pltpu.SemaphoreType.DMA((5,))],
         compiler_params=params(4),
         cost_estimate=cost(1000, 4_000_000),
         name="relay",
-    )(info, af_own, e_own, c_own, upstream, u_part)
+    )(af_own, e_own, c_own, upstream, u_part)
     p_part = send(passed, to_partner)
     au_own = send(u_rows, along_meridian)
     au_part = send(au_own, to_partner)
@@ -460,30 +475,29 @@
     partial, basis_own = pl.pallas_call(
         grad_kernel,
         out_shape=(
-            jax.ShapeDtypeStruct((NBASIS * CHANNELS, HALF), BF),
+            pltpu.HBM((NBASIS * CHANNELS, HALF), BF),
             pltpu.HBM((NBASIS, CELLS, CHANNELS), BF),
         ),
-        in_specs=[SMEM] + [ANY] * 7,
+        in_specs=[ANY] * 6 + [VMEM],
         out_specs=(HBM, HBM),
         scratch_shapes=[
             pltpu.VMEM((EXT + 1, WIDE, CHANNELS), BF),
             pltpu.VMEM((4, 2 * EDGE, CHANNELS), BF),
-            pltpu.VMEM((ROWS, NBASIS * COLS, BAND), BF),
             pltpu.VMEM((NBASIS, 2 * CELLS, CHANNELS), BF),
             pltpu.VMEM((2 * ROWS, COLS, HALF), BF),
             pltpu.VMEM((NBASIS * CHANNELS, HALF), BF),
             pltpu.SemaphoreType.DMA((FILL_SEMS + 3,)),
         ],
-        compiler_params=params(32),
+        compiler_params=params(20),
         cost_estimate=cost(8_000_000_000, 12_000_000),
         name="grad",
-    )(info, features, f_part, passed, p_part, upstream, u_part, bands)
+    )(in_hbm(features), in_hbm(f_part), passed, p_part, in_hbm(upstream), in_hbm(u_part), bands)
 
     partial = pl.pallas_call(
         tie_kernel,
-        out_shape=jax.ShapeDtypeStruct(partial.shape, BF),
-        in_specs=[ANY, ANY],
-        out_specs=ANY,
+        out_shape=pltpu.HBM(partial.shape, BF),
+        in_specs=[HBM, HBM],
+        out_specs=HBM,
         input_output_aliases={0: 0},
         compiler_params=params(1),
         name="tie",
@@ -496,7 +510,7 @@
             jax.ShapeDtypeStruct((ROWS, COLS, CHANNELS), BF),
             jax.ShapeDtypeStruct((ROWS, COLS, CHANNELS), BF),
         ),
-        in_specs=[SMEM] + [VMEM] * 3 + [ANY] * 6,
+        in_specs=[VMEM] * 3 + [ANY] * 6,
         out_specs=(VMEM, VMEM),
         scratch_shapes=[
             pltpu.VMEM((EXT, WIN, CHANNELS), BF),
@@ -505,13 +519,19 @@
             pltpu.VMEM((ROWS, COLS, CHANNELS), F32),
             pltpu.SemaphoreType.DMA((FILL_SEMS,)),
         ],
-        compiler_params=params(32),
+        compiler_params=params(28),
         cost_estimate=cost(10_000_000_000, 12_000_000),
         name="local",
-    )(info, basis_own, weights, vecs, upstream, u_part, passed, p_part, au_own, au_part)
-
-    summed = pieces.astype(F32).reshape(LAT * LON // 2, 2, OWNED, HALF).sum(0)
-    weight_grad = jnp.concatenate([summed[0], summed[1]], 1)
+    )(basis_own, weights, vecs, upstream, u_part, passed, p_part, au_own, au_part)
+
+    weight_grad = pl.pallas_call(
+        total_kernel,
+        out_shape=jax.ShapeDtypeStruct((OWNED, CHANNELS), F32),
+        in_specs=[VMEM],
+        out_specs=VMEM,
+        compiler_params=params(16),
+        name="total",
+    )(pltpu.with_memory_space_constraint(pieces.reshape(LAT * LON // 2, 2, OWNED, HALF), pltpu.VMEM))
     return convolved, state_grad, weight_grad
 
 

time: 85.6 us -> 82.3 us (0.961)
  other arithmetic: 3.74 us -> 1.16 us
  local copies, waits for them, and re-layouts: 7.15 us -> 9.18 us
  Pallas kernels: 27.5 us -> 25.6 us
  starting transfers between devices: 18.8 us -> 17.8 us
    unnamed x18 -> x40, local copies, waits for them, and re-layouts: 6.29 us -> 9.12 us
    reduce_sum x1 -> x0, other arithmetic: 2.02 us -> none  [on_device(): summed = pieces.astype(F32).reshape(LAT * LON // 2, 2, OWNED, HALF).sum(0)]
    ppermute x8, waiting for transfers between devices: 16.1 us -> 17.3 us  [send(): return lax.ppermute(block, BOTH, pairs)]
    all_to_all x1, waiting for transfers between devices: 11 us -> 9.85 us  [on_device(): lax.all_to_all(partial.reshape(LAT * LON, OWNED, HALF), BOTH, 0, 0, tiled...]
    pallas_call x3 -> x4, Pallas kernels: 10.6 us -> 10.6 us  [the longest x1 9.22 us: on_device(): pl.pallas_call(grad_kernel, out_shape=(pltpu.HBM((NBASIS * CHANNELS, HALF...]
  transfers between devices with their start and end apart: 9 -> 9, of which waited for: 6 -> 7; matrix products, arithmetic and copies ran while one was open for 2% -> 1% of each run, Pallas kernels for 31% -> 30%
where the time goes in v3:
time: 82.3 us; the launch traced here: 81.7 us
  waiting for transfers between devices  27.1 us (33%)
  Pallas kernels  25.6 us (31%)
  starting transfers between devices  17.8 us (22%)
  local copies, waits for them, and re-layouts  9.18 us (11%)
  other arithmetic  1.16 us (1%)
  between operations  0.87 us (1%)
    ppermute x8, waiting for transfers between devices, send(): return lax.ppermute(block, BOTH, pairs)  17.3 us
    pallas_call x1, Pallas kernels, on_device(): pl.pallas_call(local_kernel, out_shape=(jax.ShapeDtypeStruct((ROWS, COLS,...  12.5 us
    all_to_all x1, starting transfers between devices, on_device(): lax.all_to_all(partial.reshape(LAT * LON, OWNED, HALF), BOTH, 0, 0, tiled...  9.88 us
    all_to_all x1, waiting for transfers between devices, on_device(): lax.all_to_all(partial.reshape(LAT * LON, OWNED, HALF), BOTH, 0, 0, tiled...  9.85 us
    pallas_call x1, Pallas kernels, on_device(): pl.pallas_call(grad_kernel, out_shape=(pltpu.HBM((NBASIS * CHANNELS, HALF...  9.22 us
    unnamed x40, local copies, waits for them, and re-layouts  9.12 us
    ppermute x8, starting transfers between devices, send(): return lax.ppermute(block, BOTH, pairs)  7.94 us
    pallas_call x1, Pallas kernels, on_device(): pl.pallas_call(bands_kernel, out_shape=(jax.ShapeDtypeStruct((ROWS, NBASI...  1.99 us
  transfers between devices with their start and end apart: 9, of which 7 were waited for; matrix products, arithmetic and copies ran while one was open for 1% of the time, Pallas kernels for 30%

profile of v3, /device:TPU:0, one launch (start us, length us, event | category | flops | bytes accessed | tf_op | source)
XLA Modules:
  0.0 81.7 jit_solution(7092305628650487822)
XLA Ops:
  0.6 0.0 copy-start.16
  0.6 0.0 copy-start.19
  0.7 0.0 copy-start.18
  0.7 0.0 copy-start.17
  0.7 0.1 collective-permute-start
  0.8 0.5 collective-permute-start.2
  1.3 1.1 %slice_select_fusion.own = bf16[3,64,768]{2,1,0:T(8,128)(2,1)S(1)} fusion(bf16[6,64,768]{2,1,0:T(8,128)(2,1)} %f_own.3, pred[]{:T(512)S(6)} %eq.3), kind=kLoop, calls=%fused_computation | loop fusion | flops 147456 | bytes 884737 | tf_op jit(solution)/shard_map/jit(_where)/select_n | solution.py:413
  2.3 0.6 collective-permute-done.part.f_part
  3.0 0.0 copy-start.5
  3.0 0.1 rows.1
  3.0 1.6 %collective-permute-start.1 = (bf16[3,128,768]{2,1,0:T(8,128)(2,1)S(1)}, bf16[3,128,768]{2,1,0:T(8,128)(2,1)S(1)}, u32[]{:S(2)}, u32[]{:S(2)}) collective-permute-start(bf16[3,128,768]{2,1,0:T(8,128)(2,1)S(1)} %rows.1), channel_id=1, source_target_pairs={{0,4},{1,2},{2,6},{3,0},{4,8},{5,1},{6,10},{7,3},{8,12},{9,5},{10,... | collective-permute-start | bytes 1769480 | tf_op jit(solution)/shard_map/ppermute | solution.py:58
  4.7 0.0 copy-done.16
  4.7 0.1 reshape.15.filt
  4.8 0.0 copy-done.19
  4.8 0.0 copy-done.18
  4.8 0.0 copy-done.17
  4.8 0.1 pad_add_fusion.info
  4.9 0.0 copy-start
  4.9 2.0 %bands.1 = (bf16[6,256,768]{2,1,0:T(8,128)(2,1)S(1)}, f32[7,16,384]{2,1,0:T(8,128)S(1)}) custom-call(s32[576]{0:T(1024)S(1)} %pad_add_fusion.info, bf16[196,192]{1,0:T(8,128)(2,1)S(1)} %reshape.15.filt), custom_call_target="tpu_custom_call" | custom-call | flops 2000000000 | bytes 5000000 | tf_op jit(solution)/shard_map/bands/pallas_call | solution.py:426
  6.9 0.0 copy-start.8
  6.9 0.0 collective-permute-done.2.u_part
  6.9 0.0 copy-start.3
  6.9 0.0 copy-done.5
  6.9 0.0 copy-done
  6.9 0.0 copy-done.1
  6.9 0.4 edges.1
  7.3 1.6 %collective-permute-start.3 = (bf16[48,768]{1,0:T(8,128)(2,1)S(1)}, bf16[48,768]{1,0:T(8,128)(2,1)S(1)}, u32[]{:S(2)}, u32[]{:S(2)}) collective-permute-start(bf16[48,768]{1,0:T(8,128)(2,1)S(1)} %get-tuple-element.14), channel_id=1, source_target_pairs={{0,2},{1,3},{2,0},{3,1},{4,6},{5,7},{6,4},{7,5},{8,10},{9,11},{10,... | collective-permute-start | bytes 221192 | tf_op jit(solution)/shard_map/ppermute | solution.py:58
  9.0 3.3 %collective-permute-start.4 = (bf16[48,768]{1,0:T(8,128)(2,1)S(1)}, bf16[48,768]{1,0:T(8,128)(2,1)S(1)}, u32[]{:S(2)}, u32[]{:S(2)}) collective-permute-start(bf16[48,768]{1,0:T(8,128)(2,1)S(1)} %get-tuple-element.15), channel_id=1, source_target_pairs={{0,6},{2,4},{4,10},{5,3},{6,8},{7,1},{8,14},{9,7},{10,12},{11,5},{... | collective-permute-start | bytes 221192 | tf_op jit(solution)/shard_map/ppermute | solution.py:58
  12.2 7.3 %collective-permute-done.3.e_own = bf16[48,768]{1,0:T(8,128)(2,1)S(1)} collective-permute-done((bf16[48,768]{1,0:T(8,128)(2,1)S(1)}, bf16[48,768]{1,0:T(8,128)(2,1)S(1)}, u32[]{:S(2)}, u32[]{:S(2)}) %collective-permute-start.3) | collective-permute-done | bytes 73760 | tf_op jit(solution)/shard_map/ppermute | solution.py:58
  19.6 0.0 collective-permute-done.4.c_own
  19.6 0.8 collective-permute-done.1.a_own
  20.3 0.4 relay.1
  20.7 0.0 copy-start.11
  20.8 0.7 collective-permute-start.5
  21.5 0.0 copy-done.8
  21.5 0.0 collective-permute-start.6
  21.5 1.9 %collective-permute-done.5.p_part = bf16[4,128,768]{2,1,0:T(8,128)(2,1)S(1)} collective-permute-done((bf16[4,128,768]{2,1,0:T(8,128)(2,1)S(1)}, bf16[4,128,768]{2,1,0:T(8,128)(2,1)S(1)}, u32[]{:S(2)}, u32[]{:S(2)}) %collective-permute-start.5) | collective-permute-done | bytes 786464 | tf_op jit(solution)/shard_map/ppermute | solution.py:58
  23.4 0.0 copy-start.13
  23.4 0.0 copy-done.3
  23.4 9.2 %grad.1 = (bf16[3072,384]{1,0:T(8,128)(2,1)}, bf16[4,384,768]{2,1,0:T(8,128)(2,1)}) custom-call(bf16[6,64,768]{2,1,0:T(8,128)(2,1)} %f_own.3, bf16[6,64,768]{2,1,0:T(8,128)(2,1)} %copy-done.5, bf16[4,128,768]{2,1,0:T(8,128)(2,1)S(1)} %get-tuple-element.16.p_own, bf16[4,128,768]{2,1,0:T(8,128)(2,1)S(1)} %collective-permute-done.5.p_part, ...), custom_call_target="tpu_custom_call" | custom-call | flops 8000000000 | bytes 12000000 | tf_op jit(solution)/shard_map/grad/pallas_call | solution.py:475
  32.6 0.0 copy-done.11
  32.6 0.0 copy-done.13
  32.6 4.5 %collective-permute-done.6.a_own.after = bf16[3,128,768]{2,1,0:T(8,128)(2,1)S(1)} collective-permute-done((bf16[3,128,768]{2,1,0:T(8,128)(2,1)S(1)}, bf16[3,128,768]{2,1,0:T(8,128)(2,1)S(1)}, u32[]{:S(2)}, u32[]{:S(2)}) %collective-permute-start.6) | collective-permute-done | bytes 589856 | tf_op jit(solution)/shard_map/ppermute | solution.py:58
  37.1 0.0 copy-start.6
  37.1 0.8 copy-done.6
  37.9 0.0 copy-start.2
  37.9 0.0 copy-start.4
  37.9 9.9 %all-to-all-start = ((bf16[128,24,384]{2,1,0:T(8,128)(2,1)}), bf16[128,24,384]{2,1,0:T(8,128)(2,1)S(1)}, u32[]{:S(2)}, u32[]{:S(2)}) async-start(bf16[128,24,384]{2,1,0:T(8,128)(2,1)} %bitcast.4), calls=%async_computation | async-start | bytes 4718592 | tf_op jit(solution)/shard_map/all_to_all | solution.py:505
  47.8 0.1 collective-permute-start.7
  47.9 2.2 %collective-permute-done.7.a_part = bf16[3,128,768]{2,1,0:T(8,128)(2,1)S(1)} collective-permute-done((bf16[3,128,768]{2,1,0:T(8,128)(2,1)}, bf16[3,128,768]{2,1,0:T(8,128)(2,1)S(1)}, u32[]{:S(2)}, u32[]{:S(2)}) %collective-permute-start.7) | collective-permute-done | bytes 589856 | tf_op jit(solution)/shard_map/ppermute | solution.py:58
  50.1 0.0 copy-done.2
  50.1 0.0 copy-done.4
  50.1 0.0 copy-start.7
  50.1 1.1 %copy-done.7 = bf16[3,128,768]{2,1,0:T(8,128)(2,1)S(1)} copy-done((bf16[3,128,768]{2,1,0:T(8,128)(2,1)S(1)}, bf16[3,128,768]{2,1,0:T(8,128)(2,1)}, u32[]{:S(2)}) %copy-start.7) | copy-done | bytes 589848
  51.2 0.0 copy-start.9
  51.2 0.9 %copy-done.9 = f32[7,16,384]{2,1,0:T(8,128)S(1)} copy-done((f32[7,16,384]{2,1,0:T(8,128)S(1)}, f32[7,16,384]{2,1,0:T(8,128)}, u32[]{:S(2)}) %copy-start.9) | copy-done | bytes 172056
  52.1 0.0 copy-start.10
  52.1 2.3 %copy-done.10 = bf16[3072,768]{1,0:T(8,128)(2,1)S(1)} copy-done((bf16[3072,768]{1,0:T(8,128)(2,1)S(1)}, bf16[3072,768]{1,0:T(8,128)(2,1)}, u32[]{:S(2)}) %copy-start.10) | copy-done | bytes 4718616
  54.4 1.1 %copy-done.12 = bf16[4,128,768]{2,1,0:T(8,128)(2,1)S(1)} copy-done((bf16[4,128,768]{2,1,0:T(8,128)(2,1)S(1)}, bf16[4,128,768]{2,1,0:T(8,128)(2,1)}, u32[]{:S(2)}) %copy-start.12) | copy-done | bytes 786456
  55.6 1.1 %copy-done.14 = bf16[4,128,768]{2,1,0:T(8,128)(2,1)S(1)} copy-done((bf16[4,128,768]{2,1,0:T(8,128)(2,1)S(1)}, bf16[4,128,768]{2,1,0:T(8,128)(2,1)}, u32[]{:S(2)}) %copy-start.14) | copy-done | bytes 786456
  56.7 1.7 %copy-done.15 = bf16[4,384,768]{2,1,0:T(8,128)(2,1)S(1)} copy-done((bf16[4,384,768]{2,1,0:T(8,128)(2,1)S(1)}, bf16[4,384,768]{2,1,0:T(8,128)(2,1)}, u32[]{:S(2)}) %copy-start.15) | copy-done | bytes 2359320
  58.3 12.5 %local.1 = (bf16[6,64,768]{2,1,0:T(8,128)(2,1)}, bf16[6,64,768]{2,1,0:T(8,128)(2,1)}) custom-call(bf16[4,384,768]{2,1,0:T(8,128)(2,1)S(1)} %copy-done.15, bf16[3072,768]{1,0:T(8,128)(2,1)S(1)} %copy-done.10, f32[7,16,384]{2,1,0:T(8,128)S(1)} %copy-done.9, bf16[6,64,768]{2,1,0:T(8,128)(2,1)S(1)} %copy-done.2, bf16[6,64,768]{2,1,0:T(8,128)(2,1)S(1)} %copy-done.4, ...), custom_call_target="tpu_custom_call" | custom-call | flops 10000000000 | bytes 12000000 | tf_op jit(solution)/shard_map/local/pallas_call | solution.py:507
  70.9 9.9 %all-to-all-done = bf16[128,24,384]{2,1,0:T(8,128)(2,1)S(1)} async-done(((bf16[128,24,384]{2,1,0:T(8,128)(2,1)}), bf16[128,24,384]{2,1,0:T(8,128)(2,1)S(1)}, u32[]{:S(2)}, u32[]{:S(2)}) %all-to-all-start) | async-done | bytes 2359328 | tf_op jit(solution)/shard_map/all_to_all | solution.py:505
  80.7 1.0 %total.1 = f32[24,768]{1,0:T(8,128)} custom-call(bf16[64,2,24,384]{3,2,1,0:T(8,128)(2,1)S(1)} %bitcast.3), custom_call_target="tpu_custom_call" | custom-call | tf_op jit(solution)/shard_map/total/pallas_call | solution.py:527
  (5 shorter events, 0.0 us)
Async XLA Ops:
  0.6 4.1 %copy-start.16 = (bf16[4,192,7,7]{1,0,3,2:T(4,128)(2,1)S(1)}, bf16[4,192,7,7]{1,0,3,2:T(4,128)(2,1)}, u32[]{:S(2)}) copy-start(bf16[4,192,7,7]{1,0,3,2:T(4,128)(2,1)} %param.10) | copy-start | bytes 225796
  0.6 4.1 %copy-start.19 = (s32[192]{0:T(256)S(1)}, s32[192]{0:T(256)}, u32[]{:S(2)}) copy-start(s32[192]{0:T(256)} %param.11) | copy-start | bytes 2308
  0.7 4.1 %copy-start.18 = (s32[192]{0:T(256)S(1)}, s32[192]{0:T(256)}, u32[]{:S(2)}) copy-start(s32[192]{0:T(256)} %param.12) | copy-start | bytes 2308
  0.7 4.1 %copy-start.17 = (s32[192]{0:T(256)S(1)}, s32[192]{0:T(256)}, u32[]{:S(2)}) copy-start(s32[192]{0:T(256)} %param.13) | copy-start | bytes 2308
  0.7 2.3 %collective-permute-start = (bf16[6,64,768]{2,1,0:T(8,128)(2,1)}, bf16[6,64,768]{2,1,0:T(8,128)(2,1)S(1)}, u32[]{:S(2)}, u32[]{:S(2)}) collective-permute-start(bf16[6,64,768]{2,1,0:T(8,128)(2,1)} %f_own.3), channel_id=1, source_target_pairs={{0,1},{1,0},{2,3},{3,2},{4,5},{5,4},{6,7},{7,6},{8,9},{9,8},{10,11... | collective-permute-start | bytes 1769480 | tf_op jit(solution)/shard_map/ppermute | solution.py:58
  0.8 6.1 %collective-permute-start.2 = (bf16[6,64,768]{2,1,0:T(8,128)(2,1)}, bf16[6,64,768]{2,1,0:T(8,128)(2,1)S(1)}, u32[]{:S(2)}, u32[]{:S(2)}) collective-permute-start(bf16[6,64,768]{2,1,0:T(8,128)(2,1)} %u_own.7), channel_id=1, source_target_pairs={{0,1},{1,0},{2,3},{3,2},{4,5},{5,4},{6,7},{7,6},{8,9},{9,8},{10,11... | collective-permute-start | bytes 1769480 | tf_op jit(solution)/shard_map/ppermute | solution.py:58
  3.0 3.9 %copy-start.5 = (bf16[6,64,768]{2,1,0:T(8,128)(2,1)}, bf16[6,64,768]{2,1,0:T(8,128)(2,1)S(1)}, u32[]{:S(2)}) copy-start(bf16[6,64,768]{2,1,0:T(8,128)(2,1)S(1)} %collective-permute-done.part.f_part) | copy-start | bytes 1769476
  3.0 17.3 %collective-permute-start.1 = (bf16[3,128,768]{2,1,0:T(8,128)(2,1)S(1)}, bf16[3,128,768]{2,1,0:T(8,128)(2,1)S(1)}, u32[]{:S(2)}, u32[]{:S(2)}) collective-permute-start(bf16[3,128,768]{2,1,0:T(8,128)(2,1)S(1)} %rows.1), channel_id=1, source_target_pairs={{0,4},{1,2},{2,6},{3,0},{4,8},{5,1},{6,10},{7,3},{8,12},{9,5},{10,... | collective-permute-start | bytes 1769480 | tf_op jit(solution)/shard_map/ppermute | solution.py:58
  4.9 2.0 %copy-start = (bf16[6,64,768]{2,1,0:T(8,128)(2,1)S(1)}, bf16[6,64,768]{2,1,0:T(8,128)(2,1)}, u32[]{:S(2)}) copy-start(bf16[6,64,768]{2,1,0:T(8,128)(2,1)} %f_own.3) | copy-start | bytes 1769476
  4.9 2.1 %copy-start.1 = (bf16[6,64,768]{2,1,0:T(8,128)(2,1)S(1)}, bf16[6,64,768]{2,1,0:T(8,128)(2,1)}, u32[]{:S(2)}) copy-start(bf16[6,64,768]{2,1,0:T(8,128)(2,1)} %u_own.7) | copy-start | bytes 1769476
  6.9 14.6 %copy-start.8 = (f32[7,16,384]{2,1,0:T(8,128)}, f32[7,16,384]{2,1,0:T(8,128)S(1)}, u32[]{:S(2)}) copy-start(f32[7,16,384]{2,1,0:T(8,128)S(1)} %get-tuple-element.13.after.vec_ref) | copy-start | bytes 516100
  6.9 16.5 %copy-start.3 = (bf16[6,64,768]{2,1,0:T(8,128)(2,1)}, bf16[6,64,768]{2,1,0:T(8,128)(2,1)S(1)}, u32[]{:S(2)}) copy-start(bf16[6,64,768]{2,1,0:T(8,128)(2,1)S(1)} %collective-permute-done.2.u_part) | copy-start | bytes 1769476
  7.3 12.3 %collective-permute-start.3 = (bf16[48,768]{1,0:T(8,128)(2,1)S(1)}, bf16[48,768]{1,0:T(8,128)(2,1)S(1)}, u32[]{:S(2)}, u32[]{:S(2)}) collective-permute-start(bf16[48,768]{1,0:T(8,128)(2,1)S(1)} %get-tuple-element.14), channel_id=1, source_target_pairs={{0,2},{1,3},{2,0},{3,1},{4,6},{5,7},{6,4},{7,5},{8,10},{9,11},{10,... | collective-permute-start | bytes 221192 | tf_op jit(solution)/shard_map/ppermute | solution.py:58
  9.0 10.6 %collective-permute-start.4 = (bf16[48,768]{1,0:T(8,128)(2,1)S(1)}, bf16[48,768]{1,0:T(8,128)(2,1)S(1)}, u32[]{:S(2)}, u32[]{:S(2)}) collective-permute-start(bf16[48,768]{1,0:T(8,128)(2,1)S(1)} %get-tuple-element.15), channel_id=1, source_target_pairs={{0,6},{2,4},{4,10},{5,3},{6,8},{7,1},{8,14},{9,7},{10,12},{11,5},{... | collective-permute-start | bytes 221192 | tf_op jit(solution)/shard_map/ppermute | solution.py:58
  20.7 11.9 %copy-start.11 = (bf16[4,128,768]{2,1,0:T(8,128)(2,1)}, bf16[4,128,768]{2,1,0:T(8,128)(2,1)S(1)}, u32[]{:S(2)}) copy-start(bf16[4,128,768]{2,1,0:T(8,128)(2,1)S(1)} %get-tuple-element.16.p_own) | copy-start | bytes 2359300
  20.8 2.6 %collective-permute-start.5 = (bf16[4,128,768]{2,1,0:T(8,128)(2,1)S(1)}, bf16[4,128,768]{2,1,0:T(8,128)(2,1)S(1)}, u32[]{:S(2)}, u32[]{:S(2)}) collective-permute-start(bf16[4,128,768]{2,1,0:T(8,128)(2,1)S(1)} %get-tuple-element.16.p_own), channel_id=1, source_target_pairs={{0,1},{1,0},{2,3},{3,2},{4,5},{5,4},{6,7},{7,6},{8,9},{9,8},{10,11... | collective-permute-start | bytes 2359304 | tf_op jit(solution)/shard_map/ppermute | solution.py:58
  21.5 15.6 %collective-permute-start.6 = (bf16[3,128,768]{2,1,0:T(8,128)(2,1)S(1)}, bf16[3,128,768]{2,1,0:T(8,128)(2,1)S(1)}, u32[]{:S(2)}, u32[]{:S(2)}) collective-permute-start(bf16[3,128,768]{2,1,0:T(8,128)(2,1)S(1)} %get-tuple-element.19), channel_id=1, source_target_pairs={{0,4},{1,2},{2,6},{3,0},{4,8},{5,1},{6,10},{7,3},{8,12},{9,5},{10,... | collective-permute-start | bytes 1769480 | tf_op jit(solution)/shard_map/ppermute | solution.py:58
  23.4 9.2 %copy-start.13 = (bf16[4,128,768]{2,1,0:T(8,128)(2,1)}, bf16[4,128,768]{2,1,0:T(8,128)(2,1)S(1)}, u32[]{:S(2)}) copy-start(bf16[4,128,768]{2,1,0:T(8,128)(2,1)S(1)} %collective-permute-done.5.p_part) | copy-start | bytes 2359300
  37.1 0.8 copy-start.6
  37.9 12.2 %copy-start.2 = (bf16[6,64,768]{2,1,0:T(8,128)(2,1)S(1)}, bf16[6,64,768]{2,1,0:T(8,128)(2,1)}, u32[]{:S(2)}) copy-start(bf16[6,64,768]{2,1,0:T(8,128)(2,1)} %u_own.7) | copy-start | bytes 1769476
  37.9 12.2 %copy-start.4 = (bf16[6,64,768]{2,1,0:T(8,128)(2,1)S(1)}, bf16[6,64,768]{2,1,0:T(8,128)(2,1)}, u32[]{:S(2)}) copy-start(bf16[6,64,768]{2,1,0:T(8,128)(2,1)} %copy-done.3) | copy-start | bytes 1769476
  37.9 42.8 %all-to-all-start = ((bf16[128,24,384]{2,1,0:T(8,128)(2,1)}), bf16[128,24,384]{2,1,0:T(8,128)(2,1)S(1)}, u32[]{:S(2)}, u32[]{:S(2)}) async-start(bf16[128,24,384]{2,1,0:T(8,128)(2,1)} %bitcast.4), calls=%async_computation | async-start | bytes 4718592 | tf_op jit(solution)/shard_map/all_to_all | solution.py:505
  47.8 2.3 %collective-permute-start.7 = (bf16[3,128,768]{2,1,0:T(8,128)(2,1)}, bf16[3,128,768]{2,1,0:T(8,128)(2,1)S(1)}, u32[]{:S(2)}, u32[]{:S(2)}) collective-permute-start(bf16[3,128,768]{2,1,0:T(8,128)(2,1)} %copy-done.6), channel_id=1, source_target_pairs={{0,1},{1,0},{2,3},{3,2},{4,5},{5,4},{6,7},{7,6},{8,9},{9,8},{10,11... | collective-permute-start | bytes 1769480 | tf_op jit(solution)/shard_map/ppermute | solution.py:58
  50.1 1.1 %copy-start.7 = (bf16[3,128,768]{2,1,0:T(8,128)(2,1)S(1)}, bf16[3,128,768]{2,1,0:T(8,128)(2,1)}, u32[]{:S(2)}) copy-start(bf16[3,128,768]{2,1,0:T(8,128)(2,1)} %copy-done.6) | copy-start | bytes 1769476
  51.2 0.9 %copy-start.9 = (f32[7,16,384]{2,1,0:T(8,128)S(1)}, f32[7,16,384]{2,1,0:T(8,128)}, u32[]{:S(2)}) copy-start(f32[7,16,384]{2,1,0:T(8,128)} %copy-done.8) | copy-start | bytes 516100
  52.1 2.3 %copy-start.10 = (bf16[3072,768]{1,0:T(8,128)(2,1)S(1)}, bf16[3072,768]{1,0:T(8,128)(2,1)}, u32[]{:S(2)}) copy-start(bf16[3072,768]{1,0:T(8,128)(2,1)} %w_ref.1) | copy-start | bytes 14155780
  54.4 1.1 %copy-start.12 = (bf16[4,128,768]{2,1,0:T(8,128)(2,1)S(1)}, bf16[4,128,768]{2,1,0:T(8,128)(2,1)}, u32[]{:S(2)}) copy-start(bf16[4,128,768]{2,1,0:T(8,128)(2,1)} %copy-done.11) | copy-start | bytes 2359300
  55.5 1.1 %copy-start.14 = (bf16[4,128,768]{2,1,0:T(8,128)(2,1)S(1)}, bf16[4,128,768]{2,1,0:T(8,128)(2,1)}, u32[]{:S(2)}) copy-start(bf16[4,128,768]{2,1,0:T(8,128)(2,1)} %copy-done.13) | copy-start | bytes 2359300
  56.7 1.7 %copy-start.15 = (bf16[4,384,768]{2,1,0:T(8,128)(2,1)S(1)}, bf16[4,384,768]{2,1,0:T(8,128)(2,1)}, u32[]{:S(2)}) copy-start(bf16[4,384,768]{2,1,0:T(8,128)(2,1)} %get-tuple-element.18.own_ref) | copy-start | bytes 7077892

commit v4 on v3

--- a/solution.py
+++ b/solution.py
@@ -23,6 +23,8 @@
 CELLS = ROWS * COLS
 BAND = (TAPS + 1) * WIN
 SPAN = NBASIS * WIN
+OUTER = ROWS * EDGE + HALO * WIN
+TALL = ROWS * NBASIS * COLS
 PLACES = TAPS * TAPS * NBASIS
 OWNED = NBASIS * CHANNELS // (LAT * LON)
 BF = jnp.bfloat16
@@ -82,7 +84,7 @@
     return high, values - high * size
 
 
-def bands_kernel(info, filt, band_ref, vec_ref):
+def bands_kernel(info, filt, inner_ref, outer_ref, vec_ref):
     lat = my_lat()
     lane = lax.broadcasted_iota(jnp.int32, (1, 128), 1)
     row_of = lat * ROWS + lane - HALO
@@ -110,13 +112,41 @@
     b = b - (EDGE - HALO)
     band_at = jnp.where((a < TAPS) & (b >= 0) & (b < TAPS), (a * TAPS + b) * NBASIS, -PLACES)
     place = lax.broadcasted_iota(jnp.int32, (PLACES, BAND), 0)
+    edge_a, edge_q = split(lax.broadcasted_iota(jnp.int32, (1, 128), 1), EDGE)
+    edge_place = lax.broadcasted_iota(jnp.int32, (PLACES, 128), 0)
+    edge_at = []
+    for w in range(2):
+        b = edge_q - (EDGE - HALO) if w == 0 else edge_q + HALO + 1
+        ok = (edge_a < TAPS) & (b >= 0) & (b < TAPS)
+        edge_at.append(jnp.where(ok, (edge_a * TAPS + b) * NBASIS, -PLACES))
+    j = lax.broadcasted_iota(jnp.int32, (COLS, 128), 0)
+    _, q = split(lax.broadcasted_iota(jnp.int32, (COLS, 128), 1), EDGE)
+    inside = (q >= EDGE - HALO + j, q <= j - (COLS - HALO))
+    in_edge = lax.broadcasted_iota(jnp.int32, (COLS, 128), 1) < ROWS * EDGE
+
+    def turned(vec, i, keep, shift, width):
+        row = jnp.where(keep, vec[HALO + i : HALO + i + 1, :], 0.0)
+        return pltpu.roll(jnp.broadcast_to(row, (COLS, width)), shift % width, 1, stride=1, stride_axis=0)
+
     for k in range(NBASIS):
         put = (place == band_at + k).astype(F32).astype(BF)
         vec = lax.dot_general(rows, put, over, preferred_element_type=F32)
+        edge_vec = []
+        for w in range(2):
+            put = (edge_place == edge_at[w] + k).astype(F32).astype(BF)
+            edge_vec.append(lax.dot_general(rows, put, over, preferred_element_type=F32))
         for i in range(ROWS):
-            row = jnp.broadcast_to(vec[HALO + i : HALO + i + 1, :], (COLS, BAND))
-            block = pltpu.roll(row, 0, 1, stride=1, stride_axis=0)
-            band_ref[i, k * COLS : (k + 1) * COLS, :] = block.astype(BF)
+            to = slice((i * NBASIS + k) * COLS, (i * NBASIS + k + 1) * COLS)
+            keep = (a >= HALO - i) & (a < HALO + ROWS - i)
+            inner_ref[to, :] = turned(vec, i, keep, (i - HALO) * WIN, BAND).astype(BF)
+            keep = (a < HALO - i) if i < HALO else (a >= HALO + ROWS - i)
+            rim = turned(vec, i, keep, (1 + i if i < HALO else i - TAPS - 1) * WIN, BAND)
+            keep = (edge_a >= HALO - i) & (edge_a < HALO + ROWS - i)
+            for w in range(2):
+                edge = turned(edge_vec[w], i, keep, (i - HALO) * EDGE - w * (COLS - 1), 128)
+                edge = jnp.where(inside[w], edge, 0.0)
+                outer_ref[w, to, 0:128] = jnp.where(in_edge, edge, rim[:, 0:128]).astype(BF)
+                outer_ref[w, to, 128:OUTER] = rim[:, 128:OUTER].astype(BF)
     k, b = split(lax.broadcasted_iota(jnp.int32, (1, SPAN), 1), WIN)
     b = EDGE + HALO - b
     spread_at = jnp.where((b >= 0) & (b < TAPS), b * NBASIS + k, -PLACES)
@@ -157,42 +187,43 @@
     each(todo, wait_copy)
 
 
+def row_copies(sources, out, sems, turn):
+    todo = []
+    for n, (ref, row, columns) in enumerate(sources):
+        if turn:
+            for m in range(HALO):
+                todo.append(pltpu.make_async_copy(ref.at[row + HALO - 1 - m], out.at[m, columns], sems.at[HALO * n + m]))
+        else:
+            todo.append(pltpu.make_async_copy(ref.at[row : row + HALO], out.at[:, columns], sems.at[HALO * n]))
+    return todo
+
+
+def chip_rows(own, own_row, part, out, sems, act):
+    low, high = slice(0, COLS), slice(COLS, CHIP)
+    for core_is, row, pole in ((0, ROWS - HALO, LAT - 1), (1, 0, 0)):
+        mine, other = (low, high) if core_is == 0 else (high, low)
+        sources = ((own, row if own_row is None else own_row, mine), (part, row, other))
+        for turn in (False, True):
+
+            @pl.when((my_core() == core_is) & ((my_lat() == pole) == turn))
+            def _():
+                each(row_copies(sources, out, sems, turn), act)
+
+
 def rows_kernel(own, part, out, sems):
-    for core_is, row in enumerate((ROWS - HALO, 0)):
-        low, high = slice(0, COLS), slice(COLS, CHIP)
-        mine, other = (low, high) if core_is == 0 else (high, low)
-
-        @pl.when(my_core() == core_is)
-        def _():
-            run(
-                [
-                    pltpu.make_async_copy(own, out.at[:, mine], sems.at[0]),
-                    pltpu.make_async_copy(part.at[row : row + HALO], out.at[:, other], sems.at[1]),
-                ]
-            )
-
-
-def relay_kernel(a_own, e_own, c_own, u_own, u_part, out, u_rows, sems):
-    todo = [
-        pltpu.make_async_copy(a_own, out.at[0:HALO], sems.at[0]),
-        pltpu.make_async_copy(e_own, out.at[HALO, 0:PACKED], sems.at[1]),
-        pltpu.make_async_copy(c_own, out.at[HALO, COLS : COLS + PACKED], sems.at[2]),
-    ]
-    each(todo, start_copy)
-    for core_is, row in enumerate((ROWS - HALO, 0)):
-        half0, half1 = (u_own, u_part) if core_is == 0 else (u_part, u_own)
-        at = slice(row, row + HALO)
-
-        @pl.when(my_core() == core_is)
-        def _():
-            run(
-                [
-                    pltpu.make_async_copy(half0.at[at], u_rows.at[:, 0:COLS], sems.at[3]),
-                    pltpu.make_async_copy(half1.at[at], u_rows.at[:, COLS:CHIP], sems.at[4]),
-                ]
-            )
-
-    each(todo, wait_copy)
+    chip_rows(own, 0, part, out, sems, start_copy)
+    chip_rows(own, 0, part, out, sems, wait_copy)
+
+
+def relay_kernel(a_own, e_own, c_own, u_rows, out, u_out, sems):
+    del u_rows, u_out
+    run(
+        [
+            pltpu.make_async_copy(a_own, out.at[0:HALO], sems.at[0]),
+            pltpu.make_async_copy(e_own, out.at[HALO, 0:PACKED], sems.at[1]),
+            pltpu.make_async_copy(c_own, out.at[HALO, COLS : COLS + PACKED], sems.at[2]),
+        ]
+    )
 
 
 PACKED = 3 * EDGE
@@ -224,7 +255,7 @@
     return jnp.where(keep, moved, 0.0).astype(BF)
 
 
-def edges_kernel(f_own, f_part, u_own, u_part, after, edge, corner, outer, sides, sems):
+def edges_kernel(f_own, f_part, u_own, u_part, edge, corner, outer, sides, sems):
     first, last = slice(0, EDGE), slice(COLS - EDGE, COLS)
 
     def copies(columns, row, halves):
@@ -279,23 +310,21 @@
         if lat_is == side:
             for m in range(HALO):
                 own = HALO - 1 - m + side * (ROWS - HALO)
-                put_row(rows, HALO - 1 - m, slice(0, CHIP), EDGE, to + m, n + 3 * m)
-                put_row(half1, own, last, left, to + m, n + 3 * m + 1)
-                put_row(half0, own, first, right, to + m, n + 3 * m + 2)
-        else:
-            put(rows.at[0:HALO], slice(0, CHIP), EDGE, slice(to, to + HALO), n)
-        n += 9
+                put_row(half1, own, last, left, to + m, n + 2 * m + 1)
+                put_row(half0, own, first, right, to + m, n + 2 * m + 2)
+        put(rows.at[0:HALO], slice(0, CHIP), EDGE, slice(to, to + HALO), n)
+        n += 7
     return todo
 
 
-FILL_SEMS = 24
-
-
-def fill(act, x, rim, sems, which, half, passed, rows, window):
+FILL_SEMS = 20
+
+
+def fill(act, x, rim, sems, which, half, passed, rows):
     core, lat = my_core(), my_lat()
     for core_is in range(2):
         refs = [pair[core_is ^ c] for pair in (half, passed, rows) for c in range(2)]
-        start, stop = (core_is * COLS, core_is * COLS + WIN) if window else (0, WIDE)
+        start, stop = core_is * COLS, core_is * COLS + WIN
         for lat_is, here in ((0, lat == 0), (1, lat == LAT - 1), (None, (lat > 0) & (lat < LAT - 1))):
 
             @pl.when((core == core_is) & here)
@@ -319,56 +348,124 @@
                     x[side * (HALO + ROWS) + m, to, :] = spread_columns(rim[2 + side], which, m + (0 if first else HALO), first)
 
 
-def grad_kernel(f_own, f_part, p_own, p_part, u_own, u_part, band, g_ref, own_ref, x, rim, basis, ud, g, sems):
+def inner_kernel(f_own, f_part, u_own, u_part, band, acc, up_ref, pole_ref, u_rows, x, ud, sems, row_sems):
     core = my_core()
+    chip_rows(u_own, None, u_part, u_rows, row_sems, start_copy)
 
     def inputs(act):
-        fill(act, x, rim, sems, 0, (f_own, f_part), (p_own, p_part), (p_own, p_part), False)
-        for core_is, (u0, u1) in enumerate(((u_own, u_part), (u_part, u_own))):
+        for core_is, (f0, f1, u0, u1) in enumerate(((f_own, f_part, u_own, u_part), (f_part, f_own, u_part, u_own))):
             cols = slice(core_is * HALF, (core_is + 1) * HALF)
 
             @pl.when(core == core_is)
             def _():
-                act(pltpu.make_async_copy(u0.at[:, :, cols], ud.at[0:ROWS], sems.at[FILL_SEMS + 1]))
-                act(pltpu.make_async_copy(u1.at[:, :, cols], ud.at[ROWS : 2 * ROWS], sems.at[FILL_SEMS + 2]))
+                act(pltpu.make_async_copy(f0, x.at[0:ROWS, EDGE : EDGE + COLS], sems.at[0]))
+                act(pltpu.make_async_copy(f1, x.at[0:ROWS, EDGE + COLS : EDGE + CHIP], sems.at[1]))
+                act(pltpu.make_async_copy(u0.at[:, :, cols], ud.at[0:ROWS], sems.at[2]))
+                act(pltpu.make_async_copy(u1.at[:, :, cols], ud.at[ROWS : 2 * ROWS], sems.at[3]))
 
     inputs(start_copy)
-    x[EXT : EXT + 1, :, :] = jnp.zeros((1, WIDE, CHANNELS), BF)
+    x[0:ROWS, 0:EDGE, :] = jnp.zeros((ROWS, EDGE, CHANNELS), BF)
+    x[0:ROWS, EDGE + CHIP :, :] = jnp.zeros((ROWS, EDGE, CHANNELS), BF)
+    x[ROWS:, :, :] = jnp.zeros((2, WIDE, CHANNELS), BF)
     inputs(wait_copy)
-    fill_rim(x, rim, 0, 0, EDGE + CHIP)
-    for i in range(ROWS):
+    shift = jnp.where(my_lat() == LAT - 1, ROWS - HALO, 0)
+    for m in range(HALO):
+        row = HALO - 1 - m + shift
+        pole_ref[0, m] = x[row, CHIP : CHIP + EDGE, :]
+        pole_ref[1, m] = x[row, EDGE : 2 * EDGE, :]
+    for w in range(2):
+        cells = x[:, w * COLS : w * COLS + WIN].reshape(BAND, CHANNELS)
+        for part in range(3):
+            to = slice(part * (TALL // 3), (part + 1) * (TALL // 3))
+            acc[w, to] = jnp.dot(band[to], cells, preferred_element_type=F32)
+    up_ref[...] = ud[...].reshape(2 * CELLS, HALF).T
+    chip_rows(u_own, None, u_part, u_rows, row_sems, wait_copy)
+
+
+def outer_copies(x, rim, sems, passed0, passed1):
+    todo = []
+    for n, (ref, at) in enumerate(((passed1, 0), (passed0, 0), (passed0, COLS), (passed1, COLS))):
+        todo.append(pltpu.make_async_copy(ref.at[HALO, at : at + 2 * EDGE], rim.at[n], sems.at[n]))
+    low, high = slice(0, WIN - EDGE), slice(CHIP - WIN + EDGE, CHIP)
+    for side, rows in enumerate((passed0, passed1)):
+        n = 4 + 2 * side
+        todo.append(pltpu.make_async_copy(rows.at[0:HALO, low], x.at[side, 0, 1 : 1 + HALO, EDGE:WIN], sems.at[n]))
+        todo.append(pltpu.make_async_copy(rows.at[0:HALO, high], x.at[side, 1, 1 : 1 + HALO, 0 : WIN - EDGE], sems.at[n + 1]))
+    return todo
+
+
+OUTER_SEMS = 8
+
+
+def grad_kernel(p_own, p_part, pole_ref, acc, band, up, g_ref, own_ref, x, rim, basis, g, sems):
+    core, lat = my_core(), my_lat()
+
+    def inputs(act):
+        for core_is, refs in enumerate(((p_own, p_part), (p_part, p_own))):
+
+            @pl.when(core == core_is)
+            def _():
+                each(outer_copies(x, rim, sems, *refs), act)
+
+    inputs(start_copy)
+    inputs(wait_copy)
+    for w, first in ((0, False), (1, True)):
+        for r in range(ROWS):
+            columns = spread_columns(rim[w], 0, r, first)
+            for side in range(2):
+                x[side, w, 0, r * EDGE : (r + 1) * EDGE, :] = columns
+        at = w * (WIN - EDGE)
+        for side, pole in ((0, 0), (1, LAT - 1)):
+
+            @pl.when(lat != pole)
+            def _():
+                for m in range(HALO):
+                    x[side, w, 1 + m, at : at + EDGE, :] = spread_columns(rim[2 + side], 0, m + (0 if first else HALO), first)
+
+            @pl.when(lat == pole)
+            def _():
+                for m in range(HALO):
+                    x[side, w, 1 + m, at : at + EDGE, :] = pole_ref[w, m]
+
+    for side in range(2):
+        to = slice(side * (TALL // 2), (side + 1) * (TALL // 2))
         for w in range(2):
-            cells = x[i : i + TAPS + 1, w * COLS : w * COLS + WIN].reshape(BAND, CHANNELS)
-            rows = jnp.dot(band[i], cells, preferred_element_type=F32).astype(BF)
-            for k in range(NBASIS):
-                basis[k, w * CELLS + i * COLS : w * CELLS + (i + 1) * COLS, :] = rows[k * COLS : (k + 1) * COLS]
+            cells = x[side, w].reshape(OUTER, CHANNELS)
+            rows = (acc[w, to] + jnp.dot(band[w, to], cells, preferred_element_type=F32)).astype(BF)
+            for m in range(HALO):
+                at = w * CELLS + (side * HALO + m) * COLS
+                for k in range(NBASIS):
+                    n = (m * NBASIS + k) * COLS
+                    basis[k, at : at + COLS, :] = rows[n : n + COLS]
     at = pl.multiple_of(core * CELLS, CELLS)
-    own_copy = pltpu.make_async_copy(basis.at[:, pl.ds(at, CELLS)], own_ref, sems.at[FILL_SEMS])
+    own_copy = pltpu.make_async_copy(basis.at[:, pl.ds(at, CELLS)], own_ref, sems.at[4])
     own_copy.start()
-    up = ud[...].reshape(2 * CELLS, HALF).T
     outs = []
     for k in range(NBASIS):
         to = slice(k * CHANNELS, (k + 1) * CHANNELS)
-        g[to, :] = jnp.dot(up, basis[k], preferred_element_type=F32).astype(BF).T
+        g[to, :] = jnp.dot(up[...], basis[k], preferred_element_type=F32).astype(BF).T
         outs.append(pltpu.make_async_copy(g.at[to], g_ref.at[to], sems.at[k]))
         outs[-1].start()
     own_copy.wait()
     each(outs, wait_copy)
 
 
-def tie_kernel(partial, after, out):
-    del partial, after, out
-
-
-def local_kernel(own_ref, w_ref, vec_ref, u_own, u_part, p_own, p_part, a_own, a_part, conv_ref, state_ref, x, rim, bg, acc, sems):
-    def inputs(act):
-        fill(act, x, rim, sems, 1, (u_own, u_part), (p_own, p_part), (a_own, a_part), True)
-
-    inputs(start_copy)
+def tie_kernel(rows, after, out):
+    del rows, after, out
+
+
+def conv_kernel(own_ref, w_ref, conv_ref):
     total = jnp.zeros((CELLS, CHANNELS), F32)
     for k in range(NBASIS):
         total = total + jnp.dot(own_ref[k], w_ref[k * CHANNELS : (k + 1) * CHANNELS, :], preferred_element_type=F32)
     conv_ref[...] = total.astype(BF).reshape(ROWS, COLS, CHANNELS)
+
+
+def state_kernel(w_ref, vec_ref, u_own, u_part, p_own, p_part, a_own, a_part, state_ref, x, rim, bg, acc, sems):
+    def inputs(act):
+        fill(act, x, rim, sems, 1, (u_own, u_part), (p_own, p_part), (a_own, a_part))
+
+    inputs(start_copy)
     inputs(wait_copy)
 
     @pl.when(my_core() == 0)
@@ -416,21 +513,22 @@
         out_shape=jax.ShapeDtypeStruct((HALO, CHIP, CHANNELS), BF),
         in_specs=[ANY, ANY],
         out_specs=ANY,
-        scratch_shapes=[pltpu.SemaphoreType.DMA((2,))],
+        scratch_shapes=[pltpu.SemaphoreType.DMA((2 * HALO,))],
         compiler_params=params(4),
         cost_estimate=cost(1000, 2_000_000),
         name="rows",
     )(own_rows, f_part)
     af_own = send(rows, along_meridian)
     filt = jnp.transpose(filter_basis, (2, 3, 0, 1)).reshape(PLACES, NLAT)
-    bands, vecs = pl.pallas_call(
+    inner_band, outer_band, vecs = pl.pallas_call(
         bands_kernel,
         out_shape=(
-            jax.ShapeDtypeStruct((ROWS, NBASIS * COLS, BAND), BF),
+            jax.ShapeDtypeStruct((TALL, BAND), BF),
+            jax.ShapeDtypeStruct((2, TALL, OUTER), BF),
             jax.ShapeDtypeStruct((TAPS, 16, SPAN), F32),
         ),
         in_specs=[SMEM, VMEM],
-        out_specs=(VMEM, VMEM),
+        out_specs=(VMEM, VMEM, VMEM),
         compiler_params=params(16),
         cost_estimate=cost(2_000_000_000, 5_000_000),
         name="bands",
@@ -442,7 +540,7 @@
             jax.ShapeDtypeStruct((PACKED, CHANNELS), BF),
             jax.ShapeDtypeStruct((PACKED, CHANNELS), BF),
         ),
-        in_specs=[ANY] * 5,
+        in_specs=[ANY] * 4,
         out_specs=(VMEM, VMEM),
         scratch_shapes=[
             pltpu.VMEM((2, ROWS, EDGE, CHANNELS), BF),
@@ -452,66 +550,91 @@
         compiler_params=params(4),
         cost_estimate=cost(1000, 1_000_000),
         name="edges",
-    )(features, f_part, upstream, u_part, vecs)
+    )(features, f_part, upstream, u_part)
     e_own = send(edges, to_chip)
     c_own = send(corners, across)
+    acc, up, pole, u_rows = pl.pallas_call(
+        inner_kernel,
+        out_shape=(
+            jax.ShapeDtypeStruct((2, TALL, CHANNELS), F32),
+            jax.ShapeDtypeStruct((HALF, 2 * CELLS), BF),
+            jax.ShapeDtypeStruct((2, HALO, EDGE, CHANNELS), BF),
+            jax.ShapeDtypeStruct((HALO, CHIP, CHANNELS), BF),
+        ),
+        in_specs=[ANY] * 4 + [VMEM],
+        out_specs=(VMEM, VMEM, VMEM, ANY),
+        scratch_shapes=[
+            pltpu.VMEM((ROWS + 2, WIDE, CHANNELS), BF),
+            pltpu.VMEM((2 * ROWS, COLS, HALF), BF),
+            pltpu.SemaphoreType.DMA((4,)),
+            pltpu.SemaphoreType.DMA((2 * HALO,)),
+        ],
+        compiler_params=params(28),
+        cost_estimate=cost(4_000_000_000, 16_000_000),
+        name="inner",
+    )(features, f_part, upstream, u_part, inner_band)
     passed, u_rows = pl.pallas_call(
         relay_kernel,
         out_shape=(
             jax.ShapeDtypeStruct((HALO + 1, CHIP, CHANNELS), BF),
             jax.ShapeDtypeStruct((HALO, CHIP, CHANNELS), BF),
         ),
-        in_specs=[ANY] * 5,
+        in_specs=[ANY] * 4,
         out_specs=(ANY, ANY),
-        scratch_shapes=[pltpu.SemaphoreType.DMA((5,))],
+        input_output_aliases={3: 1},
+        scratch_shapes=[pltpu.SemaphoreType.DMA((3,))],
         compiler_params=params(4),
         cost_estimate=cost(1000, 4_000_000),
         name="relay",
-    )(af_own, e_own, c_own, upstream, u_part)
+    )(af_own, e_own, c_own, u_rows)
     p_part = send(passed, to_partner)
     au_own = send(u_rows, along_meridian)
-    au_part = send(au_own, to_partner)
-
     partial, basis_own = pl.pallas_call(
         grad_kernel,
         out_shape=(
             pltpu.HBM((NBASIS * CHANNELS, HALF), BF),
             pltpu.HBM((NBASIS, CELLS, CHANNELS), BF),
         ),
-        in_specs=[ANY] * 6 + [VMEM],
+        in_specs=[ANY] * 2 + [VMEM] * 4,
         out_specs=(HBM, HBM),
         scratch_shapes=[
-            pltpu.VMEM((EXT + 1, WIDE, CHANNELS), BF),
+            pltpu.VMEM((2, 2, 1 + HALO, WIN, CHANNELS), BF),
             pltpu.VMEM((4, 2 * EDGE, CHANNELS), BF),
             pltpu.VMEM((NBASIS, 2 * CELLS, CHANNELS), BF),
-            pltpu.VMEM((2 * ROWS, COLS, HALF), BF),
             pltpu.VMEM((NBASIS * CHANNELS, HALF), BF),
-            pltpu.SemaphoreType.DMA((FILL_SEMS + 3,)),
+            pltpu.SemaphoreType.DMA((OUTER_SEMS,)),
         ],
+        compiler_params=params(30),
+        cost_estimate=cost(6_000_000_000, 12_000_000),
+        name="grad",
+    )(passed, p_part, pole, acc, outer_band, up)
+
+    pieces = lax.all_to_all(partial.reshape(LAT * LON, OWNED, HALF), BOTH, 0, 0, tiled=True)
+
+    convolved = pl.pallas_call(
+        conv_kernel,
+        out_shape=jax.ShapeDtypeStruct((ROWS, COLS, CHANNELS), BF),
+        in_specs=[VMEM] * 2,
+        out_specs=VMEM,
         compiler_params=params(20),
-        cost_estimate=cost(8_000_000_000, 12_000_000),
-        name="grad",
-    )(in_hbm(features), in_hbm(f_part), passed, p_part, in_hbm(upstream), in_hbm(u_part), bands)
-
-    partial = pl.pallas_call(
+        cost_estimate=cost(80_000_000_000, 8_000_000),
+        name="conv",
+    )(basis_own, weights)
+    au_own = pl.pallas_call(
         tie_kernel,
-        out_shape=pltpu.HBM(partial.shape, BF),
-        in_specs=[HBM, HBM],
-        out_specs=HBM,
+        out_shape=jax.ShapeDtypeStruct(au_own.shape, BF),
+        in_specs=[ANY, ANY],
+        out_specs=ANY,
         input_output_aliases={0: 0},
         compiler_params=params(1),
         name="tie",
-    )(partial, au_own)
-    pieces = lax.all_to_all(partial.reshape(LAT * LON, OWNED, HALF), BOTH, 0, 0, tiled=True)
-
-    convolved, state_grad = pl.pallas_call(
-        local_kernel,
-        out_shape=(
-            jax.ShapeDtypeStruct((ROWS, COLS, CHANNELS), BF),
-            jax.ShapeDtypeStruct((ROWS, COLS, CHANNELS), BF),
-        ),
-        in_specs=[VMEM] * 3 + [ANY] * 6,
-        out_specs=(VMEM, VMEM),
+    )(au_own, in_hbm(convolved))
+    au_part = send(au_own, to_partner)
+    state_grad = pl.pallas_call(
+        state_kernel,
+        out_shape=jax.ShapeDtypeStruct((ROWS, COLS, CHANNELS), BF),
+        in_specs=[VMEM] * 2 + [ANY] * 6,
+        out_specs=VMEM,
         scratch_shapes=[
             pltpu.VMEM((EXT, WIN, CHANNELS), BF),
             pltpu.VMEM((4, 2 * EDGE, CHANNELS), BF),
@@ -520,9 +643,9 @@
             pltpu.SemaphoreType.DMA((FILL_SEMS,)),
         ],
         compiler_params=params(28),
-        cost_estimate=cost(10_000_000_000, 12_000_000),
-        name="local",
-    )(basis_own, weights, vecs, upstream, u_part, passed, p_part, au_own, au_part)
+        cost_estimate=cost(8_000_000_000, 12_000_000),
+        name="state",
+    )(weights, vecs, upstream, u_part, passed, p_part, au_own, au_part)
 
     weight_grad = pl.pallas_call(
         total_kernel,

time: 82.3 us -> 75.9 us (0.922)
  waiting for transfers between devices: 27.1 us -> 18.9 us
  Pallas kernels: 25.6 us -> 28 us
  local copies, waits for them, and re-layouts: 9.18 us -> 7.1 us
  starting transfers between devices: 17.8 us -> 19.5 us
    ppermute x8, waiting for transfers between devices: 17.3 us -> 7.3 us  [send(): return lax.ppermute(block, BOTH, pairs)]
    pallas_call x3 -> x5, Pallas kernels: 14.5 us -> 20 us  [the longest x1 10.2 us: on_device(): pl.pallas_call(state_kernel, out_shape=jax.ShapeDtypeStruct((ROWS, COLS,...]
    pallas_call x1, Pallas kernels: 9.22 us -> 6.23 us  [on_device(): pl.pallas_call(grad_kernel, out_shape=(pltpu.HBM((NBASIS * CHANNELS, HALF...]
    unnamed x40 -> x34, local copies, waits for them, and re-layouts: 9.12 us -> 7.03 us
    all_to_all x1, starting transfers between devices: 9.88 us -> 11.6 us  [on_device(): lax.all_to_all(partial.reshape(LAT * LON, OWNED, HALF), BOTH, 0, 0, tiled...]
    all_to_all x1, waiting for transfers between devices: 9.85 us -> 11.6 us  [on_device(): lax.all_to_all(partial.reshape(LAT * LON, OWNED, HALF), BOTH, 0, 0, tiled...]
  transfers between devices with their start and end apart: 9 -> 9, of which waited for: 7 -> 6; matrix products, arithmetic and copies ran while one was open for 1% -> 2% of each run, Pallas kernels for 30% -> 35%
where the time goes in v4:
time: 75.9 us; the launch traced here: 75.5 us
  Pallas kernels  28 us (37%)
  starting transfers between devices  19.5 us (26%)
  waiting for transfers between devices  18.9 us (25%)
  local copies, waits for them, and re-layouts  7.1 us (9%)
  other arithmetic  1.16 us (2%)
  between operations  0.87 us (1%)
    all_to_all x1, starting transfers between devices, on_device(): lax.all_to_all(partial.reshape(LAT * LON, OWNED, HALF), BOTH, 0, 0, tiled...  11.6 us
    all_to_all x1, waiting for transfers between devices, on_device(): lax.all_to_all(partial.reshape(LAT * LON, OWNED, HALF), BOTH, 0, 0, tiled...  11.6 us
    pallas_call x1, Pallas kernels, on_device(): pl.pallas_call(state_kernel, out_shape=jax.ShapeDtypeStruct((ROWS, COLS,...  10.2 us
    ppermute x8, starting transfers between devices, send(): return lax.ppermute(block, BOTH, pairs)  7.86 us
    ppermute x8, waiting for transfers between devices, send(): return lax.ppermute(block, BOTH, pairs)  7.3 us
    unnamed x34, local copies, waits for them, and re-layouts  7.03 us
    pallas_call x1, Pallas kernels, on_device(): pl.pallas_call(grad_kernel, out_shape=(pltpu.HBM((NBASIS * CHANNELS, HALF...  6.23 us
    pallas_call x1, Pallas kernels, on_device(): pl.pallas_call(inner_kernel, out_shape=(jax.ShapeDtypeStruct((2, TALL, CH...  4.18 us
  transfers between devices with their start and end apart: 9, of which 6 were waited for; matrix products, arithmetic and copies ran while one was open for 2% of the time, Pallas kernels for 35%

profile of v4, /device:TPU:0, one launch (start us, length us, event | category | flops | bytes accessed | tf_op | source)
XLA Modules:
  0.0 75.5 jit_solution(11862530112128611925)
XLA Ops:
  0.6 0.0 copy-start.14
  0.6 0.0 copy-start.15
  0.7 0.0 copy-start.16
  0.7 0.0 copy-start.13
  0.7 0.1 collective-permute-start
  0.8 0.5 collective-permute-start.2
  1.3 1.1 %slice_select_fusion.own = bf16[3,64,768]{2,1,0:T(8,128)(2,1)S(1)} fusion(bf16[6,64,768]{2,1,0:T(8,128)(2,1)} %f_own.3, pred[]{:T(512)S(6)} %eq.3), kind=kLoop, calls=%fused_computation | loop fusion | flops 147456 | bytes 884737 | tf_op jit(solution)/shard_map/jit(_where)/select_n | solution.py:510
  2.3 0.6 collective-permute-done.part.f_part
  3.0 0.1 rows.1
  3.1 1.6 %collective-permute-start.1 = (bf16[3,128,768]{2,1,0:T(8,128)(2,1)S(1)}, bf16[3,128,768]{2,1,0:T(8,128)(2,1)S(1)}, u32[]{:S(2)}, u32[]{:S(2)}) collective-permute-start(bf16[3,128,768]{2,1,0:T(8,128)(2,1)S(1)} %rows.1), channel_id=1, source_target_pairs={{0,4},{1,2},{2,6},{3,0},{4,8},{5,1},{6,10},{7,3},{8,12},{9,5},{10,... | collective-permute-start | bytes 1769480 | tf_op jit(solution)/shard_map/ppermute | solution.py:60
  4.7 0.0 copy-done.14
  4.8 0.0 copy-done.15
  4.8 0.0 copy-done.16
  4.8 0.1 pad_add_fusion.info
  4.8 0.0 copy-done.13
  4.8 0.1 reshape.15.filt
  4.9 0.0 copy-start
  4.9 0.0 copy-start.1
  4.9 2.8 %bands.1 = (bf16[1536,768]{1,0:T(8,128)(2,1)S(1)}, bf16[2,1536,384]{2,1,0:T(8,128)(2,1)S(1)}, f32[7,16,384]{2,1,0:T(8,128)S(1)}) custom-call(s32[576]{0:T(1024)S(1)} %pad_add_fusion.info, bf16[196,192]{1,0:T(8,128)(2,1)S(1)} %reshape.15.filt), custom_call_target="tpu_custom_call" | custom-call | flops 2000000000 | bytes 5000000 | tf_op jit(solution)/shard_map/bands/pallas_call | solution.py:523
  7.8 0.0 copy-start.11
  7.8 0.6 copy-done.11
  8.4 0.0 collective-permute-done.2.u_part
  8.4 0.0 copy-done
  8.4 0.0 copy-done.1
  8.4 0.0 copy-start.2
  8.4 0.4 edges.1
  8.8 1.7 %collective-permute-start.3 = (bf16[48,768]{1,0:T(8,128)(2,1)S(1)}, bf16[48,768]{1,0:T(8,128)(2,1)S(1)}, u32[]{:S(2)}, u32[]{:S(2)}) collective-permute-start(bf16[48,768]{1,0:T(8,128)(2,1)S(1)} %get-tuple-element.16), channel_id=1, source_target_pairs={{0,2},{1,3},{2,0},{3,1},{4,6},{5,7},{6,4},{7,5},{8,10},{9,11},{10,... | collective-permute-start | bytes 221192 | tf_op jit(solution)/shard_map/ppermute | solution.py:60
  10.5 3.3 %collective-permute-start.4 = (bf16[48,768]{1,0:T(8,128)(2,1)S(1)}, bf16[48,768]{1,0:T(8,128)(2,1)S(1)}, u32[]{:S(2)}, u32[]{:S(2)}) collective-permute-start(bf16[48,768]{1,0:T(8,128)(2,1)S(1)} %get-tuple-element.17), channel_id=1, source_target_pairs={{0,6},{2,4},{4,10},{5,3},{6,8},{7,1},{8,14},{9,7},{10,12},{11,5},{... | collective-permute-start | bytes 221192 | tf_op jit(solution)/shard_map/ppermute | solution.py:60
  13.8 4.2 %inner.1 = (f32[2,1536,768]{2,1,0:T(8,128)S(1)}, bf16[384,768]{1,0:T(8,128)(2,1)S(1)}, bf16[2,3,16,768]{3,2,1,0:T(8,128)(2,1)S(1)}, bf16[3,128,768]{2,1,0:T(8,128)(2,1)}) custom-call(bf16[6,64,768]{2,1,0:T(8,128)(2,1)S(1)} %copy-done, bf16[6,64,768]{2,1,0:T(8,128)(2,1)S(1)} %collective-permute-done.part.f_part, bf16[6,64,768]{2,1,0:T(8,128)(2,1)S(1)} %copy-done.1, ...), custom_call_target="tpu_custom_call" | custom-call | flops 4000000000 | bytes 16000000 | tf_op jit(solution)/shard_map/inner/pallas_call | solution.py:556
  17.9 0.0 copy-done.2
  17.9 1.7 %collective-permute-done.3.e_own = bf16[48,768]{1,0:T(8,128)(2,1)S(1)} collective-permute-done((bf16[48,768]{1,0:T(8,128)(2,1)S(1)}, bf16[48,768]{1,0:T(8,128)(2,1)S(1)}, u32[]{:S(2)}, u32[]{:S(2)}) %collective-permute-start.3) | collective-permute-done | bytes 73760 | tf_op jit(solution)/shard_map/ppermute | solution.py:60
  19.6 0.0 collective-permute-done.4.c_own
  19.6 1.1 %collective-permute-done.1.a_own = bf16[3,128,768]{2,1,0:T(8,128)(2,1)S(1)} collective-permute-done((bf16[3,128,768]{2,1,0:T(8,128)(2,1)S(1)}, bf16[3,128,768]{2,1,0:T(8,128)(2,1)S(1)}, u32[]{:S(2)}, u32[]{:S(2)}) %collective-permute-start.1) | collective-permute-done | bytes 589856 | tf_op jit(solution)/shard_map/ppermute | solution.py:60
  20.7 0.3 relay.1
  21.1 0.0 copy-start.6
  21.1 0.7 collective-permute-start.5
  21.8 0.0 collective-permute-start.6
  21.8 1.9 %collective-permute-done.5.p_part = bf16[4,128,768]{2,1,0:T(8,128)(2,1)S(1)} collective-permute-done((bf16[4,128,768]{2,1,0:T(8,128)(2,1)S(1)}, bf16[4,128,768]{2,1,0:T(8,128)(2,1)S(1)}, u32[]{:S(2)}, u32[]{:S(2)}) %collective-permute-start.5) | collective-permute-done | bytes 786464 | tf_op jit(solution)/shard_map/ppermute | solution.py:60
  23.7 0.0 copy-start.8
  23.7 6.2 %grad.1 = (bf16[3072,384]{1,0:T(8,128)(2,1)}, bf16[4,384,768]{2,1,0:T(8,128)(2,1)}) custom-call(bf16[4,128,768]{2,1,0:T(8,128)(2,1)S(1)} %get-tuple-element.20.p_own, bf16[4,128,768]{2,1,0:T(8,128)(2,1)S(1)} %collective-permute-done.5.p_part, bf16[2,3,16,768]{3,2,1,0:T(8,128)(2,1)S(1)} %get-tuple-element.21.pole_ref, ...), custom_call_target="tpu_custom_call" | custom-call | flops 6000000000 | bytes 12000000 | tf_op jit(solution)/shard_map/grad/pallas_call | solution.py:592
  29.9 0.0 copy-done.6
  29.9 0.0 copy-done.8
  29.9 11.6 %all-to-all-start = ((bf16[128,24,384]{2,1,0:T(8,128)(2,1)}), bf16[128,24,384]{2,1,0:T(8,128)(2,1)S(1)}, u32[]{:S(2)}, u32[]{:S(2)}) async-start(bf16[128,24,384]{2,1,0:T(8,128)(2,1)} %bitcast.4), calls=%async_computation | async-start | bytes 4718592 | tf_op jit(solution)/shard_map/all_to_all | solution.py:612
  41.6 0.0 copy-start.4
  41.6 2.3 %copy-done.4 = bf16[3072,768]{1,0:T(8,128)(2,1)S(1)} copy-done((bf16[3072,768]{1,0:T(8,128)(2,1)S(1)}, bf16[3072,768]{1,0:T(8,128)(2,1)}, u32[]{:S(2)}) %copy-start.4) | copy-done | bytes 4718616
  43.9 0.0 copy-start.10
  43.9 1.7 %copy-done.10 = bf16[4,384,768]{2,1,0:T(8,128)(2,1)S(1)} copy-done((bf16[4,384,768]{2,1,0:T(8,128)(2,1)S(1)}, bf16[4,384,768]{2,1,0:T(8,128)(2,1)}, u32[]{:S(2)}) %copy-start.10) | copy-done | bytes 2359320
  45.6 0.0 copy-start.3
  45.6 0.0 copy-start.7
  45.6 0.0 copy-start.9
  45.6 0.0 copy-start.12
  45.6 2.8 %conv.1.after = bf16[6,64,768]{2,1,0:T(8,128)(2,1)} custom-call(bf16[4,384,768]{2,1,0:T(8,128)(2,1)S(1)} %copy-done.10, bf16[3072,768]{1,0:T(8,128)(2,1)S(1)} %copy-done.4), custom_call_target="tpu_custom_call" | custom-call | flops 80000000000 | bytes 8000000 | tf_op jit(solution)/shard_map/conv/pallas_call | solution.py:614
  48.4 0.0 collective-permute-done.6.rows
  48.4 0.0 collective-permute-start.7
  48.4 2.0 %collective-permute-done.7.a_part = bf16[3,128,768]{2,1,0:T(8,128)(2,1)S(1)} collective-permute-done((bf16[3,128,768]{2,1,0:T(8,128)(2,1)S(1)}, bf16[3,128,768]{2,1,0:T(8,128)(2,1)S(1)}, u32[]{:S(2)}, u32[]{:S(2)}) %collective-permute-start.7) | collective-permute-done | bytes 589856 | tf_op jit(solution)/shard_map/ppermute | solution.py:60
  50.4 0.0 copy-done.3
  50.4 0.0 copy-done.7
  50.4 0.0 copy-done.9
  50.4 0.0 copy-done.12
  50.4 0.0 copy-start.5
  50.4 2.3 %copy-done.5 = bf16[3072,768]{1,0:T(8,128)(2,1)S(1)} copy-done((bf16[3072,768]{1,0:T(8,128)(2,1)S(1)}, bf16[3072,768]{1,0:T(8,128)(2,1)}, u32[]{:S(2)}) %copy-start.5) | copy-done | bytes 4718616
  52.8 10.2 %state.1 = bf16[6,64,768]{2,1,0:T(8,128)(2,1)} custom-call(bf16[3072,768]{1,0:T(8,128)(2,1)S(1)} %copy-done.5, f32[7,16,384]{2,1,0:T(8,128)S(1)} %copy-done.12, bf16[6,64,768]{2,1,0:T(8,128)(2,1)S(1)} %copy-done.1, bf16[6,64,768]{2,1,0:T(8,128)(2,1)S(1)} %copy-done.3, bf16[4,128,768]{2,1,0:T(8,128)(2,1)S(1)} %copy-done.7, ...), custom_call_target="tpu_custom_call" | custom-call | flops 8000000000 | bytes 12000000 | tf_op jit(solution)/shard_map/state/pallas_call | solution.py:633
  62.9 11.6 %all-to-all-done = bf16[128,24,384]{2,1,0:T(8,128)(2,1)S(1)} async-done(((bf16[128,24,384]{2,1,0:T(8,128)(2,1)}), bf16[128,24,384]{2,1,0:T(8,128)(2,1)S(1)}, u32[]{:S(2)}, u32[]{:S(2)}) %all-to-all-start) | async-done | bytes 2359328 | tf_op jit(solution)/shard_map/all_to_all | solution.py:612
  74.5 1.0 %total.1 = f32[24,768]{1,0:T(8,128)} custom-call(bf16[64,2,24,384]{3,2,1,0:T(8,128)(2,1)S(1)} %bitcast.3), custom_call_target="tpu_custom_call" | custom-call | tf_op jit(solution)/shard_map/total/pallas_call | solution.py:650
  (1 shorter events, 0.0 us)
Async XLA Ops:
  0.6 4.1 %copy-start.14 = (s32[192]{0:T(256)S(1)}, s32[192]{0:T(256)}, u32[]{:S(2)}) copy-start(s32[192]{0:T(256)} %param.13) | copy-start | bytes 2308
  0.6 4.1 %copy-start.15 = (s32[192]{0:T(256)S(1)}, s32[192]{0:T(256)}, u32[]{:S(2)}) copy-start(s32[192]{0:T(256)} %param.12) | copy-start | bytes 2308
  0.7 4.1 %copy-start.16 = (s32[192]{0:T(256)S(1)}, s32[192]{0:T(256)}, u32[]{:S(2)}) copy-start(s32[192]{0:T(256)} %param.11) | copy-start | bytes 2308
  0.7 4.2 %copy-start.13 = (bf16[4,192,7,7]{1,0,3,2:T(4,128)(2,1)S(1)}, bf16[4,192,7,7]{1,0,3,2:T(4,128)(2,1)}, u32[]{:S(2)}) copy-start(bf16[4,192,7,7]{1,0,3,2:T(4,128)(2,1)} %param.10) | copy-start | bytes 225796
  0.7 2.3 %collective-permute-start = (bf16[6,64,768]{2,1,0:T(8,128)(2,1)}, bf16[6,64,768]{2,1,0:T(8,128)(2,1)S(1)}, u32[]{:S(2)}, u32[]{:S(2)}) collective-permute-start(bf16[6,64,768]{2,1,0:T(8,128)(2,1)} %f_own.3), channel_id=1, source_target_pairs={{0,1},{1,0},{2,3},{3,2},{4,5},{5,4},{6,7},{7,6},{8,9},{9,8},{10,11... | collective-permute-start | bytes 1769480 | tf_op jit(solution)/shard_map/ppermute | solution.py:60
  0.8 7.7 %collective-permute-start.2 = (bf16[6,64,768]{2,1,0:T(8,128)(2,1)}, bf16[6,64,768]{2,1,0:T(8,128)(2,1)S(1)}, u32[]{:S(2)}, u32[]{:S(2)}) collective-permute-start(bf16[6,64,768]{2,1,0:T(8,128)(2,1)} %u_own.5), channel_id=1, source_target_pairs={{0,1},{1,0},{2,3},{3,2},{4,5},{5,4},{6,7},{7,6},{8,9},{9,8},{10,11... | collective-permute-start | bytes 1769480 | tf_op jit(solution)/shard_map/ppermute | solution.py:60
  3.1 17.6 %collective-permute-start.1 = (bf16[3,128,768]{2,1,0:T(8,128)(2,1)S(1)}, bf16[3,128,768]{2,1,0:T(8,128)(2,1)S(1)}, u32[]{:S(2)}, u32[]{:S(2)}) collective-permute-start(bf16[3,128,768]{2,1,0:T(8,128)(2,1)S(1)} %rows.1), channel_id=1, source_target_pairs={{0,4},{1,2},{2,6},{3,0},{4,8},{5,1},{6,10},{7,3},{8,12},{9,5},{10,... | collective-permute-start | bytes 1769480 | tf_op jit(solution)/shard_map/ppermute | solution.py:60
  4.9 3.5 %copy-start = (bf16[6,64,768]{2,1,0:T(8,128)(2,1)S(1)}, bf16[6,64,768]{2,1,0:T(8,128)(2,1)}, u32[]{:S(2)}) copy-start(bf16[6,64,768]{2,1,0:T(8,128)(2,1)} %f_own.3) | copy-start | bytes 1769476
  4.9 3.5 %copy-start.1 = (bf16[6,64,768]{2,1,0:T(8,128)(2,1)S(1)}, bf16[6,64,768]{2,1,0:T(8,128)(2,1)}, u32[]{:S(2)}) copy-start(bf16[6,64,768]{2,1,0:T(8,128)(2,1)} %u_own.5) | copy-start | bytes 1769476
  7.8 0.7 copy-start.11
  8.4 9.5 %copy-start.2 = (bf16[6,64,768]{2,1,0:T(8,128)(2,1)}, bf16[6,64,768]{2,1,0:T(8,128)(2,1)S(1)}, u32[]{:S(2)}) copy-start(bf16[6,64,768]{2,1,0:T(8,128)(2,1)S(1)} %collective-permute-done.2.u_part) | copy-start | bytes 1769476
  8.8 10.8 %collective-permute-start.3 = (bf16[48,768]{1,0:T(8,128)(2,1)S(1)}, bf16[48,768]{1,0:T(8,128)(2,1)S(1)}, u32[]{:S(2)}, u32[]{:S(2)}) collective-permute-start(bf16[48,768]{1,0:T(8,128)(2,1)S(1)} %get-tuple-element.16), channel_id=1, source_target_pairs={{0,2},{1,3},{2,0},{3,1},{4,6},{5,7},{6,4},{7,5},{8,10},{9,11},{10,... | collective-permute-start | bytes 221192 | tf_op jit(solution)/shard_map/ppermute | solution.py:60
  10.5 9.2 %collective-permute-start.4 = (bf16[48,768]{1,0:T(8,128)(2,1)S(1)}, bf16[48,768]{1,0:T(8,128)(2,1)S(1)}, u32[]{:S(2)}, u32[]{:S(2)}) collective-permute-start(bf16[48,768]{1,0:T(8,128)(2,1)S(1)} %get-tuple-element.17), channel_id=1, source_target_pairs={{0,6},{2,4},{4,10},{5,3},{6,8},{7,1},{8,14},{9,7},{10,12},{11,5},{... | collective-permute-start | bytes 221192 | tf_op jit(solution)/shard_map/ppermute | solution.py:60
  21.1 8.9 %copy-start.6 = (bf16[4,128,768]{2,1,0:T(8,128)(2,1)}, bf16[4,128,768]{2,1,0:T(8,128)(2,1)S(1)}, u32[]{:S(2)}) copy-start(bf16[4,128,768]{2,1,0:T(8,128)(2,1)S(1)} %get-tuple-element.20.p_own) | copy-start | bytes 2359300
  21.1 2.6 %collective-permute-start.5 = (bf16[4,128,768]{2,1,0:T(8,128)(2,1)S(1)}, bf16[4,128,768]{2,1,0:T(8,128)(2,1)S(1)}, u32[]{:S(2)}, u32[]{:S(2)}) collective-permute-start(bf16[4,128,768]{2,1,0:T(8,128)(2,1)S(1)} %get-tuple-element.20.p_own), channel_id=1, source_target_pairs={{0,1},{1,0},{2,3},{3,2},{4,5},{5,4},{6,7},{7,6},{8,9},{9,8},{10,11... | collective-permute-start | bytes 2359304 | tf_op jit(solution)/shard_map/ppermute | solution.py:60
  21.8 26.6 %collective-permute-start.6 = (bf16[3,128,768]{2,1,0:T(8,128)(2,1)}, bf16[3,128,768]{2,1,0:T(8,128)(2,1)S(1)}, u32[]{:S(2)}, u32[]{:S(2)}) collective-permute-start(bf16[3,128,768]{2,1,0:T(8,128)(2,1)} %get-tuple-element.27), channel_id=1, source_target_pairs={{0,4},{1,2},{2,6},{3,0},{4,8},{5,1},{6,10},{7,3},{8,12},{9,5},{10,... | collective-permute-start | bytes 1769480 | tf_op jit(solution)/shard_map/ppermute | solution.py:60
  23.7 6.2 %copy-start.8 = (bf16[4,128,768]{2,1,0:T(8,128)(2,1)}, bf16[4,128,768]{2,1,0:T(8,128)(2,1)S(1)}, u32[]{:S(2)}) copy-start(bf16[4,128,768]{2,1,0:T(8,128)(2,1)S(1)} %collective-permute-done.5.p_part) | copy-start | bytes 2359300
  29.9 44.6 %all-to-all-start = ((bf16[128,24,384]{2,1,0:T(8,128)(2,1)}), bf16[128,24,384]{2,1,0:T(8,128)(2,1)S(1)}, u32[]{:S(2)}, u32[]{:S(2)}) async-start(bf16[128,24,384]{2,1,0:T(8,128)(2,1)} %bitcast.4), calls=%async_computation | async-start | bytes 4718592 | tf_op jit(solution)/shard_map/all_to_all | solution.py:612
  41.6 2.3 %copy-start.4 = (bf16[3072,768]{1,0:T(8,128)(2,1)S(1)}, bf16[3072,768]{1,0:T(8,128)(2,1)}, u32[]{:S(2)}) copy-start(bf16[3072,768]{1,0:T(8,128)(2,1)} %w_ref.3) | copy-start | bytes 14155780
  43.9 1.7 %copy-start.10 = (bf16[4,384,768]{2,1,0:T(8,128)(2,1)S(1)}, bf16[4,384,768]{2,1,0:T(8,128)(2,1)}, u32[]{:S(2)}) copy-start(bf16[4,384,768]{2,1,0:T(8,128)(2,1)} %get-tuple-element.25.own_ref) | copy-start | bytes 7077892
  45.6 4.8 %copy-start.3 = (bf16[6,64,768]{2,1,0:T(8,128)(2,1)S(1)}, bf16[6,64,768]{2,1,0:T(8,128)(2,1)}, u32[]{:S(2)}) copy-start(bf16[6,64,768]{2,1,0:T(8,128)(2,1)} %copy-done.2) | copy-start | bytes 1769476
  45.6 4.8 %copy-start.7 = (bf16[4,128,768]{2,1,0:T(8,128)(2,1)S(1)}, bf16[4,128,768]{2,1,0:T(8,128)(2,1)}, u32[]{:S(2)}) copy-start(bf16[4,128,768]{2,1,0:T(8,128)(2,1)} %copy-done.6) | copy-start | bytes 2359300
  45.6 4.8 %copy-start.9 = (bf16[4,128,768]{2,1,0:T(8,128)(2,1)S(1)}, bf16[4,128,768]{2,1,0:T(8,128)(2,1)}, u32[]{:S(2)}) copy-start(bf16[4,128,768]{2,1,0:T(8,128)(2,1)} %copy-done.8) | copy-start | bytes 2359300
  45.6 4.8 %copy-start.12 = (f32[7,16,384]{2,1,0:T(8,128)S(1)}, f32[7,16,384]{2,1,0:T(8,128)}, u32[]{:S(2)}) copy-start(f32[7,16,384]{2,1,0:T(8,128)} %copy-done.11) | copy-start | bytes 516100
  48.4 2.0 %collective-permute-start.7 = (bf16[3,128,768]{2,1,0:T(8,128)(2,1)S(1)}, bf16[3,128,768]{2,1,0:T(8,128)(2,1)S(1)}, u32[]{:S(2)}, u32[]{:S(2)}) collective-permute-start(bf16[3,128,768]{2,1,0:T(8,128)(2,1)S(1)} %tie.1.a_own), channel_id=1, source_target_pairs={{0,1},{1,0},{2,3},{3,2},{4,5},{5,4},{6,7},{7,6},{8,9},{9,8},{10,11... | collective-permute-start | bytes 1769480 | tf_op jit(solution)/shard_map/ppermute | solution.py:60
  50.4 2.3 %copy-start.5 = (bf16[3072,768]{1,0:T(8,128)(2,1)S(1)}, bf16[3072,768]{1,0:T(8,128)(2,1)}, u32[]{:S(2)}) copy-start(bf16[3072,768]{1,0:T(8,128)(2,1)} %w_ref.3) | copy-start | bytes 14155780

commit v5 on v4

--- a/solution.py
+++ b/solution.py
@@ -23,7 +23,7 @@
 CELLS = ROWS * COLS
 BAND = (TAPS + 1) * WIN
 SPAN = NBASIS * WIN
-OUTER = ROWS * EDGE + HALO * WIN
+OUTER = (HALO + 1) * WIN
 TALL = ROWS * NBASIS * COLS
 PLACES = TAPS * TAPS * NBASIS
 OWNED = NBASIS * CHANNELS // (LAT * LON)
@@ -84,7 +84,18 @@
     return high, values - high * size
 
 
-def bands_kernel(info, filt, inner_ref, outer_ref, vec_ref):
+def outer_rows(i):
+    return ((0, 384), (96, 256), (192, 128), (64, 128), (64, 256), (0, 384))[i]
+
+
+def outer_lanes(i):
+    first = outer_rows(i)[0]
+    if i < HALO:
+        return i * WIN - first, HALO * WIN - first
+    return WIN - first, WIN - 2 * EDGE - first
+
+
+def masked_filters(info, filt):
     lat = my_lat()
     lane = lax.broadcasted_iota(jnp.int32, (1, 128), 1)
     row_of = lat * ROWS + lane - HALO
@@ -106,47 +117,79 @@
     a, rest = split(lax.broadcasted_iota(jnp.int32, (PLACES, 128), 0), TAPS * NBASIS)
     b, _ = split(rest, NBASIS)
     keep = (a >= low) & (a < high) & (jnp.abs(b - HALO) <= far)
-    rows = jnp.where(keep, rows, 0.0).astype(BF)
-    over = (((0,), (0,)), ((), ()))
+    return jnp.where(keep, rows, 0.0).astype(BF)
+
+
+OVER_ROWS = (((0,), (0,)), ((), ()))
+
+
+def bands_kernel(info, filt, inner_ref, outer_ref):
+    rows = masked_filters(info, filt)
     a, b = split(lax.broadcasted_iota(jnp.int32, (1, BAND), 1), WIN)
     b = b - (EDGE - HALO)
     band_at = jnp.where((a < TAPS) & (b >= 0) & (b < TAPS), (a * TAPS + b) * NBASIS, -PLACES)
     place = lax.broadcasted_iota(jnp.int32, (PLACES, BAND), 0)
-    edge_a, edge_q = split(lax.broadcasted_iota(jnp.int32, (1, 128), 1), EDGE)
+    edge_a, edge_c = split(lax.broadcasted_iota(jnp.int32, (1, 128), 1), 4)
     edge_place = lax.broadcasted_iota(jnp.int32, (PLACES, 128), 0)
     edge_at = []
     for w in range(2):
-        b = edge_q - (EDGE - HALO) if w == 0 else edge_q + HALO + 1
-        ok = (edge_a < TAPS) & (b >= 0) & (b < TAPS)
+        b = edge_c + w * (HALO + 1)
+        ok = (edge_a < TAPS) & (edge_c < HALO)
         edge_at.append(jnp.where(ok, (edge_a * TAPS + b) * NBASIS, -PLACES))
-    j = lax.broadcasted_iota(jnp.int32, (COLS, 128), 0)
-    _, q = split(lax.broadcasted_iota(jnp.int32, (COLS, 128), 1), EDGE)
-    inside = (q >= EDGE - HALO + j, q <= j - (COLS - HALO))
-    in_edge = lax.broadcasted_iota(jnp.int32, (COLS, 128), 1) < ROWS * EDGE
-
-    def turned(vec, i, keep, shift, width):
-        row = jnp.where(keep, vec[HALO + i : HALO + i + 1, :], 0.0)
-        return pltpu.roll(jnp.broadcast_to(row, (COLS, width)), shift % width, 1, stride=1, stride_axis=0)
+    j = lax.broadcasted_iota(jnp.int32, (8, 128), 0)
+    _, c = split(lax.broadcasted_iota(jnp.int32, (8, 128), 1), 4)
+    inside = ((c >= j) & (c < HALO), c <= j - (8 - HALO))
+    far_lane = lax.broadcasted_iota(jnp.int32, (8, 128), 1)
+
+    def moved(row, shift):
+        width = row.shape[1]
+        return pltpu.roll(jnp.broadcast_to(row, (8, width)), shift % width, 1)[0:1]
+
+    def skewed(row, rows):
+        return pltpu.roll(jnp.broadcast_to(row, (rows, row.shape[1])), 0, 1, stride=1, stride_axis=0)
 
     for k in range(NBASIS):
         put = (place == band_at + k).astype(F32).astype(BF)
-        vec = lax.dot_general(rows, put, over, preferred_element_type=F32)
+        vec = lax.dot_general(rows, put, OVER_ROWS, preferred_element_type=F32)
         edge_vec = []
         for w in range(2):
             put = (edge_place == edge_at[w] + k).astype(F32).astype(BF)
-            edge_vec.append(lax.dot_general(rows, put, over, preferred_element_type=F32))
+            edge_vec.append(lax.dot_general(rows, put, OVER_ROWS, preferred_element_type=F32))
         for i in range(ROWS):
-            to = slice((i * NBASIS + k) * COLS, (i * NBASIS + k + 1) * COLS)
-            keep = (a >= HALO - i) & (a < HALO + ROWS - i)
-            inner_ref[to, :] = turned(vec, i, keep, (i - HALO) * WIN, BAND).astype(BF)
-            keep = (a < HALO - i) if i < HALO else (a >= HALO + ROWS - i)
-            rim = turned(vec, i, keep, (1 + i if i < HALO else i - TAPS - 1) * WIN, BAND)
-            keep = (edge_a >= HALO - i) & (edge_a < HALO + ROWS - i)
+            own = slice(HALO + i, HALO + i + 1)
+            start = (i * NBASIS + k) * COLS
+            to = slice(start, start + COLS)
+            row = jnp.where((a >= HALO - i) & (a < HALO + ROWS - i), vec[own], 0.0)
+            row = jnp.broadcast_to(row, (COLS, BAND))
+            row = pltpu.roll(row, (i - HALO) * WIN % BAND, 1, stride=1, stride_axis=0)
+            inner_ref[to, :] = row.astype(BF)
+            first_rim, at_edge = outer_lanes(i)
+            size = outer_rows(i)[1]
+            if i < HALO:
+                row = jnp.where(a < HALO - i, vec[own], 0.0)[:, :size]
+            else:
+                row = jnp.where(a >= HALO + ROWS - i, vec[own], 0.0)[:, OUTER:]
+                row = moved(row, first_rim + OUTER - (HALO + ROWS - i) * WIN)[:, :size]
+            rim = skewed(row, COLS)
+            tile = slice(at_edge // 128 * 128, at_edge // 128 * 128 + 128)
+            in_edge = (far_lane >= at_edge % 128) & (far_lane < at_edge % 128 + 4 * ROWS)
             for w in range(2):
-                edge = turned(edge_vec[w], i, keep, (i - HALO) * EDGE - w * (COLS - 1), 128)
-                edge = jnp.where(inside[w], edge, 0.0)
-                outer_ref[w, to, 0:128] = jnp.where(in_edge, edge, rim[:, 0:128]).astype(BF)
-                outer_ref[w, to, 128:OUTER] = rim[:, 128:OUTER].astype(BF)
+                row = jnp.where((edge_a >= HALO - i) & (edge_a < HALO + ROWS - i), edge_vec[w][own], 0.0)
+                edge = skewed(moved(row, (i - HALO) * 4 + at_edge - 7 * w), 8)
+                edge = jnp.where(inside[w] & in_edge, edge, 0.0)
+                none = jnp.zeros((8, 128), F32)
+                outer_ref[w, to, :size] = rim.astype(BF)
+                if w == 0:
+                    edge = rim[:EDGE, tile] + jnp.concatenate([edge, none], 0)
+                    outer_ref[w, start : start + EDGE, tile] = edge.astype(BF)
+                else:
+                    edge = rim[COLS - EDGE :, tile] + jnp.concatenate([none, edge], 0)
+                    outer_ref[w, start + COLS - EDGE : start + COLS, tile] = edge.astype(BF)
+
+
+def spread_kernel(info, filt, after, vec_ref):
+    lat = my_lat()
+    rows = masked_filters(info, filt)
     k, b = split(lax.broadcasted_iota(jnp.int32, (1, SPAN), 1), WIN)
     b = EDGE + HALO - b
     spread_at = jnp.where((b >= 0) & (b < TAPS), b * NBASIS + k, -PLACES)
@@ -154,7 +197,7 @@
     vecs = []
     for a in range(TAPS):
         put = (place == spread_at + a * TAPS * NBASIS).astype(F32).astype(BF)
-        vecs.append(lax.dot_general(rows, put, over, preferred_element_type=F32)[:16])
+        vecs.append(lax.dot_general(rows, put, OVER_ROWS, preferred_element_type=F32)[:16])
     e = lax.broadcasted_iota(jnp.int32, (16, SPAN), 0)
     beyond = ((lat == 0) & (e < HALO)) | ((lat == LAT - 1) & (e >= HALO + ROWS))
     for a in range(TAPS):
@@ -198,11 +241,10 @@
     return todo
 
 
-def chip_rows(own, own_row, part, out, sems, act):
-    low, high = slice(0, COLS), slice(COLS, CHIP)
+def chip_rows(own, part, out, sems, act):
     for core_is, row, pole in ((0, ROWS - HALO, LAT - 1), (1, 0, 0)):
-        mine, other = (low, high) if core_is == 0 else (high, low)
-        sources = ((own, row if own_row is None else own_row, mine), (part, row, other))
+        half0, half1 = (own, part) if core_is == 0 else (part, own)
+        sources = ((half0, row, slice(0, COLS)), (half1, row, slice(COLS, CHIP)))
         for turn in (False, True):
 
             @pl.when((my_core() == core_is) & ((my_lat() == pole) == turn))
@@ -211,19 +253,34 @@
 
 
 def rows_kernel(own, part, out, sems):
-    chip_rows(own, 0, part, out, sems, start_copy)
-    chip_rows(own, 0, part, out, sems, wait_copy)
+    for core_is, row in ((0, ROWS - HALO), (1, 0)):
+        low, high = slice(0, COLS), slice(COLS, CHIP)
+        mine, other = (low, high) if core_is == 0 else (high, low)
+
+        @pl.when(my_core() == core_is)
+        def _():
+            run(row_copies(((own, 0, mine), (part, row, other)), out, sems, False))
 
 
 def relay_kernel(a_own, e_own, c_own, u_rows, out, u_out, sems):
     del u_rows, u_out
-    run(
-        [
-            pltpu.make_async_copy(a_own, out.at[0:HALO], sems.at[0]),
-            pltpu.make_async_copy(e_own, out.at[HALO, 0:PACKED], sems.at[1]),
-            pltpu.make_async_copy(c_own, out.at[HALO, COLS : COLS + PACKED], sems.at[2]),
-        ]
-    )
+    core, lat = my_core(), my_lat()
+    turn = ((core == 0) & (lat == 0)) | ((core == 1) & (lat == LAT - 1))
+    todo = [
+        pltpu.make_async_copy(e_own, out.at[HALO, 0:PACKED], sems.at[0]),
+        pltpu.make_async_copy(c_own, out.at[HALO, COLS : COLS + PACKED], sems.at[1]),
+    ]
+    each(todo, start_copy)
+
+    @pl.when(turn)
+    def _():
+        run([pltpu.make_async_copy(a_own.at[HALO - 1 - m], out.at[m], sems.at[2 + m]) for m in range(HALO)])
+
+    @pl.when(jnp.logical_not(turn))
+    def _():
+        run([pltpu.make_async_copy(a_own, out.at[0:HALO], sems.at[2])])
+
+    each(todo, wait_copy)
 
 
 PACKED = 3 * EDGE
@@ -350,7 +407,7 @@
 
 def inner_kernel(f_own, f_part, u_own, u_part, band, acc, up_ref, pole_ref, u_rows, x, ud, sems, row_sems):
     core = my_core()
-    chip_rows(u_own, None, u_part, u_rows, row_sems, start_copy)
+    chip_rows(u_own, u_part, u_rows, row_sems, start_copy)
 
     def inputs(act):
         for core_is, (f0, f1, u0, u1) in enumerate(((f_own, f_part, u_own, u_part), (f_part, f_own, u_part, u_own))):
@@ -379,22 +436,28 @@
             to = slice(part * (TALL // 3), (part + 1) * (TALL // 3))
             acc[w, to] = jnp.dot(band[to], cells, preferred_element_type=F32)
     up_ref[...] = ud[...].reshape(2 * CELLS, HALF).T
-    chip_rows(u_own, None, u_part, u_rows, row_sems, wait_copy)
+    chip_rows(u_own, u_part, u_rows, row_sems, wait_copy)
 
 
 def outer_copies(x, rim, sems, passed0, passed1):
     todo = []
-    for n, (ref, at) in enumerate(((passed1, 0), (passed0, 0), (passed0, COLS), (passed1, COLS))):
-        todo.append(pltpu.make_async_copy(ref.at[HALO, at : at + 2 * EDGE], rim.at[n], sems.at[n]))
+    for n, ref in enumerate((passed0, passed1)):
+        todo.append(pltpu.make_async_copy(ref.at[HALO, COLS : COLS + 2 * EDGE], rim.at[n], sems.at[n]))
     low, high = slice(0, WIN - EDGE), slice(CHIP - WIN + EDGE, CHIP)
+    n = 2
     for side, rows in enumerate((passed0, passed1)):
-        n = 4 + 2 * side
-        todo.append(pltpu.make_async_copy(rows.at[0:HALO, low], x.at[side, 0, 1 : 1 + HALO, EDGE:WIN], sems.at[n]))
-        todo.append(pltpu.make_async_copy(rows.at[0:HALO, high], x.at[side, 1, 1 : 1 + HALO, 0 : WIN - EDGE], sems.at[n + 1]))
+        first, block, at = (0, HALO, 0) if side == 0 else (1, 0, WIN - 2 * EDGE)
+        to = slice(first, first + HALO)
+        todo.append(pltpu.make_async_copy(rows.at[0:HALO, low], x.at[side, 0, to, EDGE:WIN], sems.at[n]))
+        todo.append(pltpu.make_async_copy(rows.at[0:HALO, high], x.at[side, 1, to, 0 : WIN - EDGE], sems.at[n + 1]))
+        for w, ref in enumerate((passed1, passed0)):
+            columns = ref.at[HALO, 0 : 2 * EDGE]
+            todo.append(pltpu.make_async_copy(columns, x.at[side, w, block, at : at + 2 * EDGE], sems.at[n + 2 + w]))
+        n += 4
     return todo
 
 
-OUTER_SEMS = 8
+OUTER_SEMS = 10
 
 
 def grad_kernel(p_own, p_part, pole_ref, acc, band, up, g_ref, own_ref, x, rim, basis, g, sems):
@@ -408,35 +471,33 @@
                 each(outer_copies(x, rim, sems, *refs), act)
 
     inputs(start_copy)
+    for w in range(2):
+        x[0, w, HALO, 2 * EDGE :, :] = jnp.zeros((WIN - 2 * EDGE, CHANNELS), BF)
+        x[1, w, 0, : WIN - 2 * EDGE, :] = jnp.zeros((WIN - 2 * EDGE, CHANNELS), BF)
     inputs(wait_copy)
     for w, first in ((0, False), (1, True)):
-        for r in range(ROWS):
-            columns = spread_columns(rim[w], 0, r, first)
-            for side in range(2):
-                x[side, w, 0, r * EDGE : (r + 1) * EDGE, :] = columns
         at = w * (WIN - EDGE)
         for side, pole in ((0, 0), (1, LAT - 1)):
 
             @pl.when(lat != pole)
             def _():
                 for m in range(HALO):
-                    x[side, w, 1 + m, at : at + EDGE, :] = spread_columns(rim[2 + side], 0, m + (0 if first else HALO), first)
+                    x[side, w, side + m, at : at + EDGE, :] = spread_columns(rim[side], 0, m + (0 if first else HALO), first)
 
             @pl.when(lat == pole)
             def _():
                 for m in range(HALO):
-                    x[side, w, 1 + m, at : at + EDGE, :] = pole_ref[w, m]
-
-    for side in range(2):
-        to = slice(side * (TALL // 2), (side + 1) * (TALL // 2))
+                    x[side, w, side + m, at : at + EDGE, :] = pole_ref[w, m]
+
+    for i in range(ROWS):
+        to = slice(i * NBASIS * COLS, (i + 1) * NBASIS * COLS)
+        first, size = outer_rows(i)
         for w in range(2):
-            cells = x[side, w].reshape(OUTER, CHANNELS)
-            rows = (acc[w, to] + jnp.dot(band[w, to], cells, preferred_element_type=F32)).astype(BF)
-            for m in range(HALO):
-                at = w * CELLS + (side * HALO + m) * COLS
-                for k in range(NBASIS):
-                    n = (m * NBASIS + k) * COLS
-                    basis[k, at : at + COLS, :] = rows[n : n + COLS]
+            cells = x[i // HALO, w].reshape(OUTER, CHANNELS)[first : first + size]
+            rows = (acc[w, to] + jnp.dot(band[w, to, :size], cells, preferred_element_type=F32)).astype(BF)
+            at = w * CELLS + i * COLS
+            for k in range(NBASIS):
+                basis[k, at : at + COLS, :] = rows[k * COLS : (k + 1) * COLS]
     at = pl.multiple_of(core * CELLS, CELLS)
     own_copy = pltpu.make_async_copy(basis.at[:, pl.ds(at, CELLS)], own_ref, sems.at[4])
     own_copy.start()
@@ -520,15 +581,14 @@
     )(own_rows, f_part)
     af_own = send(rows, along_meridian)
     filt = jnp.transpose(filter_basis, (2, 3, 0, 1)).reshape(PLACES, NLAT)
-    inner_band, outer_band, vecs = pl.pallas_call(
+    inner_band, outer_band = pl.pallas_call(
         bands_kernel,
         out_shape=(
             jax.ShapeDtypeStruct((TALL, BAND), BF),
             jax.ShapeDtypeStruct((2, TALL, OUTER), BF),
-            jax.ShapeDtypeStruct((TAPS, 16, SPAN), F32),
         ),
         in_specs=[SMEM, VMEM],
-        out_specs=(VMEM, VMEM, VMEM),
+        out_specs=(VMEM, VMEM),
         compiler_params=params(16),
         cost_estimate=cost(2_000_000_000, 5_000_000),
         name="bands",
@@ -582,7 +642,7 @@
         in_specs=[ANY] * 4,
         out_specs=(ANY, ANY),
         input_output_aliases={3: 1},
-        scratch_shapes=[pltpu.SemaphoreType.DMA((3,))],
+        scratch_shapes=[pltpu.SemaphoreType.DMA((2 + HALO,))],
         compiler_params=params(4),
         cost_estimate=cost(1000, 4_000_000),
         name="relay",
@@ -599,7 +659,7 @@
         out_specs=(HBM, HBM),
         scratch_shapes=[
             pltpu.VMEM((2, 2, 1 + HALO, WIN, CHANNELS), BF),
-            pltpu.VMEM((4, 2 * EDGE, CHANNELS), BF),
+            pltpu.VMEM((2, 2 * EDGE, CHANNELS), BF),
             pltpu.VMEM((NBASIS, 2 * CELLS, CHANNELS), BF),
             pltpu.VMEM((NBASIS * CHANNELS, HALF), BF),
             pltpu.SemaphoreType.DMA((OUTER_SEMS,)),
@@ -630,6 +690,15 @@
         name="tie",
     )(au_own, in_hbm(convolved))
     au_part = send(au_own, to_partner)
+    vecs = pl.pallas_call(
+        spread_kernel,
+        out_shape=jax.ShapeDtypeStruct((TAPS, 16, SPAN), F32),
+        in_specs=[SMEM, VMEM, HBM],
+        out_specs=VMEM,
+        compiler_params=params(8),
+        cost_estimate=cost(1_000_000_000, 1_000_000),
+        name="spread",
+    )(info, filt, in_hbm(convolved))
     state_grad = pl.pallas_call(
         state_kernel,
         out_shape=jax.ShapeDtypeStruct((ROWS, COLS, CHANNELS), BF),

time: 75.9 us -> 75 us (0.988)
  Pallas kernels: 28 us -> 29.3 us
  waiting for transfers between devices: 18.9 us -> 18 us
    pallas_call x0 -> x1, Pallas kernels: none -> 1.23 us  [on_device(): pl.pallas_call(spread_kernel, out_shape=jax.ShapeDtypeStruct((TAPS, 16, S...]
    ppermute x8, waiting for transfers between devices: 7.3 us -> 6.32 us  [send(): return lax.ppermute(block, BOTH, pairs)]
  transfers between devices with their start and end apart: 9 -> 9, of which waited for: 6 -> 6; matrix products, arithmetic and copies ran while one was open for 2% -> 2% of each run, Pallas kernels for 35% -> 37%
where the time goes in v5:
time: 75 us; the launch traced here: 74.6 us
  Pallas kernels  29.3 us (39%)
  starting transfers between devices  18.8 us (25%)
  waiting for transfers between devices  18 us (24%)
  local copies, waits for them, and re-layouts  6.45 us (9%)
  other arithmetic  1.16 us (2%)
  between operations  0.93 us (1%)
    all_to_all x1, waiting for transfers between devices, on_device(): lax.all_to_all(partial.reshape(LAT * LON, OWNED, HALF), BOTH, 0, 0, tiled...  11.7 us
    all_to_all x1, starting transfers between devices, on_device(): lax.all_to_all(partial.reshape(LAT * LON, OWNED, HALF), BOTH, 0, 0, tiled...  11.4 us
    pallas_call x1, Pallas kernels, on_device(): pl.pallas_call(state_kernel, out_shape=jax.ShapeDtypeStruct((ROWS, COLS,...  9.95 us
    ppermute x8, starting transfers between devices, send(): return lax.ppermute(block, BOTH, pairs)  7.41 us
    unnamed x34, local copies, waits for them, and re-layouts  6.39 us
    ppermute x8, waiting for transfers between devices, send(): return lax.ppermute(block, BOTH, pairs)  6.32 us
    pallas_call x1, Pallas kernels, on_device(): pl.pallas_call(grad_kernel, out_shape=(pltpu.HBM((NBASIS * CHANNELS, HALF...  5.56 us
    pallas_call x1, Pallas kernels, on_device(): pl.pallas_call(inner_kernel, out_shape=(jax.ShapeDtypeStruct((2, TALL, CH...  4.2 us
  transfers between devices with their start and end apart: 9, of which 6 were waited for; matrix products, arithmetic and copies ran while one was open for 2% of the time, Pallas kernels for 37%

profile of v5, /device:TPU:0, one launch (start us, length us, event | category | flops | bytes accessed | tf_op | source)
XLA Modules:
  0.0 74.6 jit_solution(18208348593922774547)
XLA Ops:
  0.6 0.0 copy-start.14
  0.6 0.0 copy-start.15
  0.7 0.0 copy-start.16
  0.7 0.0 copy-start.13
  0.7 0.1 collective-permute-start
  0.8 0.5 collective-permute-start.2
  1.3 1.1 %slice_select_fusion.own = bf16[3,64,768]{2,1,0:T(8,128)(2,1)S(1)} fusion(bf16[6,64,768]{2,1,0:T(8,128)(2,1)} %f_own.3, pred[]{:T(512)S(6)} %eq.3), kind=kLoop, calls=%fused_computation | loop fusion | flops 147456 | bytes 884737 | tf_op jit(solution)/shard_map/jit(_where)/select_n | solution.py:571
  2.3 0.6 collective-permute-done.part.f_part
  3.0 0.1 rows.1
  3.1 1.6 %collective-permute-start.1 = (bf16[3,128,768]{2,1,0:T(8,128)(2,1)S(1)}, bf16[3,128,768]{2,1,0:T(8,128)(2,1)S(1)}, u32[]{:S(2)}, u32[]{:S(2)}) collective-permute-start(bf16[3,128,768]{2,1,0:T(8,128)(2,1)S(1)} %rows.1), channel_id=1, source_target_pairs={{0,4},{1,2},{2,6},{3,0},{4,8},{5,1},{6,10},{7,3},{8,12},{9,5},{10,... | collective-permute-start | bytes 1769480 | tf_op jit(solution)/shard_map/ppermute | solution.py:60
  4.7 0.0 copy-done.14
  4.7 0.0 copy-done.15
  4.7 0.0 copy-done.16
  4.7 0.1 pad_add_fusion.info
  4.8 0.0 copy-done.13
  4.8 0.1 reshape.15.filt
  4.9 0.0 copy-start.4
  4.9 0.0 copy-start
  4.9 0.0 copy-start.1
  4.9 3.1 %bands.1 = (bf16[1536,768]{1,0:T(8,128)(2,1)S(1)}, bf16[2,1536,384]{2,1,0:T(8,128)(2,1)S(1)}) custom-call(s32[576]{0:T(1024)S(1)} %pad_add_fusion.info, bf16[196,192]{1,0:T(8,128)(2,1)S(1)} %reshape.15.filt), custom_call_target="tpu_custom_call" | custom-call | flops 2000000000 | bytes 5000000 | tf_op jit(solution)/shard_map/bands/pallas_call | solution.py:584
  8.0 0.0 copy-done.4
  8.0 0.0 collective-permute-done.2.u_part
  8.0 0.0 copy-done
  8.0 0.0 copy-done.1
  8.0 0.0 copy-start.2
  8.1 0.4 edges.1
  8.4 1.7 %collective-permute-start.3 = (bf16[48,768]{1,0:T(8,128)(2,1)S(1)}, bf16[48,768]{1,0:T(8,128)(2,1)S(1)}, u32[]{:S(2)}, u32[]{:S(2)}) collective-permute-start(bf16[48,768]{1,0:T(8,128)(2,1)S(1)} %get-tuple-element.15), channel_id=1, source_target_pairs={{0,2},{1,3},{2,0},{3,1},{4,6},{5,7},{6,4},{7,5},{8,10},{9,11},{10,... | collective-permute-start | bytes 221192 | tf_op jit(solution)/shard_map/ppermute | solution.py:60
  10.1 3.3 %collective-permute-start.4 = (bf16[48,768]{1,0:T(8,128)(2,1)S(1)}, bf16[48,768]{1,0:T(8,128)(2,1)S(1)}, u32[]{:S(2)}, u32[]{:S(2)}) collective-permute-start(bf16[48,768]{1,0:T(8,128)(2,1)S(1)} %get-tuple-element.16), channel_id=1, source_target_pairs={{0,6},{2,4},{4,10},{5,3},{6,8},{7,1},{8,14},{9,7},{10,12},{11,5},{... | collective-permute-start | bytes 221192 | tf_op jit(solution)/shard_map/ppermute | solution.py:60
  13.4 4.2 %inner.1 = (f32[2,1536,768]{2,1,0:T(8,128)S(1)}, bf16[384,768]{1,0:T(8,128)(2,1)S(1)}, bf16[2,3,16,768]{3,2,1,0:T(8,128)(2,1)S(1)}, bf16[3,128,768]{2,1,0:T(8,128)(2,1)}) custom-call(bf16[6,64,768]{2,1,0:T(8,128)(2,1)S(1)} %copy-done, bf16[6,64,768]{2,1,0:T(8,128)(2,1)S(1)} %collective-permute-done.part.f_part, bf16[6,64,768]{2,1,0:T(8,128)(2,1)S(1)} %copy-done.1, ...), custom_call_target="tpu_custom_call" | custom-call | flops 4000000000 | bytes 16000000 | tf_op jit(solution)/shard_map/inner/pallas_call | solution.py:616
  17.6 0.0 copy-done.2
  17.6 2.0 %collective-permute-done.3.e_own = bf16[48,768]{1,0:T(8,128)(2,1)S(1)} collective-permute-done((bf16[48,768]{1,0:T(8,128)(2,1)S(1)}, bf16[48,768]{1,0:T(8,128)(2,1)S(1)}, u32[]{:S(2)}, u32[]{:S(2)}) %collective-permute-start.3) | collective-permute-done | bytes 73760 | tf_op jit(solution)/shard_map/ppermute | solution.py:60
  19.6 0.0 collective-permute-done.4.c_own
  19.6 0.8 %collective-permute-done.1.a_own = bf16[3,128,768]{2,1,0:T(8,128)(2,1)S(1)} collective-permute-done((bf16[3,128,768]{2,1,0:T(8,128)(2,1)S(1)}, bf16[3,128,768]{2,1,0:T(8,128)(2,1)S(1)}, u32[]{:S(2)}, u32[]{:S(2)}) %collective-permute-start.1) | collective-permute-done | bytes 589856 | tf_op jit(solution)/shard_map/ppermute | solution.py:60
  20.4 1.0 %relay.1 = (bf16[4,128,768]{2,1,0:T(8,128)(2,1)S(1)}, bf16[3,128,768]{2,1,0:T(8,128)(2,1)}) custom-call(bf16[3,128,768]{2,1,0:T(8,128)(2,1)S(1)} %collective-permute-done.1.a_own, bf16[48,768]{1,0:T(8,128)(2,1)S(1)} %collective-permute-done.3.e_own, bf16[48,768]{1,0:T(8,128)(2,1)S(1)} %collective-permute-done.4.c_own, ...), custom_call_target="tpu_custom_call", output_to_operand_aliasing={{1}: (3, {})} | custom-call | flops 1000 | bytes 4000000 | tf_op jit(solution)/shard_map/relay/pallas_call | solution.py:636
  21.3 0.0 copy-start.8
  21.3 0.1 collective-permute-start.5
  21.4 0.1 collective-permute-start.6
  21.5 2.2 %collective-permute-done.5.p_part = bf16[4,128,768]{2,1,0:T(8,128)(2,1)S(1)} collective-permute-done((bf16[4,128,768]{2,1,0:T(8,128)(2,1)S(1)}, bf16[4,128,768]{2,1,0:T(8,128)(2,1)S(1)}, u32[]{:S(2)}, u32[]{:S(2)}) %collective-permute-start.5) | collective-permute-done | bytes 786464 | tf_op jit(solution)/shard_map/ppermute | solution.py:60
  23.7 0.0 copy-start.10
  23.7 5.6 %grad.1 = (bf16[3072,384]{1,0:T(8,128)(2,1)}, bf16[4,384,768]{2,1,0:T(8,128)(2,1)}) custom-call(bf16[4,128,768]{2,1,0:T(8,128)(2,1)S(1)} %get-tuple-element.19.p_own, bf16[4,128,768]{2,1,0:T(8,128)(2,1)S(1)} %collective-permute-done.5.p_part, bf16[2,3,16,768]{3,2,1,0:T(8,128)(2,1)S(1)} %get-tuple-element.20.pole_ref, ...), custom_call_target="tpu_custom_call" | custom-call | flops 6000000000 | bytes 12000000 | tf_op jit(solution)/shard_map/grad/pallas_call | solution.py:652
  29.3 0.0 copy-done.8
  29.3 0.0 copy-done.10
  29.3 11.4 %all-to-all-start = ((bf16[128,24,384]{2,1,0:T(8,128)(2,1)}), bf16[128,24,384]{2,1,0:T(8,128)(2,1)S(1)}, u32[]{:S(2)}, u32[]{:S(2)}) async-start(bf16[128,24,384]{2,1,0:T(8,128)(2,1)} %bitcast.4), calls=%async_computation | async-start | bytes 4718592 | tf_op jit(solution)/shard_map/all_to_all | solution.py:672
  40.7 0.0 copy-start.6
  40.7 2.3 %copy-done.6 = bf16[3072,768]{1,0:T(8,128)(2,1)S(1)} copy-done((bf16[3072,768]{1,0:T(8,128)(2,1)S(1)}, bf16[3072,768]{1,0:T(8,128)(2,1)}, u32[]{:S(2)}) %copy-start.6) | copy-done | bytes 4718616
  43.0 0.0 copy-start.12
  43.0 1.7 %copy-done.12 = bf16[4,384,768]{2,1,0:T(8,128)(2,1)S(1)} copy-done((bf16[4,384,768]{2,1,0:T(8,128)(2,1)S(1)}, bf16[4,384,768]{2,1,0:T(8,128)(2,1)}, u32[]{:S(2)}) %copy-start.12) | copy-done | bytes 2359320
  44.7 0.0 copy-start.5
  44.7 2.8 %conv.1.after = bf16[6,64,768]{2,1,0:T(8,128)(2,1)} custom-call(bf16[4,384,768]{2,1,0:T(8,128)(2,1)S(1)} %copy-done.12, bf16[3072,768]{1,0:T(8,128)(2,1)S(1)} %copy-done.6), custom_call_target="tpu_custom_call" | custom-call | flops 80000000000 | bytes 8000000 | tf_op jit(solution)/shard_map/conv/pallas_call | solution.py:674
  47.5 0.0 copy-start.3
  47.5 0.0 copy-start.9
  47.5 0.0 collective-permute-done.6.rows
  47.5 0.1 collective-permute-start.7
  47.6 0.0 copy-done.5
  47.6 1.2 %spread.1.vec_ref = f32[7,16,384]{2,1,0:T(8,128)S(1)} custom-call(s32[576]{0:T(1024)S(1)} %pad_add_fusion.info, bf16[196,192]{1,0:T(8,128)(2,1)S(1)} %copy-done.5, bf16[6,64,768]{2,1,0:T(8,128)(2,1)} %conv.1.after), custom_call_target="tpu_custom_call" | custom-call | flops 1000000000 | bytes 1000000 | tf_op jit(solution)/shard_map/spread/pallas_call | solution.py:693
  48.9 0.7 collective-permute-done.7.a_part
  49.6 0.0 copy-done.3
  49.6 0.0 copy-done.9
  49.6 0.0 copy-done.11
  49.6 0.0 copy-start.7
  49.6 2.3 %copy-done.7 = bf16[3072,768]{1,0:T(8,128)(2,1)S(1)} copy-done((bf16[3072,768]{1,0:T(8,128)(2,1)S(1)}, bf16[3072,768]{1,0:T(8,128)(2,1)}, u32[]{:S(2)}) %copy-start.7) | copy-done | bytes 4718616
  52.0 10.0 %state.1 = bf16[6,64,768]{2,1,0:T(8,128)(2,1)} custom-call(bf16[3072,768]{1,0:T(8,128)(2,1)S(1)} %copy-done.7, f32[7,16,384]{2,1,0:T(8,128)S(1)} %spread.1.vec_ref, bf16[6,64,768]{2,1,0:T(8,128)(2,1)S(1)} %copy-done.1, bf16[6,64,768]{2,1,0:T(8,128)(2,1)S(1)} %copy-done.3, bf16[4,128,768]{2,1,0:T(8,128)(2,1)S(1)} %copy-done.9, ...), custom_call_target="tpu_custom_call" | custom-call | flops 8000000000 | bytes 12000000 | tf_op jit(solution)/shard_map/state/pallas_call | solution.py:702
  61.9 11.7 %all-to-all-done = bf16[128,24,384]{2,1,0:T(8,128)(2,1)S(1)} async-done(((bf16[128,24,384]{2,1,0:T(8,128)(2,1)}), bf16[128,24,384]{2,1,0:T(8,128)(2,1)S(1)}, u32[]{:S(2)}, u32[]{:S(2)}) %all-to-all-start) | async-done | bytes 2359328 | tf_op jit(solution)/shard_map/all_to_all | solution.py:672
  73.6 1.0 %total.1 = f32[24,768]{1,0:T(8,128)} custom-call(bf16[64,2,24,384]{3,2,1,0:T(8,128)(2,1)S(1)} %bitcast.3), custom_call_target="tpu_custom_call" | custom-call | tf_op jit(solution)/shard_map/total/pallas_call | solution.py:719
  (2 shorter events, 0.0 us)
Async XLA Ops:
  0.6 4.1 %copy-start.14 = (s32[192]{0:T(256)S(1)}, s32[192]{0:T(256)}, u32[]{:S(2)}) copy-start(s32[192]{0:T(256)} %param.13) | copy-start | bytes 2308
  0.6 4.1 %copy-start.15 = (s32[192]{0:T(256)S(1)}, s32[192]{0:T(256)}, u32[]{:S(2)}) copy-start(s32[192]{0:T(256)} %param.12) | copy-start | bytes 2308
  0.7 4.1 %copy-start.16 = (s32[192]{0:T(256)S(1)}, s32[192]{0:T(256)}, u32[]{:S(2)}) copy-start(s32[192]{0:T(256)} %param.11) | copy-start | bytes 2308
  0.7 4.1 %copy-start.13 = (bf16[4,192,7,7]{1,0,3,2:T(4,128)(2,1)S(1)}, bf16[4,192,7,7]{1,0,3,2:T(4,128)(2,1)}, u32[]{:S(2)}) copy-start(bf16[4,192,7,7]{1,0,3,2:T(4,128)(2,1)} %param.10) | copy-start | bytes 225796
  0.7 2.3 %collective-permute-start = (bf16[6,64,768]{2,1,0:T(8,128)(2,1)}, bf16[6,64,768]{2,1,0:T(8,128)(2,1)S(1)}, u32[]{:S(2)}, u32[]{:S(2)}) collective-permute-start(bf16[6,64,768]{2,1,0:T(8,128)(2,1)} %f_own.3), channel_id=1, source_target_pairs={{0,1},{1,0},{2,3},{3,2},{4,5},{5,4},{6,7},{7,6},{8,9},{9,8},{10,11... | collective-permute-start | bytes 1769480 | tf_op jit(solution)/shard_map/ppermute | solution.py:60
  0.8 7.2 %collective-permute-start.2 = (bf16[6,64,768]{2,1,0:T(8,128)(2,1)}, bf16[6,64,768]{2,1,0:T(8,128)(2,1)S(1)}, u32[]{:S(2)}, u32[]{:S(2)}) collective-permute-start(bf16[6,64,768]{2,1,0:T(8,128)(2,1)} %u_own.5), channel_id=1, source_target_pairs={{0,1},{1,0},{2,3},{3,2},{4,5},{5,4},{6,7},{7,6},{8,9},{9,8},{10,11... | collective-permute-start | bytes 1769480 | tf_op jit(solution)/shard_map/ppermute | solution.py:60
  3.1 17.3 %collective-permute-start.1 = (bf16[3,128,768]{2,1,0:T(8,128)(2,1)S(1)}, bf16[3,128,768]{2,1,0:T(8,128)(2,1)S(1)}, u32[]{:S(2)}, u32[]{:S(2)}) collective-permute-start(bf16[3,128,768]{2,1,0:T(8,128)(2,1)S(1)} %rows.1), channel_id=1, source_target_pairs={{0,4},{1,2},{2,6},{3,0},{4,8},{5,1},{6,10},{7,3},{8,12},{9,5},{10,... | collective-permute-start | bytes 1769480 | tf_op jit(solution)/shard_map/ppermute | solution.py:60
  4.9 3.1 %copy-start.4 = (bf16[196,192]{1,0:T(8,128)(2,1)}, bf16[196,192]{1,0:T(8,128)(2,1)S(1)}, u32[]{:S(2)}) copy-start(bf16[196,192]{1,0:T(8,128)(2,1)S(1)} %reshape.15.filt) | copy-start | bytes 225796
  4.9 3.1 %copy-start = (bf16[6,64,768]{2,1,0:T(8,128)(2,1)S(1)}, bf16[6,64,768]{2,1,0:T(8,128)(2,1)}, u32[]{:S(2)}) copy-start(bf16[6,64,768]{2,1,0:T(8,128)(2,1)} %f_own.3) | copy-start | bytes 1769476
  4.9 3.1 %copy-start.1 = (bf16[6,64,768]{2,1,0:T(8,128)(2,1)S(1)}, bf16[6,64,768]{2,1,0:T(8,128)(2,1)}, u32[]{:S(2)}) copy-start(bf16[6,64,768]{2,1,0:T(8,128)(2,1)} %u_own.5) | copy-start | bytes 1769476
  8.0 9.5 %copy-start.2 = (bf16[6,64,768]{2,1,0:T(8,128)(2,1)}, bf16[6,64,768]{2,1,0:T(8,128)(2,1)S(1)}, u32[]{:S(2)}) copy-start(bf16[6,64,768]{2,1,0:T(8,128)(2,1)S(1)} %collective-permute-done.2.u_part) | copy-start | bytes 1769476
  8.4 11.2 %collective-permute-start.3 = (bf16[48,768]{1,0:T(8,128)(2,1)S(1)}, bf16[48,768]{1,0:T(8,128)(2,1)S(1)}, u32[]{:S(2)}, u32[]{:S(2)}) collective-permute-start(bf16[48,768]{1,0:T(8,128)(2,1)S(1)} %get-tuple-element.15), channel_id=1, source_target_pairs={{0,2},{1,3},{2,0},{3,1},{4,6},{5,7},{6,4},{7,5},{8,10},{9,11},{10,... | collective-permute-start | bytes 221192 | tf_op jit(solution)/shard_map/ppermute | solution.py:60
  10.1 9.5 %collective-permute-start.4 = (bf16[48,768]{1,0:T(8,128)(2,1)S(1)}, bf16[48,768]{1,0:T(8,128)(2,1)S(1)}, u32[]{:S(2)}, u32[]{:S(2)}) collective-permute-start(bf16[48,768]{1,0:T(8,128)(2,1)S(1)} %get-tuple-element.16), channel_id=1, source_target_pairs={{0,6},{2,4},{4,10},{5,3},{6,8},{7,1},{8,14},{9,7},{10,12},{11,5},{... | collective-permute-start | bytes 221192 | tf_op jit(solution)/shard_map/ppermute | solution.py:60
  21.3 7.9 %copy-start.8 = (bf16[4,128,768]{2,1,0:T(8,128)(2,1)}, bf16[4,128,768]{2,1,0:T(8,128)(2,1)S(1)}, u32[]{:S(2)}) copy-start(bf16[4,128,768]{2,1,0:T(8,128)(2,1)S(1)} %get-tuple-element.19.p_own) | copy-start | bytes 2359300
  21.3 2.4 %collective-permute-start.5 = (bf16[4,128,768]{2,1,0:T(8,128)(2,1)S(1)}, bf16[4,128,768]{2,1,0:T(8,128)(2,1)S(1)}, u32[]{:S(2)}, u32[]{:S(2)}) collective-permute-start(bf16[4,128,768]{2,1,0:T(8,128)(2,1)S(1)} %get-tuple-element.19.p_own), channel_id=1, source_target_pairs={{0,1},{1,0},{2,3},{3,2},{4,5},{5,4},{6,7},{7,6},{8,9},{9,8},{10,11... | collective-permute-start | bytes 2359304 | tf_op jit(solution)/shard_map/ppermute | solution.py:60
  21.4 26.1 %collective-permute-start.6 = (bf16[3,128,768]{2,1,0:T(8,128)(2,1)}, bf16[3,128,768]{2,1,0:T(8,128)(2,1)S(1)}, u32[]{:S(2)}, u32[]{:S(2)}) collective-permute-start(bf16[3,128,768]{2,1,0:T(8,128)(2,1)} %get-tuple-element.25), channel_id=1, source_target_pairs={{0,4},{1,2},{2,6},{3,0},{4,8},{5,1},{6,10},{7,3},{8,12},{9,5},{10,... | collective-permute-start | bytes 1769480 | tf_op jit(solution)/shard_map/ppermute | solution.py:60
  23.7 5.6 %copy-start.10 = (bf16[4,128,768]{2,1,0:T(8,128)(2,1)}, bf16[4,128,768]{2,1,0:T(8,128)(2,1)S(1)}, u32[]{:S(2)}) copy-start(bf16[4,128,768]{2,1,0:T(8,128)(2,1)S(1)} %collective-permute-done.5.p_part) | copy-start | bytes 2359300
  29.3 44.3 %all-to-all-start = ((bf16[128,24,384]{2,1,0:T(8,128)(2,1)}), bf16[128,24,384]{2,1,0:T(8,128)(2,1)S(1)}, u32[]{:S(2)}, u32[]{:S(2)}) async-start(bf16[128,24,384]{2,1,0:T(8,128)(2,1)} %bitcast.4), calls=%async_computation | async-start | bytes 4718592 | tf_op jit(solution)/shard_map/all_to_all | solution.py:672
  40.7 2.3 %copy-start.6 = (bf16[3072,768]{1,0:T(8,128)(2,1)S(1)}, bf16[3072,768]{1,0:T(8,128)(2,1)}, u32[]{:S(2)}) copy-start(bf16[3072,768]{1,0:T(8,128)(2,1)} %w_ref.3) | copy-start | bytes 14155780
  43.0 1.7 %copy-start.12 = (bf16[4,384,768]{2,1,0:T(8,128)(2,1)S(1)}, bf16[4,384,768]{2,1,0:T(8,128)(2,1)}, u32[]{:S(2)}) copy-start(bf16[4,384,768]{2,1,0:T(8,128)(2,1)} %get-tuple-element.24.own_ref) | copy-start | bytes 7077892
  44.7 2.9 %copy-start.5 = (bf16[196,192]{1,0:T(8,128)(2,1)S(1)}, bf16[196,192]{1,0:T(8,128)(2,1)}, u32[]{:S(2)}) copy-start(bf16[196,192]{1,0:T(8,128)(2,1)} %copy-done.4) | copy-start | bytes 225796
  47.5 2.1 %copy-start.3 = (bf16[6,64,768]{2,1,0:T(8,128)(2,1)S(1)}, bf16[6,64,768]{2,1,0:T(8,128)(2,1)}, u32[]{:S(2)}) copy-start(bf16[6,64,768]{2,1,0:T(8,128)(2,1)} %copy-done.2) | copy-start | bytes 1769476
  47.5 2.1 %copy-start.9 = (bf16[4,128,768]{2,1,0:T(8,128)(2,1)S(1)}, bf16[4,128,768]{2,1,0:T(8,128)(2,1)}, u32[]{:S(2)}) copy-start(bf16[4,128,768]{2,1,0:T(8,128)(2,1)} %copy-done.8) | copy-start | bytes 2359300
  47.5 2.1 %copy-start.11 = (bf16[4,128,768]{2,1,0:T(8,128)(2,1)S(1)}, bf16[4,128,768]{2,1,0:T(8,128)(2,1)}, u32[]{:S(2)}) copy-start(bf16[4,128,768]{2,1,0:T(8,128)(2,1)} %copy-done.10) | copy-start | bytes 2359300
  47.5 2.1 %collective-permute-start.7 = (bf16[3,128,768]{2,1,0:T(8,128)(2,1)S(1)}, bf16[3,128,768]{2,1,0:T(8,128)(2,1)S(1)}, u32[]{:S(2)}, u32[]{:S(2)}) collective-permute-start(bf16[3,128,768]{2,1,0:T(8,128)(2,1)S(1)} %tie.1.a_own), channel_id=1, source_target_pairs={{0,1},{1,0},{2,3},{3,2},{4,5},{5,4},{6,7},{7,6},{8,9},{9,8},{10,11... | collective-permute-start | bytes 1769480 | tf_op jit(solution)/shard_map/ppermute | solution.py:60
  49.6 2.3 %copy-start.7 = (bf16[3072,768]{1,0:T(8,128)(2,1)S(1)}, bf16[3072,768]{1,0:T(8,128)(2,1)}, u32[]{:S(2)}) copy-start(bf16[3072,768]{1,0:T(8,128)(2,1)} %w_ref.3) | copy-start | bytes 14155780

commit v6 on v5

--- a/solution.py
+++ b/solution.py
@@ -262,25 +262,21 @@
             run(row_copies(((own, 0, mine), (part, row, other)), out, sems, False))
 
 
-def relay_kernel(a_own, e_own, c_own, u_rows, out, u_out, sems):
+def relay_kernel(a_own, e_own, c_own, u_rows, out, u_out):
     del u_rows, u_out
     core, lat = my_core(), my_lat()
     turn = ((core == 0) & (lat == 0)) | ((core == 1) & (lat == LAT - 1))
-    todo = [
-        pltpu.make_async_copy(e_own, out.at[HALO, 0:PACKED], sems.at[0]),
-        pltpu.make_async_copy(c_own, out.at[HALO, COLS : COLS + PACKED], sems.at[1]),
-    ]
-    each(todo, start_copy)
+    out[HALO, 0:PACKED] = e_own[...]
+    out[HALO, COLS : COLS + PACKED] = c_own[...]
 
     @pl.when(turn)
     def _():
-        run([pltpu.make_async_copy(a_own.at[HALO - 1 - m], out.at[m], sems.at[2 + m]) for m in range(HALO)])
+        for m in range(HALO):
+            out[m] = a_own[HALO - 1 - m]
 
     @pl.when(jnp.logical_not(turn))
     def _():
-        run([pltpu.make_async_copy(a_own, out.at[0:HALO], sems.at[2])])
-
-    each(todo, wait_copy)
+        out[0:HALO] = a_own[...]
 
 
 PACKED = 3 * EDGE
@@ -439,55 +435,44 @@
     chip_rows(u_own, u_part, u_rows, row_sems, wait_copy)
 
 
-def outer_copies(x, rim, sems, passed0, passed1):
-    todo = []
-    for n, ref in enumerate((passed0, passed1)):
-        todo.append(pltpu.make_async_copy(ref.at[HALO, COLS : COLS + 2 * EDGE], rim.at[n], sems.at[n]))
+def fill_outer(x, passed0, passed1, pole_ref):
+    lat = my_lat()
     low, high = slice(0, WIN - EDGE), slice(CHIP - WIN + EDGE, CHIP)
-    n = 2
-    for side, rows in enumerate((passed0, passed1)):
-        first, block, at = (0, HALO, 0) if side == 0 else (1, 0, WIN - 2 * EDGE)
-        to = slice(first, first + HALO)
-        todo.append(pltpu.make_async_copy(rows.at[0:HALO, low], x.at[side, 0, to, EDGE:WIN], sems.at[n]))
-        todo.append(pltpu.make_async_copy(rows.at[0:HALO, high], x.at[side, 1, to, 0 : WIN - EDGE], sems.at[n + 1]))
-        for w, ref in enumerate((passed1, passed0)):
-            columns = ref.at[HALO, 0 : 2 * EDGE]
-            todo.append(pltpu.make_async_copy(columns, x.at[side, w, block, at : at + 2 * EDGE], sems.at[n + 2 + w]))
-        n += 4
-    return todo
-
-
-OUTER_SEMS = 10
-
-
-def grad_kernel(p_own, p_part, pole_ref, acc, band, up, g_ref, own_ref, x, rim, basis, g, sems):
-    core, lat = my_core(), my_lat()
-
-    def inputs(act):
-        for core_is, refs in enumerate(((p_own, p_part), (p_part, p_own))):
-
-            @pl.when(core == core_is)
-            def _():
-                each(outer_copies(x, rim, sems, *refs), act)
-
-    inputs(start_copy)
-    for w in range(2):
-        x[0, w, HALO, 2 * EDGE :, :] = jnp.zeros((WIN - 2 * EDGE, CHANNELS), BF)
-        x[1, w, 0, : WIN - 2 * EDGE, :] = jnp.zeros((WIN - 2 * EDGE, CHANNELS), BF)
-    inputs(wait_copy)
-    for w, first in ((0, False), (1, True)):
-        at = w * (WIN - EDGE)
-        for side, pole in ((0, 0), (1, LAT - 1)):
-
-            @pl.when(lat != pole)
-            def _():
+    for side, (rows, pole) in enumerate(((passed0, 0), (passed1, LAT - 1))):
+        block, at, none = (HALO, 0, slice(2 * EDGE, WIN)) if side == 0 else (0, WIN - 2 * EDGE, slice(0, WIN - 2 * EDGE))
+        for w, edges in enumerate((passed1, passed0)):
+            x[side, w, block, none, :] = jnp.zeros((WIN - 2 * EDGE, CHANNELS), BF)
+            x[side, w, block, at : at + 2 * EDGE, :] = edges[HALO, 0 : 2 * EDGE]
+            to = slice(EDGE, WIN) if w == 0 else slice(0, WIN - EDGE)
+            for m in range(HALO):
+                x[side, w, side + m, to, :] = rows[m, low if w == 0 else high]
+        corners = rows.at[HALO, COLS : COLS + 2 * EDGE]
+
+        @pl.when(lat != pole)
+        def _():
+            for w in range(2):
+                at = w * (WIN - EDGE)
                 for m in range(HALO):
-                    x[side, w, side + m, at : at + EDGE, :] = spread_columns(rim[side], 0, m + (0 if first else HALO), first)
-
-            @pl.when(lat == pole)
-            def _():
+                    x[side, w, side + m, at : at + EDGE, :] = spread_columns(corners, 0, m + (HALO if w == 0 else 0), w == 1)
+
+        @pl.when(lat == pole)
+        def _():
+            for w in range(2):
+                at = w * (WIN - EDGE)
                 for m in range(HALO):
                     x[side, w, side + m, at : at + EDGE, :] = pole_ref[w, m]
+
+
+def grad_kernel(p_own, p_part, pole_ref, acc, band, up, g_ref, own_ref, x, basis, g, sems):
+    core = my_core()
+
+    @pl.when(core == 0)
+    def _():
+        fill_outer(x, p_own, p_part, pole_ref)
+
+    @pl.when(core == 1)
+    def _():
+        fill_outer(x, p_part, p_own, pole_ref)
 
     for i in range(ROWS):
         to = slice(i * NBASIS * COLS, (i + 1) * NBASIS * COLS)
@@ -639,11 +624,10 @@
             jax.ShapeDtypeStruct((HALO + 1, CHIP, CHANNELS), BF),
             jax.ShapeDtypeStruct((HALO, CHIP, CHANNELS), BF),
         ),
-        in_specs=[ANY] * 4,
-        out_specs=(ANY, ANY),
+        in_specs=[VMEM] * 3 + [ANY],
+        out_specs=(VMEM, ANY),
         input_output_aliases={3: 1},
-        scratch_shapes=[pltpu.SemaphoreType.DMA((2 + HALO,))],
-        compiler_params=params(4),
+        compiler_params=params(8),
         cost_estimate=cost(1000, 4_000_000),
         name="relay",
     )(af_own, e_own, c_own, u_rows)
@@ -655,14 +639,13 @@
             pltpu.HBM((NBASIS * CHANNELS, HALF), BF),
             pltpu.HBM((NBASIS, CELLS, CHANNELS), BF),
         ),
-        in_specs=[ANY] * 2 + [VMEM] * 4,
+        in_specs=[VMEM] * 6,
         out_specs=(HBM, HBM),
         scratch_shapes=[
             pltpu.VMEM((2, 2, 1 + HALO, WIN, CHANNELS), BF),
-            pltpu.VMEM((2, 2 * EDGE, CHANNELS), BF),
             pltpu.VMEM((NBASIS, 2 * CELLS, CHANNELS), BF),
             pltpu.VMEM((NBASIS * CHANNELS, HALF), BF),
-            pltpu.SemaphoreType.DMA((OUTER_SEMS,)),
+            pltpu.SemaphoreType.DMA((5,)),
         ],
         compiler_params=params(30),
         cost_estimate=cost(6_000_000_000, 12_000_000),

time: 75 us -> 74.2 us (0.989)
  Pallas kernels: 29.3 us -> 27.8 us
  starting transfers between devices: 18.8 us -> 19.7 us
    pallas_call x1, Pallas kernels: 0.97 us -> 0.05 us  [on_device(): pl.pallas_call(relay_kernel, out_shape=(jax.ShapeDtypeStruct((HALO + 1, C...]
  transfers between devices with their start and end apart: 9 -> 9, of which waited for: 6 -> 6; matrix products, arithmetic and copies ran while one was open for 2% -> 2% of each run, Pallas kernels for 37% -> 36%
where the time goes in v6:
time: 74.2 us; the launch traced here: 73.8 us
  Pallas kernels  27.8 us (37%)
  starting transfers between devices  19.7 us (27%)
  waiting for transfers between devices  17.7 us (24%)
  local copies, waits for them, and re-layouts  6.45 us (9%)
  other arithmetic  1.16 us (2%)
  between operations  0.92 us (1%)
    all_to_all x1, starting transfers between devices, on_device(): lax.all_to_all(partial.reshape(LAT * LON, OWNED, HALF), BOTH, 0, 0, tiled...  11.8 us
    all_to_all x1, waiting for transfers between devices, on_device(): lax.all_to_all(partial.reshape(LAT * LON, OWNED, HALF), BOTH, 0, 0, tiled...  11.7 us
    pallas_call x1, Pallas kernels, on_device(): pl.pallas_call(state_kernel, out_shape=jax.ShapeDtypeStruct((ROWS, COLS,...  9.96 us
    ppermute x8, starting transfers between devices, send(): return lax.ppermute(block, BOTH, pairs)  7.95 us
    unnamed x34, local copies, waits for them, and re-layouts  6.39 us
    ppermute x8, waiting for transfers between devices, send(): return lax.ppermute(block, BOTH, pairs)  6.05 us
    pallas_call x1, Pallas kernels, on_device(): pl.pallas_call(grad_kernel, out_shape=(pltpu.HBM((NBASIS * CHANNELS, HALF...  5 us
    pallas_call x1, Pallas kernels, on_device(): pl.pallas_call(inner_kernel, out_shape=(jax.ShapeDtypeStruct((2, TALL, CH...  4.2 us
  transfers between devices with their start and end apart: 9, of which 6 were waited for; matrix products, arithmetic and copies ran while one was open for 2% of the time, Pallas kernels for 36%

profile of v6, /device:TPU:0, one launch (start us, length us, event | category | flops | bytes accessed | tf_op | source)
XLA Modules:
  0.0 73.8 jit_solution(1532516816299846048)
XLA Ops:
  0.6 0.0 copy-start.14
  0.6 0.0 copy-start.15
  0.7 0.0 copy-start.16
  0.7 0.0 copy-start.13
  0.7 0.1 collective-permute-start
  0.8 0.5 collective-permute-start.2
  1.3 1.1 %slice_select_fusion.own = bf16[3,64,768]{2,1,0:T(8,128)(2,1)S(1)} fusion(bf16[6,64,768]{2,1,0:T(8,128)(2,1)} %f_own.3, pred[]{:T(512)S(6)} %eq.3), kind=kLoop, calls=%fused_computation | loop fusion | flops 147456 | bytes 884737 | tf_op jit(solution)/shard_map/jit(_where)/select_n | solution.py:556
  2.3 0.6 collective-permute-done.part.f_part
  3.0 0.1 rows.1
  3.1 1.6 %collective-permute-start.1 = (bf16[3,128,768]{2,1,0:T(8,128)(2,1)S(1)}, bf16[3,128,768]{2,1,0:T(8,128)(2,1)S(1)}, u32[]{:S(2)}, u32[]{:S(2)}) collective-permute-start(bf16[3,128,768]{2,1,0:T(8,128)(2,1)S(1)} %rows.1), channel_id=1, source_target_pairs={{0,4},{1,2},{2,6},{3,0},{4,8},{5,1},{6,10},{7,3},{8,12},{9,5},{10,... | collective-permute-start | bytes 1769480 | tf_op jit(solution)/shard_map/ppermute | solution.py:60
  4.7 0.0 copy-done.14
  4.7 0.0 copy-done.15
  4.7 0.0 copy-done.16
  4.7 0.1 pad_add_fusion.info
  4.8 0.0 copy-done.13
  4.8 0.1 reshape.15.filt
  4.9 0.0 copy-start.4
  4.9 0.0 copy-start
  4.9 0.0 copy-start.1
  4.9 3.1 %bands.1 = (bf16[1536,768]{1,0:T(8,128)(2,1)S(1)}, bf16[2,1536,384]{2,1,0:T(8,128)(2,1)S(1)}) custom-call(s32[576]{0:T(1024)S(1)} %pad_add_fusion.info, bf16[196,192]{1,0:T(8,128)(2,1)S(1)} %reshape.15.filt), custom_call_target="tpu_custom_call" | custom-call | flops 2000000000 | bytes 5000000 | tf_op jit(solution)/shard_map/bands/pallas_call | solution.py:569
  8.0 0.0 copy-done.4
  8.0 0.0 collective-permute-done.2.u_part
  8.0 0.0 copy-done
  8.0 0.0 copy-done.1
  8.0 0.0 copy-start.2
  8.1 0.4 edges.1
  8.4 1.7 %collective-permute-start.3 = (bf16[48,768]{1,0:T(8,128)(2,1)S(1)}, bf16[48,768]{1,0:T(8,128)(2,1)S(1)}, u32[]{:S(2)}, u32[]{:S(2)}) collective-permute-start(bf16[48,768]{1,0:T(8,128)(2,1)S(1)} %get-tuple-element.15), channel_id=1, source_target_pairs={{0,2},{1,3},{2,0},{3,1},{4,6},{5,7},{6,4},{7,5},{8,10},{9,11},{10,... | collective-permute-start | bytes 221192 | tf_op jit(solution)/shard_map/ppermute | solution.py:60
  10.1 3.3 %collective-permute-start.4 = (bf16[48,768]{1,0:T(8,128)(2,1)S(1)}, bf16[48,768]{1,0:T(8,128)(2,1)S(1)}, u32[]{:S(2)}, u32[]{:S(2)}) collective-permute-start(bf16[48,768]{1,0:T(8,128)(2,1)S(1)} %get-tuple-element.16), channel_id=1, source_target_pairs={{0,6},{2,4},{4,10},{5,3},{6,8},{7,1},{8,14},{9,7},{10,12},{11,5},{... | collective-permute-start | bytes 221192 | tf_op jit(solution)/shard_map/ppermute | solution.py:60
  13.4 4.2 %inner.1 = (f32[2,1536,768]{2,1,0:T(8,128)S(1)}, bf16[384,768]{1,0:T(8,128)(2,1)S(1)}, bf16[2,3,16,768]{3,2,1,0:T(8,128)(2,1)S(1)}, bf16[3,128,768]{2,1,0:T(8,128)(2,1)}) custom-call(bf16[6,64,768]{2,1,0:T(8,128)(2,1)S(1)} %copy-done, bf16[6,64,768]{2,1,0:T(8,128)(2,1)S(1)} %collective-permute-done.part.f_part, bf16[6,64,768]{2,1,0:T(8,128)(2,1)S(1)} %copy-done.1, ...), custom_call_target="tpu_custom_call" | custom-call | flops 4000000000 | bytes 16000000 | tf_op jit(solution)/shard_map/inner/pallas_call | solution.py:601
  17.6 0.0 copy-done.2
  17.6 2.0 %collective-permute-done.3.e_own = bf16[48,768]{1,0:T(8,128)(2,1)S(1)} collective-permute-done((bf16[48,768]{1,0:T(8,128)(2,1)S(1)}, bf16[48,768]{1,0:T(8,128)(2,1)S(1)}, u32[]{:S(2)}, u32[]{:S(2)}) %collective-permute-start.3) | collective-permute-done | bytes 73760 | tf_op jit(solution)/shard_map/ppermute | solution.py:60
  19.6 0.0 collective-permute-done.4.c_own
  19.6 0.8 %collective-permute-done.1.a_own = bf16[3,128,768]{2,1,0:T(8,128)(2,1)S(1)} collective-permute-done((bf16[3,128,768]{2,1,0:T(8,128)(2,1)S(1)}, bf16[3,128,768]{2,1,0:T(8,128)(2,1)S(1)}, u32[]{:S(2)}, u32[]{:S(2)}) %collective-permute-start.1) | collective-permute-done | bytes 589856 | tf_op jit(solution)/shard_map/ppermute | solution.py:60
  20.4 0.1 relay.1
  20.4 0.0 copy-start.8
  20.4 0.7 collective-permute-start.5
  21.1 0.0 collective-permute-start.6
  21.1 1.9 %collective-permute-done.5.p_part = bf16[4,128,768]{2,1,0:T(8,128)(2,1)S(1)} collective-permute-done((bf16[4,128,768]{2,1,0:T(8,128)(2,1)S(1)}, bf16[4,128,768]{2,1,0:T(8,128)(2,1)S(1)}, u32[]{:S(2)}, u32[]{:S(2)}) %collective-permute-start.5) | collective-permute-done | bytes 786464 | tf_op jit(solution)/shard_map/ppermute | solution.py:60
  23.0 0.0 copy-start.10
  23.0 5.0 %grad.1 = (bf16[3072,384]{1,0:T(8,128)(2,1)}, bf16[4,384,768]{2,1,0:T(8,128)(2,1)}) custom-call(bf16[4,128,768]{2,1,0:T(8,128)(2,1)S(1)} %get-tuple-element.19.p_own, bf16[4,128,768]{2,1,0:T(8,128)(2,1)S(1)} %collective-permute-done.5.p_part, bf16[2,3,16,768]{3,2,1,0:T(8,128)(2,1)S(1)} %get-tuple-element.20.pole_ref, ...), custom_call_target="tpu_custom_call" | custom-call | flops 6000000000 | bytes 12000000 | tf_op jit(solution)/shard_map/grad/pallas_call | solution.py:636
  28.0 0.0 copy-done.8
  28.1 0.0 copy-done.10
  28.1 11.8 %all-to-all-start = ((bf16[128,24,384]{2,1,0:T(8,128)(2,1)}), bf16[128,24,384]{2,1,0:T(8,128)(2,1)S(1)}, u32[]{:S(2)}, u32[]{:S(2)}) async-start(bf16[128,24,384]{2,1,0:T(8,128)(2,1)} %bitcast.4), calls=%async_computation | async-start | bytes 4718592 | tf_op jit(solution)/shard_map/all_to_all | solution.py:655
  39.8 0.0 copy-start.6
  39.8 2.3 %copy-done.6 = bf16[3072,768]{1,0:T(8,128)(2,1)S(1)} copy-done((bf16[3072,768]{1,0:T(8,128)(2,1)S(1)}, bf16[3072,768]{1,0:T(8,128)(2,1)}, u32[]{:S(2)}) %copy-start.6) | copy-done | bytes 4718616
  42.2 0.0 copy-start.12
  42.2 1.7 %copy-done.12 = bf16[4,384,768]{2,1,0:T(8,128)(2,1)S(1)} copy-done((bf16[4,384,768]{2,1,0:T(8,128)(2,1)S(1)}, bf16[4,384,768]{2,1,0:T(8,128)(2,1)}, u32[]{:S(2)}) %copy-start.12) | copy-done | bytes 2359320
  43.8 0.0 copy-start.5
  43.8 2.8 %conv.1.after = bf16[6,64,768]{2,1,0:T(8,128)(2,1)} custom-call(bf16[4,384,768]{2,1,0:T(8,128)(2,1)S(1)} %copy-done.12, bf16[3072,768]{1,0:T(8,128)(2,1)S(1)} %copy-done.6), custom_call_target="tpu_custom_call" | custom-call | flops 80000000000 | bytes 8000000 | tf_op jit(solution)/shard_map/conv/pallas_call | solution.py:657
  46.6 0.0 copy-start.9
  46.7 0.0 copy-start.11
  46.7 0.0 collective-permute-done.6.rows
  46.7 0.1 collective-permute-start.7
  46.8 0.0 copy-done.5
  46.8 1.2 %spread.1.vec_ref = f32[7,16,384]{2,1,0:T(8,128)S(1)} custom-call(s32[576]{0:T(1024)S(1)} %pad_add_fusion.info, bf16[196,192]{1,0:T(8,128)(2,1)S(1)} %copy-done.5, bf16[6,64,768]{2,1,0:T(8,128)(2,1)} %conv.1.after), custom_call_target="tpu_custom_call" | custom-call | flops 1000000000 | bytes 1000000 | tf_op jit(solution)/shard_map/spread/pallas_call | solution.py:676
  48.0 0.7 %collective-permute-done.7.a_part = bf16[3,128,768]{2,1,0:T(8,128)(2,1)S(1)} collective-permute-done((bf16[3,128,768]{2,1,0:T(8,128)(2,1)S(1)}, bf16[3,128,768]{2,1,0:T(8,128)(2,1)S(1)}, u32[]{:S(2)}, u32[]{:S(2)}) %collective-permute-start.7) | collective-permute-done | bytes 589856 | tf_op jit(solution)/shard_map/ppermute | solution.py:60
  48.8 0.0 copy-done.3
  48.8 0.0 copy-done.9
  48.8 0.0 copy-done.11
  48.8 0.0 copy-start.7
  48.8 2.3 %copy-done.7 = bf16[3072,768]{1,0:T(8,128)(2,1)S(1)} copy-done((bf16[3072,768]{1,0:T(8,128)(2,1)S(1)}, bf16[3072,768]{1,0:T(8,128)(2,1)}, u32[]{:S(2)}) %copy-start.7) | copy-done | bytes 4718616
  51.1 10.0 %state.1 = bf16[6,64,768]{2,1,0:T(8,128)(2,1)} custom-call(bf16[3072,768]{1,0:T(8,128)(2,1)S(1)} %copy-done.7, f32[7,16,384]{2,1,0:T(8,128)S(1)} %spread.1.vec_ref, bf16[6,64,768]{2,1,0:T(8,128)(2,1)S(1)} %copy-done.1, bf16[6,64,768]{2,1,0:T(8,128)(2,1)S(1)} %copy-done.3, bf16[4,128,768]{2,1,0:T(8,128)(2,1)S(1)} %copy-done.9, ...), custom_call_target="tpu_custom_call" | custom-call | flops 8000000000 | bytes 12000000 | tf_op jit(solution)/shard_map/state/pallas_call | solution.py:685
  61.1 11.7 %all-to-all-done = bf16[128,24,384]{2,1,0:T(8,128)(2,1)S(1)} async-done(((bf16[128,24,384]{2,1,0:T(8,128)(2,1)}), bf16[128,24,384]{2,1,0:T(8,128)(2,1)S(1)}, u32[]{:S(2)}, u32[]{:S(2)}) %all-to-all-start) | async-done | bytes 2359328 | tf_op jit(solution)/shard_map/all_to_all | solution.py:655
  72.8 1.0 %total.1 = f32[24,768]{1,0:T(8,128)} custom-call(bf16[64,2,24,384]{3,2,1,0:T(8,128)(2,1)S(1)} %bitcast.3), custom_call_target="tpu_custom_call" | custom-call | tf_op jit(solution)/shard_map/total/pallas_call | solution.py:702
  (2 shorter events, 0.0 us)
Async XLA Ops:
  0.6 4.1 %copy-start.14 = (s32[192]{0:T(256)S(1)}, s32[192]{0:T(256)}, u32[]{:S(2)}) copy-start(s32[192]{0:T(256)} %param.13) | copy-start | bytes 2308
  0.6 4.1 %copy-start.15 = (s32[192]{0:T(256)S(1)}, s32[192]{0:T(256)}, u32[]{:S(2)}) copy-start(s32[192]{0:T(256)} %param.12) | copy-start | bytes 2308
  0.7 4.1 %copy-start.16 = (s32[192]{0:T(256)S(1)}, s32[192]{0:T(256)}, u32[]{:S(2)}) copy-start(s32[192]{0:T(256)} %param.11) | copy-start | bytes 2308
  0.7 4.1 %copy-start.13 = (bf16[4,192,7,7]{1,0,3,2:T(4,128)(2,1)S(1)}, bf16[4,192,7,7]{1,0,3,2:T(4,128)(2,1)}, u32[]{:S(2)}) copy-start(bf16[4,192,7,7]{1,0,3,2:T(4,128)(2,1)} %param.10) | copy-start | bytes 225796
  0.7 2.3 %collective-permute-start = (bf16[6,64,768]{2,1,0:T(8,128)(2,1)}, bf16[6,64,768]{2,1,0:T(8,128)(2,1)S(1)}, u32[]{:S(2)}, u32[]{:S(2)}) collective-permute-start(bf16[6,64,768]{2,1,0:T(8,128)(2,1)} %f_own.3), channel_id=1, source_target_pairs={{0,1},{1,0},{2,3},{3,2},{4,5},{5,4},{6,7},{7,6},{8,9},{9,8},{10,11... | collective-permute-start | bytes 1769480 | tf_op jit(solution)/shard_map/ppermute | solution.py:60
  0.8 7.2 %collective-permute-start.2 = (bf16[6,64,768]{2,1,0:T(8,128)(2,1)}, bf16[6,64,768]{2,1,0:T(8,128)(2,1)S(1)}, u32[]{:S(2)}, u32[]{:S(2)}) collective-permute-start(bf16[6,64,768]{2,1,0:T(8,128)(2,1)} %u_own.5), channel_id=1, source_target_pairs={{0,1},{1,0},{2,3},{3,2},{4,5},{5,4},{6,7},{7,6},{8,9},{9,8},{10,11... | collective-permute-start | bytes 1769480 | tf_op jit(solution)/shard_map/ppermute | solution.py:60
  3.1 17.3 %collective-permute-start.1 = (bf16[3,128,768]{2,1,0:T(8,128)(2,1)S(1)}, bf16[3,128,768]{2,1,0:T(8,128)(2,1)S(1)}, u32[]{:S(2)}, u32[]{:S(2)}) collective-permute-start(bf16[3,128,768]{2,1,0:T(8,128)(2,1)S(1)} %rows.1), channel_id=1, source_target_pairs={{0,4},{1,2},{2,6},{3,0},{4,8},{5,1},{6,10},{7,3},{8,12},{9,5},{10,... | collective-permute-start | bytes 1769480 | tf_op jit(solution)/shard_map/ppermute | solution.py:60
  4.9 3.1 %copy-start.4 = (bf16[196,192]{1,0:T(8,128)(2,1)}, bf16[196,192]{1,0:T(8,128)(2,1)S(1)}, u32[]{:S(2)}) copy-start(bf16[196,192]{1,0:T(8,128)(2,1)S(1)} %reshape.15.filt) | copy-start | bytes 225796
  4.9 3.1 %copy-start = (bf16[6,64,768]{2,1,0:T(8,128)(2,1)S(1)}, bf16[6,64,768]{2,1,0:T(8,128)(2,1)}, u32[]{:S(2)}) copy-start(bf16[6,64,768]{2,1,0:T(8,128)(2,1)} %f_own.3) | copy-start | bytes 1769476
  4.9 3.1 %copy-start.1 = (bf16[6,64,768]{2,1,0:T(8,128)(2,1)S(1)}, bf16[6,64,768]{2,1,0:T(8,128)(2,1)}, u32[]{:S(2)}) copy-start(bf16[6,64,768]{2,1,0:T(8,128)(2,1)} %u_own.5) | copy-start | bytes 1769476
  8.0 9.5 %copy-start.2 = (bf16[6,64,768]{2,1,0:T(8,128)(2,1)}, bf16[6,64,768]{2,1,0:T(8,128)(2,1)S(1)}, u32[]{:S(2)}) copy-start(bf16[6,64,768]{2,1,0:T(8,128)(2,1)S(1)} %collective-permute-done.2.u_part) | copy-start | bytes 1769476
  8.4 11.2 %collective-permute-start.3 = (bf16[48,768]{1,0:T(8,128)(2,1)S(1)}, bf16[48,768]{1,0:T(8,128)(2,1)S(1)}, u32[]{:S(2)}, u32[]{:S(2)}) collective-permute-start(bf16[48,768]{1,0:T(8,128)(2,1)S(1)} %get-tuple-element.15), channel_id=1, source_target_pairs={{0,2},{1,3},{2,0},{3,1},{4,6},{5,7},{6,4},{7,5},{8,10},{9,11},{10,... | collective-permute-start | bytes 221192 | tf_op jit(solution)/shard_map/ppermute | solution.py:60
  10.1 9.5 %collective-permute-start.4 = (bf16[48,768]{1,0:T(8,128)(2,1)S(1)}, bf16[48,768]{1,0:T(8,128)(2,1)S(1)}, u32[]{:S(2)}, u32[]{:S(2)}) collective-permute-start(bf16[48,768]{1,0:T(8,128)(2,1)S(1)} %get-tuple-element.16), channel_id=1, source_target_pairs={{0,6},{2,4},{4,10},{5,3},{6,8},{7,1},{8,14},{9,7},{10,12},{11,5},{... | collective-permute-start | bytes 221192 | tf_op jit(solution)/shard_map/ppermute | solution.py:60
  20.4 7.6 %copy-start.8 = (bf16[4,128,768]{2,1,0:T(8,128)(2,1)}, bf16[4,128,768]{2,1,0:T(8,128)(2,1)S(1)}, u32[]{:S(2)}) copy-start(bf16[4,128,768]{2,1,0:T(8,128)(2,1)S(1)} %get-tuple-element.19.p_own) | copy-start | bytes 2359300
  20.4 2.6 %collective-permute-start.5 = (bf16[4,128,768]{2,1,0:T(8,128)(2,1)S(1)}, bf16[4,128,768]{2,1,0:T(8,128)(2,1)S(1)}, u32[]{:S(2)}, u32[]{:S(2)}) collective-permute-start(bf16[4,128,768]{2,1,0:T(8,128)(2,1)S(1)} %get-tuple-element.19.p_own), channel_id=1, source_target_pairs={{0,1},{1,0},{2,3},{3,2},{4,5},{5,4},{6,7},{7,6},{8,9},{9,8},{10,11... | collective-permute-start | bytes 2359304 | tf_op jit(solution)/shard_map/ppermute | solution.py:60
  21.1 25.5 %collective-permute-start.6 = (bf16[3,128,768]{2,1,0:T(8,128)(2,1)}, bf16[3,128,768]{2,1,0:T(8,128)(2,1)S(1)}, u32[]{:S(2)}, u32[]{:S(2)}) collective-permute-start(bf16[3,128,768]{2,1,0:T(8,128)(2,1)} %get-tuple-element.25), channel_id=1, source_target_pairs={{0,4},{1,2},{2,6},{3,0},{4,8},{5,1},{6,10},{7,3},{8,12},{9,5},{10,... | collective-permute-start | bytes 1769480 | tf_op jit(solution)/shard_map/ppermute | solution.py:60
  23.0 5.0 %copy-start.10 = (bf16[4,128,768]{2,1,0:T(8,128)(2,1)}, bf16[4,128,768]{2,1,0:T(8,128)(2,1)S(1)}, u32[]{:S(2)}) copy-start(bf16[4,128,768]{2,1,0:T(8,128)(2,1)S(1)} %collective-permute-done.5.p_part) | copy-start | bytes 2359300
  28.1 44.7 %all-to-all-start = ((bf16[128,24,384]{2,1,0:T(8,128)(2,1)}), bf16[128,24,384]{2,1,0:T(8,128)(2,1)S(1)}, u32[]{:S(2)}, u32[]{:S(2)}) async-start(bf16[128,24,384]{2,1,0:T(8,128)(2,1)} %bitcast.4), calls=%async_computation | async-start | bytes 4718592 | tf_op jit(solution)/shard_map/all_to_all | solution.py:655
  39.8 2.3 %copy-start.6 = (bf16[3072,768]{1,0:T(8,128)(2,1)S(1)}, bf16[3072,768]{1,0:T(8,128)(2,1)}, u32[]{:S(2)}) copy-start(bf16[3072,768]{1,0:T(8,128)(2,1)} %w_ref.3) | copy-start | bytes 14155780
  42.2 1.7 %copy-start.12 = (bf16[4,384,768]{2,1,0:T(8,128)(2,1)S(1)}, bf16[4,384,768]{2,1,0:T(8,128)(2,1)}, u32[]{:S(2)}) copy-start(bf16[4,384,768]{2,1,0:T(8,128)(2,1)} %get-tuple-element.24.own_ref) | copy-start | bytes 7077892
  43.8 2.9 %copy-start.5 = (bf16[196,192]{1,0:T(8,128)(2,1)S(1)}, bf16[196,192]{1,0:T(8,128)(2,1)}, u32[]{:S(2)}) copy-start(bf16[196,192]{1,0:T(8,128)(2,1)} %copy-done.4) | copy-start | bytes 225796
  46.6 2.1 %copy-start.3 = (bf16[6,64,768]{2,1,0:T(8,128)(2,1)S(1)}, bf16[6,64,768]{2,1,0:T(8,128)(2,1)}, u32[]{:S(2)}) copy-start(bf16[6,64,768]{2,1,0:T(8,128)(2,1)} %copy-done.2) | copy-start | bytes 1769476
  46.6 2.1 %copy-start.9 = (bf16[4,128,768]{2,1,0:T(8,128)(2,1)S(1)}, bf16[4,128,768]{2,1,0:T(8,128)(2,1)}, u32[]{:S(2)}) copy-start(bf16[4,128,768]{2,1,0:T(8,128)(2,1)} %copy-done.8) | copy-start | bytes 2359300
  46.7 2.1 %copy-start.11 = (bf16[4,128,768]{2,1,0:T(8,128)(2,1)S(1)}, bf16[4,128,768]{2,1,0:T(8,128)(2,1)}, u32[]{:S(2)}) copy-start(bf16[4,128,768]{2,1,0:T(8,128)(2,1)} %copy-done.10) | copy-start | bytes 2359300
  46.7 2.1 %collective-permute-start.7 = (bf16[3,128,768]{2,1,0:T(8,128)(2,1)S(1)}, bf16[3,128,768]{2,1,0:T(8,128)(2,1)S(1)}, u32[]{:S(2)}, u32[]{:S(2)}) collective-permute-start(bf16[3,128,768]{2,1,0:T(8,128)(2,1)S(1)} %tie.1.a_own), channel_id=1, source_target_pairs={{0,1},{1,0},{2,3},{3,2},{4,5},{5,4},{6,7},{7,6},{8,9},{9,8},{10,11... | collective-permute-start | bytes 1769480 | tf_op jit(solution)/shard_map/ppermute | solution.py:60
  48.8 2.3 %copy-start.7 = (bf16[3072,768]{1,0:T(8,128)(2,1)S(1)}, bf16[3072,768]{1,0:T(8,128)(2,1)}, u32[]{:S(2)}) copy-start(bf16[3072,768]{1,0:T(8,128)(2,1)} %w_ref.3) | copy-start | bytes 14155780

commit v7 on v6

--- a/solution.py
+++ b/solution.py
@@ -262,12 +262,16 @@
             run(row_copies(((own, 0, mine), (part, row, other)), out, sems, False))
 
 
-def relay_kernel(a_own, e_own, c_own, u_rows, out, u_out):
-    del u_rows, u_out
+def join_kernel(e_own, c_own, after, out):
+    del after
+    out[0:PACKED] = e_own[...]
+    out[COLS : COLS + PACKED] = c_own[...]
+
+
+def relay_kernel(a_own, u_rows, after, out, u_out):
+    del u_rows, after, u_out
     core, lat = my_core(), my_lat()
     turn = ((core == 0) & (lat == 0)) | ((core == 1) & (lat == LAT - 1))
-    out[HALO, 0:PACKED] = e_own[...]
-    out[HALO, COLS : COLS + PACKED] = c_own[...]
 
     @pl.when(turn)
     def _():
@@ -276,7 +280,7 @@
 
     @pl.when(jnp.logical_not(turn))
     def _():
-        out[0:HALO] = a_own[...]
+        out[...] = a_own[...]
 
 
 PACKED = 3 * EDGE
@@ -354,7 +358,7 @@
     mid = slice(HALO, HALO + ROWS)
     for n, (ref, at) in enumerate(((passed1, 0), (passed0, 0), (passed0, COLS), (passed1, COLS))):
         at += EDGE * which
-        todo.append(pltpu.make_async_copy(ref.at[HALO, at : at + 2 * EDGE], rim.at[n], sems.at[n]))
+        todo.append(pltpu.make_async_copy(ref.at[at : at + 2 * EDGE], rim.at[n], sems.at[n]))
     put(half0, whole, EDGE, mid, 4)
     put(half1, whole, EDGE + COLS, mid, 5)
     n = 6
@@ -435,18 +439,18 @@
     chip_rows(u_own, u_part, u_rows, row_sems, wait_copy)
 
 
-def fill_outer(x, passed0, passed1, pole_ref):
+def fill_outer(x, passed0, passed1, joined0, joined1, pole_ref):
     lat = my_lat()
     low, high = slice(0, WIN - EDGE), slice(CHIP - WIN + EDGE, CHIP)
-    for side, (rows, pole) in enumerate(((passed0, 0), (passed1, LAT - 1))):
+    for side, (rows, joined, pole) in enumerate(((passed0, joined0, 0), (passed1, joined1, LAT - 1))):
         block, at, none = (HALO, 0, slice(2 * EDGE, WIN)) if side == 0 else (0, WIN - 2 * EDGE, slice(0, WIN - 2 * EDGE))
-        for w, edges in enumerate((passed1, passed0)):
+        for w, edges in enumerate((joined1, joined0)):
             x[side, w, block, none, :] = jnp.zeros((WIN - 2 * EDGE, CHANNELS), BF)
-            x[side, w, block, at : at + 2 * EDGE, :] = edges[HALO, 0 : 2 * EDGE]
+            x[side, w, block, at : at + 2 * EDGE, :] = edges[0 : 2 * EDGE]
             to = slice(EDGE, WIN) if w == 0 else slice(0, WIN - EDGE)
             for m in range(HALO):
                 x[side, w, side + m, to, :] = rows[m, low if w == 0 else high]
-        corners = rows.at[HALO, COLS : COLS + 2 * EDGE]
+        corners = joined.at[COLS : COLS + 2 * EDGE]
 
         @pl.when(lat != pole)
         def _():
@@ -463,16 +467,16 @@
                     x[side, w, side + m, at : at + EDGE, :] = pole_ref[w, m]
 
 
-def grad_kernel(p_own, p_part, pole_ref, acc, band, up, g_ref, own_ref, x, basis, g, sems):
+def grad_kernel(p_own, p_part, j_own, j_part, pole_ref, acc, band, up, g_ref, own_ref, x, basis, g, sems):
     core = my_core()
 
     @pl.when(core == 0)
     def _():
-        fill_outer(x, p_own, p_part, pole_ref)
+        fill_outer(x, p_own, p_part, j_own, j_part, pole_ref)
 
     @pl.when(core == 1)
     def _():
-        fill_outer(x, p_part, p_own, pole_ref)
+        fill_outer(x, p_part, p_own, j_part, j_own, pole_ref)
 
     for i in range(ROWS):
         to = slice(i * NBASIS * COLS, (i + 1) * NBASIS * COLS)
@@ -618,19 +622,29 @@
         cost_estimate=cost(4_000_000_000, 16_000_000),
         name="inner",
     )(features, f_part, upstream, u_part, inner_band)
+    joined = pl.pallas_call(
+        join_kernel,
+        out_shape=jax.ShapeDtypeStruct((COLS + PACKED, CHANNELS), BF),
+        in_specs=[VMEM, VMEM, ANY],
+        out_specs=VMEM,
+        compiler_params=params(4),
+        cost_estimate=cost(1000, 300_000),
+        name="join",
+    )(e_own, c_own, up)
+    j_part = send(joined, to_partner)
     passed, u_rows = pl.pallas_call(
         relay_kernel,
         out_shape=(
-            jax.ShapeDtypeStruct((HALO + 1, CHIP, CHANNELS), BF),
+            jax.ShapeDtypeStruct((HALO, CHIP, CHANNELS), BF),
             jax.ShapeDtypeStruct((HALO, CHIP, CHANNELS), BF),
         ),
-        in_specs=[VMEM] * 3 + [ANY],
+        in_specs=[VMEM, ANY, ANY],
         out_specs=(VMEM, ANY),
-        input_output_aliases={3: 1},
+        input_output_aliases={1: 1},
         compiler_params=params(8),
         cost_estimate=cost(1000, 4_000_000),
         name="relay",
-    )(af_own, e_own, c_own, u_rows)
+    )(af_own, u_rows, joined)
     p_part = send(passed, to_partner)
     au_own = send(u_rows, along_meridian)
     partial, basis_own = pl.pallas_call(
@@ -639,7 +653,7 @@
             pltpu.HBM((NBASIS * CHANNELS, HALF), BF),
             pltpu.HBM((NBASIS, CELLS, CHANNELS), BF),
         ),
-        in_specs=[VMEM] * 6,
+        in_specs=[VMEM] * 8,
         out_specs=(HBM, HBM),
         scratch_shapes=[
             pltpu.VMEM((2, 2, 1 + HALO, WIN, CHANNELS), BF),
@@ -650,7 +664,7 @@
         compiler_params=params(30),
         cost_estimate=cost(6_000_000_000, 12_000_000),
         name="grad",
-    )(passed, p_part, pole, acc, outer_band, up)
+    )(passed, p_part, joined, j_part, pole, acc, outer_band, up)
 
     pieces = lax.all_to_all(partial.reshape(LAT * LON, OWNED, HALF), BOTH, 0, 0, tiled=True)
 
@@ -697,7 +711,7 @@
         compiler_params=params(28),
         cost_estimate=cost(8_000_000_000, 12_000_000),
         name="state",
-    )(weights, vecs, upstream, u_part, passed, p_part, au_own, au_part)
+    )(weights, vecs, upstream, u_part, joined, j_part, au_own, au_part)
 
     weight_grad = pl.pallas_call(
         total_kernel,

time: 74.2 us -> 74 us (level)
    ppermute x8 -> x9, starting transfers between devices: 7.95 us -> 8.08 us  [send(): return lax.ppermute(block, BOTH, pairs)]
    ppermute x8 -> x9, waiting for transfers between devices: 6.05 us -> 5.96 us  [send(): return lax.ppermute(block, BOTH, pairs)]
    unnamed x34 -> x24, local copies, waits for them, and re-layouts: 6.39 us -> 6.38 us
  transfers between devices with their start and end apart: 9 -> 10, of which waited for: 6 -> 6; matrix products, arithmetic and copies ran while one was open for 2% -> 2% of each run, Pallas kernels for 36% -> 36%
where the time goes in v7:
time: 74 us; the launch traced here: 73.5 us
  Pallas kernels  27.6 us (37%)
  starting transfers between devices  19.8 us (27%)
  waiting for transfers between devices  17.7 us (24%)
  local copies, waits for them, and re-layouts  6.44 us (9%)
  other arithmetic  1.16 us (2%)
  between operations  0.85 us (1%)
    all_to_all x1, starting transfers between devices, on_device(): lax.all_to_all(partial.reshape(LAT * LON, OWNED, HALF), BOTH, 0, 0, tiled...  11.8 us
    all_to_all x1, waiting for transfers between devices, on_device(): lax.all_to_all(partial.reshape(LAT * LON, OWNED, HALF), BOTH, 0, 0, tiled...  11.7 us
    pallas_call x1, Pallas kernels, on_device(): pl.pallas_call(state_kernel, out_shape=jax.ShapeDtypeStruct((ROWS, COLS,...  9.94 us
    ppermute x9, starting transfers between devices, send(): return lax.ppermute(block, BOTH, pairs)  8.08 us
    unnamed x24, local copies, waits for them, and re-layouts  6.38 us
    ppermute x9, waiting for transfers between devices, send(): return lax.ppermute(block, BOTH, pairs)  5.96 us
    pallas_call x1, Pallas kernels, on_device(): pl.pallas_call(grad_kernel, out_shape=(pltpu.HBM((NBASIS * CHANNELS, HALF...  4.83 us
    pallas_call x1, Pallas kernels, on_device(): pl.pallas_call(inner_kernel, out_shape=(jax.ShapeDtypeStruct((2, TALL, CH...  4.18 us
  transfers between devices with their start and end apart: 10, of which 6 were waited for; matrix products, arithmetic and copies ran while one was open for 2% of the time, Pallas kernels for 36%

profile of v7, /device:TPU:0, one launch (start us, length us, event | category | flops | bytes accessed | tf_op | source)
XLA Modules:
  0.0 73.5 jit_solution(15007459450956277180)
XLA Ops:
  0.6 0.0 copy-start.9
  0.6 0.0 copy-start.10
  0.7 0.0 copy-start.11
  0.7 0.0 copy-start.8
  0.7 0.1 collective-permute-start
  0.8 0.5 collective-permute-start.2
  1.3 1.1 %slice_select_fusion.own = bf16[3,64,768]{2,1,0:T(8,128)(2,1)S(1)} fusion(bf16[6,64,768]{2,1,0:T(8,128)(2,1)} %f_own.3, pred[]{:T(512)S(6)} %eq.3), kind=kLoop, calls=%fused_computation | loop fusion | flops 147456 | bytes 884737 | tf_op jit(solution)/shard_map/jit(_where)/select_n | solution.py:560
  2.3 0.6 collective-permute-done.part.f_part
  3.0 0.1 rows.1
  3.1 1.6 %collective-permute-start.1 = (bf16[3,128,768]{2,1,0:T(8,128)(2,1)S(1)}, bf16[3,128,768]{2,1,0:T(8,128)(2,1)S(1)}, u32[]{:S(2)}, u32[]{:S(2)}) collective-permute-start(bf16[3,128,768]{2,1,0:T(8,128)(2,1)S(1)} %rows.1), channel_id=1, source_target_pairs={{0,4},{1,2},{2,6},{3,0},{4,8},{5,1},{6,10},{7,3},{8,12},{9,5},{10,... | collective-permute-start | bytes 1769480 | tf_op jit(solution)/shard_map/ppermute | solution.py:60
  4.7 0.0 copy-done.9
  4.7 0.0 copy-done.10
  4.7 0.0 copy-done.11
  4.7 0.1 pad_add_fusion.info
  4.8 0.0 copy-done.8
  4.8 0.1 reshape.15.filt
  4.9 0.0 copy-start
  4.9 0.0 copy-start.1
  4.9 3.1 %bands.1 = (bf16[1536,768]{1,0:T(8,128)(2,1)S(1)}, bf16[2,1536,384]{2,1,0:T(8,128)(2,1)S(1)}) custom-call(s32[576]{0:T(1024)S(1)} %pad_add_fusion.info, bf16[196,192]{1,0:T(8,128)(2,1)S(1)} %reshape.15.filt), custom_call_target="tpu_custom_call" | custom-call | flops 2000000000 | bytes 5000000 | tf_op jit(solution)/shard_map/bands/pallas_call | solution.py:573
  8.0 0.0 collective-permute-done.2.u_part
  8.0 0.0 copy-done
  8.0 0.0 copy-done.1
  8.0 0.0 copy-start.3
  8.0 0.4 edges.1
  8.4 1.7 %collective-permute-start.3 = (bf16[48,768]{1,0:T(8,128)(2,1)S(1)}, bf16[48,768]{1,0:T(8,128)(2,1)S(1)}, u32[]{:S(2)}, u32[]{:S(2)}) collective-permute-start(bf16[48,768]{1,0:T(8,128)(2,1)S(1)} %get-tuple-element.17), channel_id=1, source_target_pairs={{0,2},{1,3},{2,0},{3,1},{4,6},{5,7},{6,4},{7,5},{8,10},{9,11},{10,... | collective-permute-start | bytes 221192 | tf_op jit(solution)/shard_map/ppermute | solution.py:60
  10.1 3.3 %collective-permute-start.4 = (bf16[48,768]{1,0:T(8,128)(2,1)S(1)}, bf16[48,768]{1,0:T(8,128)(2,1)S(1)}, u32[]{:S(2)}, u32[]{:S(2)}) collective-permute-start(bf16[48,768]{1,0:T(8,128)(2,1)S(1)} %get-tuple-element.18), channel_id=1, source_target_pairs={{0,6},{2,4},{4,10},{5,3},{6,8},{7,1},{8,14},{9,7},{10,12},{11,5},{... | collective-permute-start | bytes 221192 | tf_op jit(solution)/shard_map/ppermute | solution.py:60
  13.3 4.2 %inner.1 = (f32[2,1536,768]{2,1,0:T(8,128)S(1)}, bf16[384,768]{1,0:T(8,128)(2,1)S(1)}, bf16[2,3,16,768]{3,2,1,0:T(8,128)(2,1)S(1)}, bf16[3,128,768]{2,1,0:T(8,128)(2,1)}) custom-call(bf16[6,64,768]{2,1,0:T(8,128)(2,1)S(1)} %copy-done, bf16[6,64,768]{2,1,0:T(8,128)(2,1)S(1)} %collective-permute-done.part.f_part, bf16[6,64,768]{2,1,0:T(8,128)(2,1)S(1)} %copy-done.1, ...), custom_call_target="tpu_custom_call" | custom-call | flops 4000000000 | bytes 16000000 | tf_op jit(solution)/shard_map/inner/pallas_call | solution.py:605
  17.5 0.0 copy-done.3
  17.5 2.1 %collective-permute-done.3.e_own = bf16[48,768]{1,0:T(8,128)(2,1)S(1)} collective-permute-done((bf16[48,768]{1,0:T(8,128)(2,1)S(1)}, bf16[48,768]{1,0:T(8,128)(2,1)S(1)}, u32[]{:S(2)}, u32[]{:S(2)}) %collective-permute-start.3) | collective-permute-done | bytes 73760 | tf_op jit(solution)/shard_map/ppermute | solution.py:60
  19.6 0.0 collective-permute-done.4.c_own
  19.6 0.7 %collective-permute-done.1.a_own = bf16[3,128,768]{2,1,0:T(8,128)(2,1)S(1)} collective-permute-done((bf16[3,128,768]{2,1,0:T(8,128)(2,1)S(1)}, bf16[3,128,768]{2,1,0:T(8,128)(2,1)S(1)}, u32[]{:S(2)}, u32[]{:S(2)}) %collective-permute-start.1) | collective-permute-done | bytes 589856 | tf_op jit(solution)/shard_map/ppermute | solution.py:60
  20.4 0.7 %collective-permute-start.5 = (bf16[3,128,768]{2,1,0:T(8,128)(2,1)S(1)}, bf16[3,128,768]{2,1,0:T(8,128)(2,1)S(1)}, u32[]{:S(2)}, u32[]{:S(2)}) collective-permute-start(bf16[3,128,768]{2,1,0:T(8,128)(2,1)S(1)} %get-tuple-element.20.p_own), channel_id=1, source_target_pairs={{0,1},{1,0},{2,3},{3,2},{4,5},{5,4},{6,7},{7,6},{8,9},{9,8},{10,11... | collective-permute-start | bytes 1769480 | tf_op jit(solution)/shard_map/ppermute | solution.py:60
  21.1 0.1 collective-permute-start.6
  21.2 0.0 collective-permute-start.7
  21.2 1.8 %collective-permute-done.6.j_part.p_part = bf16[112,768]{1,0:T(8,128)(2,1)S(1)} collective-permute-done((bf16[112,768]{1,0:T(8,128)(2,1)S(1)}, bf16[112,768]{1,0:T(8,128)(2,1)S(1)}, u32[]{:S(2)}, u32[]{:S(2)}) %collective-permute-start.6) | collective-permute-done | bytes 172064 | tf_op jit(solution)/shard_map/ppermute | solution.py:60
  23.0 0.0 collective-permute-done.5.p_part
  23.0 4.8 %grad.1 = (bf16[3072,384]{1,0:T(8,128)(2,1)}, bf16[4,384,768]{2,1,0:T(8,128)(2,1)}) custom-call(bf16[3,128,768]{2,1,0:T(8,128)(2,1)S(1)} %get-tuple-element.20.p_own, bf16[3,128,768]{2,1,0:T(8,128)(2,1)S(1)} %collective-permute-done.5.p_part, bf16[112,768]{1,0:T(8,128)(2,1)S(1)} %join.1.after.j_own.p_own, ...), custom_call_target="tpu_custom_call" | custom-call | flops 6000000000 | bytes 12000000 | tf_op jit(solution)/shard_map/grad/pallas_call | solution.py:650
  27.9 11.8 %all-to-all-start = ((bf16[128,24,384]{2,1,0:T(8,128)(2,1)}), bf16[128,24,384]{2,1,0:T(8,128)(2,1)S(1)}, u32[]{:S(2)}, u32[]{:S(2)}) async-start(bf16[128,24,384]{2,1,0:T(8,128)(2,1)} %bitcast.4), calls=%async_computation | async-start | bytes 4718592 | tf_op jit(solution)/shard_map/all_to_all | solution.py:669
  39.6 0.0 copy-start.5
  39.6 2.3 %copy-done.5 = bf16[3072,768]{1,0:T(8,128)(2,1)S(1)} copy-done((bf16[3072,768]{1,0:T(8,128)(2,1)S(1)}, bf16[3072,768]{1,0:T(8,128)(2,1)}, u32[]{:S(2)}) %copy-start.5) | copy-done | bytes 4718616
  42.0 0.0 copy-start.7
  42.0 1.7 %copy-done.7 = bf16[4,384,768]{2,1,0:T(8,128)(2,1)S(1)} copy-done((bf16[4,384,768]{2,1,0:T(8,128)(2,1)S(1)}, bf16[4,384,768]{2,1,0:T(8,128)(2,1)}, u32[]{:S(2)}) %copy-start.7) | copy-done | bytes 2359320
  43.6 2.8 %conv.1.after = bf16[6,64,768]{2,1,0:T(8,128)(2,1)} custom-call(bf16[4,384,768]{2,1,0:T(8,128)(2,1)S(1)} %copy-done.7, bf16[3072,768]{1,0:T(8,128)(2,1)S(1)} %copy-done.5), custom_call_target="tpu_custom_call" | custom-call | flops 80000000000 | bytes 8000000 | tf_op jit(solution)/shard_map/conv/pallas_call | solution.py:671
  46.4 0.0 copy-start.2
  46.4 0.0 copy-start.4
  46.4 0.0 collective-permute-done.7.rows
  46.4 0.1 collective-permute-start.8
  46.5 1.2 %spread.1.vec_ref = f32[7,16,384]{2,1,0:T(8,128)S(1)} custom-call(s32[576]{0:T(1024)S(1)} %pad_add_fusion.info, bf16[196,192]{1,0:T(8,128)(2,1)S(1)} %reshape.15.filt, bf16[6,64,768]{2,1,0:T(8,128)(2,1)} %conv.1.after), custom_call_target="tpu_custom_call" | custom-call | flops 1000000000 | bytes 1000000 | tf_op jit(solution)/shard_map/spread/pallas_call | solution.py:690
  47.8 0.8 %collective-permute-done.8.a_part = bf16[3,128,768]{2,1,0:T(8,128)(2,1)S(1)} collective-permute-done((bf16[3,128,768]{2,1,0:T(8,128)(2,1)S(1)}, bf16[3,128,768]{2,1,0:T(8,128)(2,1)S(1)}, u32[]{:S(2)}, u32[]{:S(2)}) %collective-permute-start.8) | collective-permute-done | bytes 589856 | tf_op jit(solution)/shard_map/ppermute | solution.py:60
  48.5 0.0 copy-done.2
  48.5 0.0 copy-done.4
  48.5 0.0 copy-start.6
  48.5 2.3 %copy-done.6 = bf16[3072,768]{1,0:T(8,128)(2,1)S(1)} copy-done((bf16[3072,768]{1,0:T(8,128)(2,1)S(1)}, bf16[3072,768]{1,0:T(8,128)(2,1)}, u32[]{:S(2)}) %copy-start.6) | copy-done | bytes 4718616
  50.9 9.9 %state.1 = bf16[6,64,768]{2,1,0:T(8,128)(2,1)} custom-call(bf16[3072,768]{1,0:T(8,128)(2,1)S(1)} %copy-done.6, f32[7,16,384]{2,1,0:T(8,128)S(1)} %spread.1.vec_ref, bf16[6,64,768]{2,1,0:T(8,128)(2,1)S(1)} %copy-done.2, bf16[6,64,768]{2,1,0:T(8,128)(2,1)S(1)} %copy-done.4, bf16[112,768]{1,0:T(8,128)(2,1)S(1)} %join.1.after.j_own.p_own, ...), custom_call_target="tpu_custom_call" | custom-call | flops 8000000000 | bytes 12000000 | tf_op jit(solution)/shard_map/state/pallas_call | solution.py:699
  60.8 11.7 %all-to-all-done = bf16[128,24,384]{2,1,0:T(8,128)(2,1)S(1)} async-done(((bf16[128,24,384]{2,1,0:T(8,128)(2,1)}), bf16[128,24,384]{2,1,0:T(8,128)(2,1)S(1)}, u32[]{:S(2)}, u32[]{:S(2)}) %all-to-all-start) | async-done | bytes 2359328 | tf_op jit(solution)/shard_map/all_to_all | solution.py:669
  72.6 1.0 %total.1 = f32[24,768]{1,0:T(8,128)} custom-call(bf16[64,2,24,384]{3,2,1,0:T(8,128)(2,1)S(1)} %bitcast.3), custom_call_target="tpu_custom_call" | custom-call | tf_op jit(solution)/shard_map/total/pallas_call | solution.py:716
  (3 shorter events, 0.1 us)
Async XLA Ops:
  0.6 4.1 %copy-start.9 = (s32[192]{0:T(256)S(1)}, s32[192]{0:T(256)}, u32[]{:S(2)}) copy-start(s32[192]{0:T(256)} %param.13) | copy-start | bytes 2308
  0.6 4.1 %copy-start.10 = (s32[192]{0:T(256)S(1)}, s32[192]{0:T(256)}, u32[]{:S(2)}) copy-start(s32[192]{0:T(256)} %param.12) | copy-start | bytes 2308
  0.7 4.1 %copy-start.11 = (s32[192]{0:T(256)S(1)}, s32[192]{0:T(256)}, u32[]{:S(2)}) copy-start(s32[192]{0:T(256)} %param.11) | copy-start | bytes 2308
  0.7 4.1 %copy-start.8 = (bf16[4,192,7,7]{1,0,3,2:T(4,128)(2,1)S(1)}, bf16[4,192,7,7]{1,0,3,2:T(4,128)(2,1)}, u32[]{:S(2)}) copy-start(bf16[4,192,7,7]{1,0,3,2:T(4,128)(2,1)} %param.10) | copy-start | bytes 225796
  0.7 2.3 %collective-permute-start = (bf16[6,64,768]{2,1,0:T(8,128)(2,1)}, bf16[6,64,768]{2,1,0:T(8,128)(2,1)S(1)}, u32[]{:S(2)}, u32[]{:S(2)}) collective-permute-start(bf16[6,64,768]{2,1,0:T(8,128)(2,1)} %f_own.3), channel_id=1, source_target_pairs={{0,1},{1,0},{2,3},{3,2},{4,5},{5,4},{6,7},{7,6},{8,9},{9,8},{10,11... | collective-permute-start | bytes 1769480 | tf_op jit(solution)/shard_map/ppermute | solution.py:60
  0.8 7.2 %collective-permute-start.2 = (bf16[6,64,768]{2,1,0:T(8,128)(2,1)}, bf16[6,64,768]{2,1,0:T(8,128)(2,1)S(1)}, u32[]{:S(2)}, u32[]{:S(2)}) collective-permute-start(bf16[6,64,768]{2,1,0:T(8,128)(2,1)} %u_own.5), channel_id=1, source_target_pairs={{0,1},{1,0},{2,3},{3,2},{4,5},{5,4},{6,7},{7,6},{8,9},{9,8},{10,11... | collective-permute-start | bytes 1769480 | tf_op jit(solution)/shard_map/ppermute | solution.py:60
  3.1 17.3 %collective-permute-start.1 = (bf16[3,128,768]{2,1,0:T(8,128)(2,1)S(1)}, bf16[3,128,768]{2,1,0:T(8,128)(2,1)S(1)}, u32[]{:S(2)}, u32[]{:S(2)}) collective-permute-start(bf16[3,128,768]{2,1,0:T(8,128)(2,1)S(1)} %rows.1), channel_id=1, source_target_pairs={{0,4},{1,2},{2,6},{3,0},{4,8},{5,1},{6,10},{7,3},{8,12},{9,5},{10,... | collective-permute-start | bytes 1769480 | tf_op jit(solution)/shard_map/ppermute | solution.py:60
  4.9 3.1 %copy-start = (bf16[6,64,768]{2,1,0:T(8,128)(2,1)S(1)}, bf16[6,64,768]{2,1,0:T(8,128)(2,1)}, u32[]{:S(2)}) copy-start(bf16[6,64,768]{2,1,0:T(8,128)(2,1)} %f_own.3) | copy-start | bytes 1769476
  4.9 3.1 %copy-start.1 = (bf16[6,64,768]{2,1,0:T(8,128)(2,1)S(1)}, bf16[6,64,768]{2,1,0:T(8,128)(2,1)}, u32[]{:S(2)}) copy-start(bf16[6,64,768]{2,1,0:T(8,128)(2,1)} %u_own.5) | copy-start | bytes 1769476
  8.0 9.5 %copy-start.3 = (bf16[6,64,768]{2,1,0:T(8,128)(2,1)}, bf16[6,64,768]{2,1,0:T(8,128)(2,1)S(1)}, u32[]{:S(2)}) copy-start(bf16[6,64,768]{2,1,0:T(8,128)(2,1)S(1)} %collective-permute-done.2.u_part) | copy-start | bytes 1769476
  8.4 11.2 %collective-permute-start.3 = (bf16[48,768]{1,0:T(8,128)(2,1)S(1)}, bf16[48,768]{1,0:T(8,128)(2,1)S(1)}, u32[]{:S(2)}, u32[]{:S(2)}) collective-permute-start(bf16[48,768]{1,0:T(8,128)(2,1)S(1)} %get-tuple-element.17), channel_id=1, source_target_pairs={{0,2},{1,3},{2,0},{3,1},{4,6},{5,7},{6,4},{7,5},{8,10},{9,11},{10,... | collective-permute-start | bytes 221192 | tf_op jit(solution)/shard_map/ppermute | solution.py:60
  10.1 9.5 %collective-permute-start.4 = (bf16[48,768]{1,0:T(8,128)(2,1)S(1)}, bf16[48,768]{1,0:T(8,128)(2,1)S(1)}, u32[]{:S(2)}, u32[]{:S(2)}) collective-permute-start(bf16[48,768]{1,0:T(8,128)(2,1)S(1)} %get-tuple-element.18), channel_id=1, source_target_pairs={{0,6},{2,4},{4,10},{5,3},{6,8},{7,1},{8,14},{9,7},{10,12},{11,5},{... | collective-permute-start | bytes 221192 | tf_op jit(solution)/shard_map/ppermute | solution.py:60
  20.4 2.6 %collective-permute-start.5 = (bf16[3,128,768]{2,1,0:T(8,128)(2,1)S(1)}, bf16[3,128,768]{2,1,0:T(8,128)(2,1)S(1)}, u32[]{:S(2)}, u32[]{:S(2)}) collective-permute-start(bf16[3,128,768]{2,1,0:T(8,128)(2,1)S(1)} %get-tuple-element.20.p_own), channel_id=1, source_target_pairs={{0,1},{1,0},{2,3},{3,2},{4,5},{5,4},{6,7},{7,6},{8,9},{9,8},{10,11... | collective-permute-start | bytes 1769480 | tf_op jit(solution)/shard_map/ppermute | solution.py:60
  21.1 1.9 %collective-permute-start.6 = (bf16[112,768]{1,0:T(8,128)(2,1)S(1)}, bf16[112,768]{1,0:T(8,128)(2,1)S(1)}, u32[]{:S(2)}, u32[]{:S(2)}) collective-permute-start(bf16[112,768]{1,0:T(8,128)(2,1)S(1)} %join.1.after.j_own.p_own), channel_id=1, source_target_pairs={{0,1},{1,0},{2,3},{3,2},{4,5},{5,4},{6,7},{7,6},{8,9},{9,8},{10,11... | collective-permute-start | bytes 516104 | tf_op jit(solution)/shard_map/ppermute | solution.py:60
  21.2 25.2 %collective-permute-start.7 = (bf16[3,128,768]{2,1,0:T(8,128)(2,1)}, bf16[3,128,768]{2,1,0:T(8,128)(2,1)S(1)}, u32[]{:S(2)}, u32[]{:S(2)}) collective-permute-start(bf16[3,128,768]{2,1,0:T(8,128)(2,1)} %get-tuple-element.25), channel_id=1, source_target_pairs={{0,4},{1,2},{2,6},{3,0},{4,8},{5,1},{6,10},{7,3},{8,12},{9,5},{10,... | collective-permute-start | bytes 1769480 | tf_op jit(solution)/shard_map/ppermute | solution.py:60
  27.9 44.7 %all-to-all-start = ((bf16[128,24,384]{2,1,0:T(8,128)(2,1)}), bf16[128,24,384]{2,1,0:T(8,128)(2,1)S(1)}, u32[]{:S(2)}, u32[]{:S(2)}) async-start(bf16[128,24,384]{2,1,0:T(8,128)(2,1)} %bitcast.4), calls=%async_computation | async-start | bytes 4718592 | tf_op jit(solution)/shard_map/all_to_all | solution.py:669
  39.6 2.3 %copy-start.5 = (bf16[3072,768]{1,0:T(8,128)(2,1)S(1)}, bf16[3072,768]{1,0:T(8,128)(2,1)}, u32[]{:S(2)}) copy-start(bf16[3072,768]{1,0:T(8,128)(2,1)} %w_ref.3) | copy-start | bytes 14155780
  42.0 1.7 %copy-start.7 = (bf16[4,384,768]{2,1,0:T(8,128)(2,1)S(1)}, bf16[4,384,768]{2,1,0:T(8,128)(2,1)}, u32[]{:S(2)}) copy-start(bf16[4,384,768]{2,1,0:T(8,128)(2,1)} %get-tuple-element.24.own_ref) | copy-start | bytes 7077892
  46.4 2.1 %copy-start.2 = (bf16[6,64,768]{2,1,0:T(8,128)(2,1)S(1)}, bf16[6,64,768]{2,1,0:T(8,128)(2,1)}, u32[]{:S(2)}) copy-start(bf16[6,64,768]{2,1,0:T(8,128)(2,1)} %u_own.5) | copy-start | bytes 1769476
  46.4 2.1 %copy-start.4 = (bf16[6,64,768]{2,1,0:T(8,128)(2,1)S(1)}, bf16[6,64,768]{2,1,0:T(8,128)(2,1)}, u32[]{:S(2)}) copy-start(bf16[6,64,768]{2,1,0:T(8,128)(2,1)} %copy-done.3) | copy-start | bytes 1769476
  46.4 2.1 %collective-permute-start.8 = (bf16[3,128,768]{2,1,0:T(8,128)(2,1)S(1)}, bf16[3,128,768]{2,1,0:T(8,128)(2,1)S(1)}, u32[]{:S(2)}, u32[]{:S(2)}) collective-permute-start(bf16[3,128,768]{2,1,0:T(8,128)(2,1)S(1)} %tie.1.a_own), channel_id=1, source_target_pairs={{0,1},{1,0},{2,3},{3,2},{4,5},{5,4},{6,7},{7,6},{8,9},{9,8},{10,11... | collective-permute-start | bytes 1769480 | tf_op jit(solution)/shard_map/ppermute | solution.py:60
  48.5 2.3 %copy-start.6 = (bf16[3072,768]{1,0:T(8,128)(2,1)S(1)}, bf16[3072,768]{1,0:T(8,128)(2,1)}, u32[]{:S(2)}) copy-start(bf16[3072,768]{1,0:T(8,128)(2,1)} %w_ref.3) | copy-start | bytes 14155780
